TPU v7x, 128 devices: a whole 4x4x4 slice. The times are simulated.
128 devices in a mesh: fsdp: 128 (over y, x, z, core).
Axes of the slice: x: 4, y: 4, z: 4, core: 2. Of those that a mesh axis runs over, the one named last changes fastest.
Arguments:
- tokens: bfloat16 [16384, 1024], P('fsdp'), may hold values from -6 to 6
- cotangent: bfloat16 [16384, 1024], P('fsdp'), may hold values from -6 to 6
- input_weight: bfloat16 [1024, 4120], P('fsdp'), may hold values from -0.1875 to 0.1875
- output_weight: bfloat16 [2048, 1024], P('fsdp'), as said below
- gate_up_weight: bfloat16 [1024, 4096], P('fsdp'), may hold values from -0.1875 to 0.1875
- down_weight: bfloat16 [2048, 1024], P('fsdp'), may hold values from -0.125 to 0.125
- norm_gains: bfloat16 [2, 1024], P(None, 'fsdp'), may hold values from 0.5 to 1.5
- conv_params: bfloat16 [5, 1792], P(None, 'fsdp'), may hold values from -3 to 3
- mixer_scale: bfloat16 [1, 1536], P(None, 'fsdp'), may hold values from 0.5 to 1.5
- decay_log: float32 [24], replicated, may hold values from -4 to 1
- step_bias: float32 [24], replicated, may hold values from -4 to -1
- mixer_skip_factor: float32 [24], replicated, may hold values from 0.5 to 1.5
Outputs:
- layer_output: bfloat16 [16384, 1024], P('fsdp')
- input_grad: bfloat16 [16384, 1024], P('fsdp')
- input_weight_grad: float32 [1024, 4120], P('fsdp')
- output_weight_grad: float32 [2048, 1024], P('fsdp')
- gate_up_weight_grad: float32 [1024, 4096], P('fsdp')
- down_weight_grad: float32 [2048, 1024], P('fsdp')
- norm_gains_grad: float32 [2, 1024], P(None, 'fsdp')
- conv_params_grad: float32 [5, 1792], P(None, 'fsdp')
- mixer_scale_grad: float32 [1, 1536], P(None, 'fsdp')
- decay_log_grad: float32 [24], replicated
- step_bias_grad: float32 [24], replicated
- skip_gain_grad: float32 [24], replicated
Inputs may be any that keep to these rules, and one draw needn't show every extreme that they name: `output_weight`: independent entries, at most 20 / sqrt(2048) in magnitude in the first 512 rows and at most 5 / sqrt(2048) in the others.
All inputs are finite; a program needn't handle non-finite values.
Results may differ from a plain program's by a relative error of at most 0.022.
Values may be sent and summed in bfloat16 or wider, within the bound.
A program may use at most 192 MiB of HBM per device.

v0:
```python
import math

import jax
import jax.numpy as jnp
from jax import lax
from jax.sharding import PartitionSpec as P

FF = 2048
QH = 8
KVH = 2
HD = 64
MIXER_HEADS = 24
MIXER_HEAD_SIZE = 64
STATE = 128
CONVK = 4
Q_WIDTH = 512
KV_WIDTH = 128
MIXER_FEATURES = 1536
CONV_WIDTH = 1792


norm_eps = 1e-05
rope_base = 10000.0
masked_value = -1e30


def rms_scale(values, gain):
    return values * lax.rsqrt(jnp.mean(values * values, axis=-1, keepdims=True) + norm_eps) * gain


def rope_tables(length_total):
    position = lax.broadcasted_iota(jnp.int32, (length_total, HD // 2), 0).astype(jnp.float32)
    column = lax.broadcasted_iota(jnp.int32, (length_total, HD // 2), 1).astype(jnp.float32)
    angle = position * jnp.exp(column * (-2.0 * math.log(rope_base) / HD))
    cosine_table = jnp.concatenate([jnp.cos(angle), jnp.cos(angle)], axis=1)
    sine_table = jnp.concatenate([jnp.sin(angle), jnp.sin(angle)], axis=1)
    return (cosine_table, sine_table)


def rotate(values, cosine_table, sine_table):
    half_size = values.shape[-1] // 2
    turned = jnp.concatenate([-values[..., half_size:], values[..., :half_size]], axis=-1)
    return values * cosine_table + turned * sine_table


def pre_mixer(projected, conv_all, step_bias, decay_log):
    length_total = projected.shape[0]
    cosine_table, sine_table = rope_tables(length_total)
    cosine_table = cosine_table[:, None, :]
    sine_table = sine_table[:, None, :]
    queries = projected[:, :Q_WIDTH].reshape(length_total, QH, HD)
    key_rows = projected[:, Q_WIDTH : Q_WIDTH + KV_WIDTH].reshape(length_total, KVH, HD)
    value_rows = projected[:, Q_WIDTH + KV_WIDTH : Q_WIDTH + 2 * KV_WIDTH]
    offset = Q_WIDTH + 2 * KV_WIDTH
    zgate = projected[:, offset : offset + MIXER_FEATURES]
    conv_in = projected[:, offset + MIXER_FEATURES : offset + MIXER_FEATURES + CONV_WIDTH]
    dt_raw = projected[:, offset + MIXER_FEATURES + CONV_WIDTH :]
    padded = jnp.concatenate([jnp.zeros((CONVK - 1, CONV_WIDTH), jnp.float32), conv_in], axis=0)
    summed = conv_all[CONVK]
    for tap_index in range(CONVK):
        summed = summed + conv_all[tap_index] * padded[tap_index : tap_index + length_total]
    active = jax.nn.silu(summed)
    step_sizes = jax.nn.softplus(dt_raw + step_bias)
    cumulative = jnp.cumsum(step_sizes * -jnp.exp(decay_log), axis=0)
    query_rot = rotate(queries, cosine_table, sine_table).reshape(length_total, Q_WIDTH)
    key_rot = rotate(key_rows, cosine_table, sine_table).reshape(length_total, KV_WIDTH)
    return (
        query_rot,
        key_rot,
        value_rows,
        zgate,
        active[:, :MIXER_FEATURES],
        active[:, MIXER_FEATURES : MIXER_FEATURES + STATE],
        active[:, MIXER_FEATURES + STATE :],
        step_sizes,
        cumulative,
    )


def post_mixer(state_result, mixer_input_activated, zgate, mixer_skip_factor, scale_row):
    length_total = state_result.shape[0]
    central_output = state_result.reshape(
        length_total, MIXER_HEADS, MIXER_HEAD_SIZE
    ) + mixer_skip_factor[:, None] * mixer_input_activated.reshape(
        length_total, MIXER_HEADS, MIXER_HEAD_SIZE
    )
    gated = central_output.reshape(length_total, MIXER_FEATURES) * jax.nn.silu(zgate)
    return rms_scale(gated, scale_row)


def swiglu(gate_up):
    return jax.nn.silu(gate_up[:, :FF]) * gate_up[:, FF:]


def fold_rows(left_low, piece):
    return jnp.dot(left_low, piece, preferred_element_type=jnp.float32)


def back_rows(grad_low, piece):
    return lax.dot_general(
        grad_low, piece, (((1,), (1,)), ((), ())), preferred_element_type=jnp.float32
    )


def grad_rows(left_low, right_low):
    return lax.dot_general(
        left_low, right_low, (((0,), (0,)), ((), ())), preferred_element_type=jnp.float32
    )


def attend_scores(query_group_rows, key_head_rows, causal):
    unscaled_scores = jnp.einsum(
        "ixnb,qxb->xniq", query_group_rows, key_head_rows, preferred_element_type=jnp.float32
    )
    return jnp.where(causal, unscaled_scores * (1.0 / math.sqrt(HD)), masked_value)


def local(
    tokens,
    cotangent,
    input_weight,
    output_weight,
    gate_up_weight,
    down_weight,
    norm_gains,
    conv_params,
    mixer_scale,
    decay_log,
    step_bias,
    mixer_skip_factor,
):
    length_total = tokens.shape[0]
    hidden = tokens.astype(jnp.float32)
    gains_all, conv_all, scale_all = (
        lax.all_gather(norm_gains, "fsdp", axis=1, tiled=True),
        lax.all_gather(conv_params, "fsdp", axis=1, tiled=True),
        lax.all_gather(mixer_scale, "fsdp", axis=1, tiled=True),
    )
    gains_all = gains_all.astype(jnp.float32)
    conv_all = conv_all.astype(jnp.float32)
    scale_all = scale_all.astype(jnp.float32)
    causal = lax.broadcasted_iota(
        jnp.int32, (length_total, length_total), 0
    ) >= lax.broadcasted_iota(jnp.int32, (length_total, length_total), 1)
    normed, norm_in_back = jax.vjp(rms_scale, hidden, gains_all[0])
    normed_low = normed.astype(jnp.bfloat16)
    projected = fold_rows(normed_low, lax.all_gather(input_weight, "fsdp", axis=0, tiled=True))
    mixer_in, pre_back = jax.vjp(pre_mixer, projected, conv_all, step_bias, decay_log)
    (
        query_rot,
        key_rot,
        value_rows,
        zgate,
        mixer_input_activated,
        b_active,
        c_active,
        step_sizes,
        cumulative,
    ) = mixer_in
    query_group_rows = query_rot.astype(jnp.bfloat16).reshape(length_total, KVH, QH // KVH, HD)
    key_head_rows = key_rot.astype(jnp.bfloat16).reshape(length_total, KVH, HD)
    value_head_rows = value_rows.astype(jnp.bfloat16).reshape(length_total, KVH, HD)
    scores = attend_scores(query_group_rows, key_head_rows, causal)
    row_peak = jnp.max(scores, axis=-1, keepdims=True)
    exponent = jnp.exp(scores - row_peak)
    totals = jnp.sum(exponent, axis=-1, keepdims=True)
    log_total = row_peak + jnp.log(totals)
    probability_reduced = (exponent / totals).astype(jnp.bfloat16)
    attention_result = jnp.einsum(
        "mfbi,imq->bmfq", probability_reduced, value_head_rows, preferred_element_type=jnp.float32
    )
    attention_result = attention_result.reshape(length_total, Q_WIDTH).astype(jnp.bfloat16)
    c_low = c_active.astype(jnp.bfloat16)
    b_low = b_active.astype(jnp.bfloat16)
    mixer_input_reduced = mixer_input_activated.astype(jnp.bfloat16)
    inner_prod = lax.dot_general(
        c_low, b_low, (((1,), (1,)), ((), ())), preferred_element_type=jnp.float32
    )
    head_grouping = math.gcd(MIXER_HEADS, 8)
    head_block_list = MIXER_HEADS // head_grouping
    cum_heads = cumulative.T.reshape(head_block_list, head_grouping, length_total)
    step_heads = step_sizes.T.reshape(head_block_list, head_grouping, length_total)
    mixer_input_heads = (
        mixer_input_reduced.reshape(length_total, MIXER_HEADS, MIXER_HEAD_SIZE)
        .transpose(1, 0, 2)
        .reshape(head_block_list, head_grouping, length_total, MIXER_HEAD_SIZE)
    )

    def mixing_of(cum_block, step_block):
        gaps = cum_block[:, :, None] - cum_block[:, None, :]
        decay_table = jnp.exp(jnp.where(causal[None], gaps, masked_value))
        return (inner_prod[None] * decay_table * step_block[:, None, :], decay_table)

    def state_block(block_items):
        cum_block, step_block, x_block = block_items
        mixing, _ = mixing_of(cum_block, step_block)
        return jnp.einsum(
            "hts,hsp->htp", mixing.astype(jnp.bfloat16), x_block, preferred_element_type=jnp.float32
        )

    state_result = lax.map(state_block, (cum_heads, step_heads, mixer_input_heads))
    state_result = (
        state_result.reshape(MIXER_HEADS, length_total, MIXER_HEAD_SIZE)
        .transpose(1, 0, 2)
        .reshape(length_total, MIXER_FEATURES)
    )
    normed_state, post_back = jax.vjp(
        post_mixer, state_result, mixer_input_activated, zgate, mixer_skip_factor, scale_all[0]
    )
    mixed = jnp.concatenate([attention_result, normed_state.astype(jnp.bfloat16)], axis=1)
    branch = fold_rows(mixed, lax.all_gather(output_weight, "fsdp", axis=0, tiled=True))
    residual = hidden + branch
    normed_ff, norm_ff_back = jax.vjp(rms_scale, residual, gains_all[1])
    normed_ff_low = normed_ff.astype(jnp.bfloat16)
    gate_up = fold_rows(normed_ff_low, lax.all_gather(gate_up_weight, "fsdp", axis=0, tiled=True))
    hidden_ff, swiglu_back = jax.vjp(swiglu, gate_up)
    hidden_low = hidden_ff.astype(jnp.bfloat16)
    down_out = fold_rows(hidden_low, lax.all_gather(down_weight, "fsdp", axis=0, tiled=True))
    layer_output = (residual + down_out).astype(jnp.bfloat16)
    grad_out = cotangent.astype(jnp.float32)
    d_hidden_ff = back_rows(cotangent, lax.all_gather(down_weight, "fsdp", axis=0, tiled=True))
    down_weight_grad = lax.psum_scatter(
        grad_rows(hidden_low, cotangent), "fsdp", scatter_dimension=0, tiled=True
    )
    (d_gate_up,) = swiglu_back(d_hidden_ff)
    d_gate_low = d_gate_up.astype(jnp.bfloat16)
    d_normed_ff = back_rows(d_gate_low, lax.all_gather(gate_up_weight, "fsdp", axis=0, tiled=True))
    gate_up_weight_grad = lax.psum_scatter(
        grad_rows(normed_ff_low, d_gate_low), "fsdp", scatter_dimension=0, tiled=True
    )
    d_resid_ff, d_gain_ff = norm_ff_back(d_normed_ff)
    d_residual = grad_out + d_resid_ff
    d_branch_low = d_residual.astype(jnp.bfloat16)
    d_mixed = back_rows(d_branch_low, lax.all_gather(output_weight, "fsdp", axis=0, tiled=True))
    output_weight_grad = lax.psum_scatter(
        grad_rows(mixed, d_branch_low), "fsdp", scatter_dimension=0, tiled=True
    )
    d_attended = d_mixed[:, :Q_WIDTH].astype(jnp.bfloat16)
    d_state_out, d_x_skip, d_zgate, d_skip_gain, d_scale = post_back(d_mixed[:, Q_WIDTH:])
    state_gradient_reduced = d_state_out.astype(jnp.bfloat16)
    d_heads = (
        state_gradient_reduced.reshape(length_total, MIXER_HEADS, MIXER_HEAD_SIZE)
        .transpose(1, 0, 2)
        .reshape(head_block_list, head_grouping, length_total, MIXER_HEAD_SIZE)
    )

    def state_back(d_inner, block_items):
        cum_block, step_block, x_block, d_block = block_items
        mixing, decay_table = mixing_of(cum_block, step_block)
        d_mixing = jnp.einsum("htp,hsp->hts", d_block, x_block, preferred_element_type=jnp.float32)
        d_x_block = jnp.einsum(
            "hts,htp->hsp", mixing.astype(jnp.bfloat16), d_block, preferred_element_type=jnp.float32
        )
        scaled = d_mixing * step_block[:, None, :]
        d_inner = d_inner + jnp.sum(scaled * decay_table, axis=0)
        d_step = jnp.sum(d_mixing * (inner_prod[None] * decay_table), axis=1)
        flow = scaled * inner_prod[None] * decay_table
        d_cum = jnp.sum(flow, axis=2) - jnp.sum(flow, axis=1)
        return (d_inner, (d_x_block, d_step, d_cum))

    d_inner, (mixer_input_heads_gradient, d_step_heads, d_cum_heads) = lax.scan(
        state_back,
        jnp.zeros((length_total, length_total), jnp.float32),
        (cum_heads, step_heads, mixer_input_heads, d_heads),
    )
    mixer_input_state_gradient = (
        mixer_input_heads_gradient.reshape(MIXER_HEADS, length_total, MIXER_HEAD_SIZE)
        .transpose(1, 0, 2)
        .reshape(length_total, MIXER_FEATURES)
    )
    d_steps = d_step_heads.reshape(MIXER_HEADS, length_total).T
    d_cumulative = d_cum_heads.reshape(MIXER_HEADS, length_total).T
    d_inner_low = d_inner.astype(jnp.bfloat16)
    d_c_active = jnp.dot(d_inner_low, b_low, preferred_element_type=jnp.float32)
    d_b_active = lax.dot_general(
        d_inner_low, c_low, (((0,), (0,)), ((), ())), preferred_element_type=jnp.float32
    )
    output_heads_gradient = d_attended.reshape(length_total, KVH, QH // KVH, HD)
    probability_table = jnp.exp(attend_scores(query_group_rows, key_head_rows, causal) - log_total)
    d_probs = jnp.einsum(
        "ixnb,qxb->xniq", output_heads_gradient, value_head_rows, preferred_element_type=jnp.float32
    )
    d_scores = probability_table * (
        d_probs - jnp.sum(probability_table * d_probs, axis=-1, keepdims=True)
    )
    unscaled_gradient = (d_scores * (1.0 / math.sqrt(HD))).astype(jnp.bfloat16)
    d_query = jnp.einsum(
        "mfbi,imq->bmfq", unscaled_gradient, key_head_rows, preferred_element_type=jnp.float32
    ).reshape(length_total, Q_WIDTH)
    d_key = jnp.einsum(
        "mcnp,nmca->pma", unscaled_gradient, query_group_rows, preferred_element_type=jnp.float32
    ).reshape(length_total, KV_WIDTH)
    d_value = jnp.einsum(
        "mcnp,nmca->pma",
        probability_table.astype(jnp.bfloat16),
        output_heads_gradient,
        preferred_element_type=jnp.float32,
    ).reshape(length_total, KV_WIDTH)
    d_projected, d_conv, d_step_bias, d_decay_log = pre_back(
        (
            d_query,
            d_key,
            d_value,
            d_zgate,
            mixer_input_state_gradient + d_x_skip,
            d_b_active,
            d_c_active,
            d_steps,
            d_cumulative,
        )
    )
    d_proj_low = d_projected.astype(jnp.bfloat16)
    d_normed = back_rows(d_proj_low, lax.all_gather(input_weight, "fsdp", axis=0, tiled=True))
    summed_rows = lax.psum_scatter(
        grad_rows(normed_low, d_proj_low), "fsdp", scatter_dimension=0, tiled=True
    )
    d_hidden, d_gain_in = norm_in_back(d_normed)
    input_grad = (d_residual + d_hidden).astype(jnp.bfloat16)
    full_gains, full_conv, full_scale, decay_log_grad, step_bias_grad, skip_gain_grad = lax.psum(
        (
            jnp.stack([d_gain_in, d_gain_ff]),
            d_conv,
            d_scale[None, :],
            d_decay_log,
            d_step_bias,
            d_skip_gain,
        ),
        "fsdp",
    )
    position = lax.axis_index("fsdp")
    norm_gains_grad = lax.dynamic_slice_in_dim(
        full_gains, position * norm_gains.shape[1], norm_gains.shape[1], 1
    )
    conv_params_grad = lax.dynamic_slice_in_dim(
        full_conv, position * conv_params.shape[1], conv_params.shape[1], 1
    )
    mixer_scale_grad = lax.dynamic_slice_in_dim(
        full_scale, position * mixer_scale.shape[1], mixer_scale.shape[1], 1
    )
    return (
        layer_output,
        input_grad,
        summed_rows,
        output_weight_grad,
        gate_up_weight_grad,
        down_weight_grad,
        norm_gains_grad,
        conv_params_grad,
        mixer_scale_grad,
        decay_log_grad,
        step_bias_grad,
        skip_gain_grad,
    )


def solution(mesh):
    in_specs = (
        P("fsdp", None),
        P("fsdp", None),
        P("fsdp", None),
        P("fsdp", None),
        P("fsdp", None),
        P("fsdp", None),
        P(None, "fsdp"),
        P(None, "fsdp"),
        P(None, "fsdp"),
        P(),
        P(),
        P(),
    )
    out_specs = (
        P("fsdp", None),
        P("fsdp", None),
        P("fsdp", None),
        P("fsdp", None),
        P("fsdp", None),
        P("fsdp", None),
        P(None, "fsdp"),
        P(None, "fsdp"),
        P(None, "fsdp"),
        P(),
        P(),
        P(),
    )
    return jax.shard_map(local, mesh=mesh, in_specs=in_specs, out_specs=out_specs, check_vma=False)
```

profile of v0, /device:TPU:1, one launch (start us, length us, event | category | flops | bytes accessed | tf_op | source)
XLA Modules:
  0.0 2557.9 jit_solution(2055271486765146400)
XLA Ops:
  10.1 34.5 %all-gather = bf16[128,8,2]{1,2,0:T(2,128)(2,1)S(1)} all-gather(bf16[1,8,2]{1,2,0:T(2,128)(2,1)} %bitcast.240), channel_id=1, replica_groups=mesh['fsdp'=128] {'fsdp'}, dimensions={0}, use_global_device_ids=true | all-gather | bytes 4128 | tf_op jit(solution)/shard_map/all_gather | solution.py:135
  44.9 33.6 %all-gather.1 = bf16[128,14,5]{1,2,0:T(8,128)(2,1)S(1)} all-gather(bf16[1,14,5]{1,2,0:T(8,128)(2,1)} %bitcast.239), channel_id=1, replica_groups=mesh['fsdp'=128] {'fsdp'}, dimensions={0}, use_global_device_ids=true | all-gather | bytes 18060 | tf_op jit(solution)/shard_map/all_gather | solution.py:136
  80.0 63.6 %all-reduce.25 = bf16[1536]{0:T(1024)(128)(2,1)S(1)} all-reduce(bf16[1536]{0:T(1024)(128)(2,1)S(1)} %dynamic-update-slice), channel_id=1, replica_groups=mesh['fsdp'=128] {'fsdp'}, use_global_device_ids=true, to_apply=%add.25 | all-reduce | flops 1536 | bytes 6144
  146.7 7.1 fusion.90
  153.9 3.2 fusion.123
  165.1 8.3 while.28
  180.3 42.9 %all-gather.11.cloned.1.call-done = bf16[1024,4096]{1,0:T(8,128)(2,1)} async-done(((bf16[8,4096]{1,0:T(8,128)(2,1)}), bf16[1024,4096]{1,0:T(8,128)(2,1)}) %all-gather.11.cloned.1.call-update) | async-done | bytes 8388624 | tf_op jit(solution)/shard_map/all_gather | solution.py:215
  223.2 6.0 fusion.117
  229.2 61.5 %all-gather.13.cloned.1.call-done = bf16[2048,1024]{1,0:T(8,128)(2,1)} async-done(((bf16[16,1024]{1,0:T(8,128)(2,1)}), bf16[2048,1024]{1,0:T(8,128)(2,1)}) %all-gather.13.cloned.1.call-update) | async-done | bytes 4194320 | tf_op jit(solution)/shard_map/all_gather | solution.py:218
  290.7 5.6 fusion.87
  296.3 3.5 multiply_reduce_fusion.11
  321.1 3.5 multiply_reduce_fusion.7
  327.3 22.8 while.29
  373.4 8.5 fusion.88
  383.1 4.5 fusion.69
  388.9 4.6 fusion.131
  395.1 8.5 fusion.82
  405.3 7.5 fusion.60
  413.0 64.2 %all-reduce.27 = (f32[2,1024]{1,0:T(2,128)S(1)}, f32[5,1792]{1,0:T(8,128)S(1)}, f32[1,1536]{1,0:T(1,128)S(1)}, f32[24]{0:T(128)}, f32[24]{0:T(128)}, /*index=5*/f32[24]{0:T(128)}) all-reduce(f32[2,1024]{1,0:T(2,128)S(1)} %pad_maximum_fusion.5, f32[5,1792]{1,0:T(8,128)S(1)} %pad_add_fusion.4, ...), channel_id=1, replica_groups=mesh['fsdp'=128] {'fsdp'}, use_global_device_ids=true, to_apply=%region_25.26 | all-reduce | flops 12616 | bytes 100928 | tf_op jit(solution)/shard_map/psum | solution.py:319
  481.0 3.6 fusion.42
  484.6 112.7 %all-reduce.30.cloned.1.call-done = f32[1024,4120]{1,0:T(8,128)} async-done(((f32[1024,4120]{1,0:T(8,128)}), f32[1024,4120]{1,0:T(8,128)}) %all-reduce.30.cloned.1.call-update) | async-done | bytes 16875536
  598.9 643.0 %reduce-scatter.4.cloned.1.call-done = f32[16,1024]{1,0:T(8,128)} async-done(((f32[2048,1024]{1,0:T(8,128)}), f32[16,1024]{1,0:T(8,128)}) %reduce-scatter.4.cloned.1.call-update) | async-done | bytes 65552 | tf_op jit(solution)/shard_map/reduce_scatter | solution.py:235
  1241.9 646.8 %reduce-scatter.8.cloned.1.call-done = f32[16,1024]{1,0:T(8,128)} async-done(((f32[2048,1024]{1,0:T(8,128)}), f32[16,1024]{1,0:T(8,128)}) %reduce-scatter.8.cloned.1.call-update) | async-done | bytes 65552 | tf_op jit(solution)/shard_map/reduce_scatter | solution.py:222
  1888.8 661.9 %reduce-scatter.6.cloned.1.call-done = f32[8,4096]{1,0:T(8,128)} async-done(((f32[1024,4096]{1,0:T(8,128)}), f32[8,4096]{1,0:T(8,128)}) %reduce-scatter.6.cloned.1.call-update) | async-done | bytes 131088 | tf_op jit(solution)/shard_map/reduce_scatter | solution.py:228
  (323 shorter events, 110.8 us)
Async XLA Ops:
  7.2 138.7 %copy-start.11 = (bf16[128,1024]{1,0:T(8,128)(2,1)S(1)}, bf16[128,1024]{1,0:T(8,128)(2,1)}, u32[]{:S(2)}) copy-start(bf16[128,1024]{1,0:T(8,128)(2,1)} %param.16) | copy-start | bytes 786436
  7.2 138.9 %copy-start.80 = (f32[24]{0:T(128)S(1)}, f32[24]{0:T(128)}, u32[]{:S(2)}) copy-start(f32[24]{0:T(128)} %param.25) | copy-start | bytes 292
  7.2 139.5 %all-gather.7.cloned.1.call-start = ((), (), s32[]{:S(2)}) async-start(), calls=%async_computation.3 | async-start | bytes 8718336 | tf_op jit(solution)/shard_map/all_gather | solution.py:147
  7.9 169.1 %all-gather.9.cloned.1.call-start = ((), (), s32[]{:S(2)}) async-start(), calls=%async_computation.4 | async-start | bytes 4227072 | tf_op jit(solution)/shard_map/all_gather | solution.py:211
  8.7 214.6 %all-gather.11.cloned.1.call-start = ((), (), s32[]{:S(2)}) async-start(), calls=%async_computation.5 | async-start | bytes 8454144 | tf_op jit(solution)/shard_map/all_gather | solution.py:215
  9.4 281.3 %all-gather.13.cloned.1.call-start = ((), (), s32[]{:S(2)}) async-start(), calls=%async_computation.6 | async-start | bytes 4227072 | tf_op jit(solution)/shard_map/all_gather | solution.py:218
  10.0 587.3 %all-reduce.30.cloned.1.call-start = ((), (), s32[]{:S(2)}) async-start(), calls=%async_computation.10 | async-start | bytes 34603008
  145.8 15.0 copy-start.31
  145.8 163.9 %copy-start.33 = (f32[128,64]{0,1:T(8,128)}, f32[128,64]{0,1:T(8,128)S(1)}, u32[]{:S(2)}) copy-start(f32[128,64]{0,1:T(8,128)S(1)} %get-tuple-element.286) | copy-start | bytes 98308
  145.9 8.0 copy-start.47
  145.9 8.0 copy-start.49
  145.9 8.0 copy-start.51
  145.9 8.0 copy-start.53
  146.1 7.7 copy-start.71
  146.6 12.3 copy-start.75
  161.8 13.3 copy-start.13
  180.3 119.6 %copy-start.67 = (f32[128]{0:T(128)}, f32[128]{0:T(128)S(1)}, u32[]{:S(2)}) copy-start(f32[128]{0:T(128)S(1)} %fusion.111) | copy-start | bytes 1540
  327.3 27.8 %copy-start.10 = (f32[128,1536]{0,1:T(8,128)S(1)}, f32[128,1536]{0,1:T(8,128)}, u32[]{:S(2)}) copy-start(f32[128,1536]{0,1:T(8,128)} %copy-done.9) | copy-start | bytes 2359300
  373.3 8.6 copy-start.20
  381.9 860.0 %reduce-scatter.4.cloned.1.call-start = ((), (), s32[]{:S(2)}) async-start(), calls=%async_computation.7 | async-start | bytes 8454144 | tf_op jit(solution)/shard_map/reduce_scatter | solution.py:235
  387.6 1501.1 %reduce-scatter.8.cloned.1.call-start = ((), (), s32[]{:S(2)}) async-start(), calls=%async_computation.9 | async-start | bytes 8454144 | tf_op jit(solution)/shard_map/reduce_scatter | solution.py:222
  393.6 2157.0 %reduce-scatter.6.cloned.1.call-start = ((), (), s32[]{:S(2)}) async-start(), calls=%async_computation.8 | async-start | bytes 16908288 | tf_op jit(solution)/shard_map/reduce_scatter | solution.py:228
  405.3 73.8 %copy-start.78 = (f32[128]{0:T(128)S(1)}, f32[128]{0:T(128)}, u32[]{:S(2)}) copy-start(f32[128]{0:T(128)} %copy-done.77) | copy-start | bytes 1540
  412.9 68.2 %copy-start.26 = (bf16[128,2048]{1,0:T(8,128)(2,1)S(1)}, bf16[128,2048]{1,0:T(8,128)(2,1)}, u32[]{:S(2)}) copy-start(bf16[128,2048]{1,0:T(8,128)(2,1)} %get-tuple-element.260) | copy-start | bytes 1572868
  (72 other events, 182.1 us)
Sparse Core Ops, SparseCore 0:
  10.9 74.0 all-gather.6
  88.1 64.4 all-gather.8
  155.6 67.6 all-gather.10
  226.3 64.4 all-gather.12
  382.1 215.2 all-reduce.29
  600.2 641.6 reduce-scatter.3
  1244.9 643.8 reduce-scatter.7
  1891.8 658.7 reduce-scatter.5
where the time goes:
time: 2570 us; the launch traced here: 2560 us
  waiting for transfers between devices  2170 us (84%)
  blocking collectives  196 us (8%)
  matrix products  96.8 us (4%)
  other arithmetic  39.7 us (2%)
  local copies, waits for them, and re-layouts  37.2 us (1%)
    reduce_scatter x1, waiting for transfers between devices, local(): lax.psum_scatter(grad_rows(normed_ff_low, d_gate_low), 'fsdp', scatter_di...  662 us
    reduce_scatter x1, waiting for transfers between devices, local(): lax.psum_scatter(grad_rows(hidden_low, cotangent), 'fsdp', scatter_dimens...  647 us
    reduce_scatter x1, waiting for transfers between devices, local(): lax.psum_scatter(grad_rows(mixed, d_branch_low), 'fsdp', scatter_dimensio...  643 us
    unnamed x9, waiting for transfers between devices  115 us
    psum x1, blocking collectives, local(): lax.psum((jnp.stack([d_gain_in, d_gain_ff]), d_conv, d_scale[None, :], d_...  64.2 us
    unnamed x1, blocking collectives  63.6 us
    all_gather x1, waiting for transfers between devices, local(): lax.all_gather(down_weight, 'fsdp', axis=0, tiled=True)  61.5 us
  transfers between devices with their start and end apart: 8, of which 6 were waited for; matrix products, arithmetic and copies ran while one was open for 3% of the time, Pallas kernels for 0%

commit v1 on v0

v1 whole, which is shorter than its diff:
```python
import math

import jax
import jax.numpy as jnp
import numpy as np
from jax import lax
from jax.experimental import pallas as pl
from jax.experimental.pallas import tpu as pltpu
from jax.sharding import PartitionSpec as P

HD = 64
MIXER_HEADS = 24
MIXER_HEAD_SIZE = 64
CONVK = 4
MIXER_FEATURES = 1536
TOK = 128
norm_eps = 1e-05
rope_base = 10000.0
masked_value = -1e30

Y, X, Z = range(3)
AXES = (Y, X, Z)
ORDERS = ((X, Y, Z), (Y, Z, X), (Z, X, Y))
STEPS = (1, 3, 2)
SMALL, INA, INB, OUT, GU, DOWN = range(6)
WEIGHTS = (SMALL, INA, INB, OUT, GU, DOWN)
ROWS = (16, 16, 16, 32, 16, 32)
COLS = (128, 1024, 1024, 512, 2048, 512)
PARTS = (
    ((0, 128),),
    ((0, 384), (384, 768), (768, 1024)),
    ((0, 384), (384, 640), (640, 1024)),
    ((0, 128), (128, 384), (384, 512)),
    ((0, 768), (768, 1408), (1408, 2048)),
    ((0, 128), (128, 256), (256, 512)),
)


class Place:
    def __init__(self):
        me = lax.axis_index("fsdp")
        self.me = me
        self.core = lax.rem(me, 2)
        self.at = [lax.div(me, 32), lax.rem(lax.div(me, 8), 4), lax.rem(lax.div(me, 2), 4)]
        self.sibling = me + 1 - 2 * self.core

    def moved(self, axis, step):
        return lax.rem(self.at[axis] + step, 4)

    def peer(self, axis, step):
        at = list(self.at)
        at[axis] = self.moved(axis, step)
        return ((at[Y] * 4 + at[X]) * 4 + at[Z]) * 2 + self.core

    def partners(self):
        return [self.sibling] + [self.peer(axis, step) for axis in AXES for step in STEPS]


def arrive(place):
    for partner in place.partners():
        pl.semaphore_signal(
            pltpu.get_barrier_semaphore(),
            inc=1,
            device_id=(partner,),
            device_id_type=pl.DeviceIdType.MESH,
        )


def meet(place):
    pl.semaphore_wait(pltpu.get_barrier_semaphore(), len(place.partners()))


def push(src, dst, send_sem, recv_sem, device):
    return pltpu.make_async_remote_copy(
        src_ref=src,
        dst_ref=dst,
        send_sem=send_sem,
        recv_sem=recv_sem,
        device_id=(device,),
        device_id_type=pl.DeviceIdType.MESH,
    )


def block_index(where, low, high):
    return tuple(where.get(axis, slice(None)) for axis in AXES) + (
        slice(None),
        pl.ds(low, high - low),
    )


def some_blocks(ref, count):
    lead = {1: (0, 0, 0), 3: (0, 0, pl.ds(0, 3)), 4: (0, 0), 12: (0, pl.ds(0, 3)), 16: (0,)}
    lead |= {32: (pl.ds(0, 2),), 48: (pl.ds(0, 3),), 64: (slice(None),)}
    return ref.at[lead[count]]


def expect(ref, count, sem, place):
    view = some_blocks(ref, count)
    return push(view, view, sem, sem, place.sibling)


def halved(part, phase_axis, half, order):
    axis = min(one for one in order if one != phase_axis)
    return {axis: pl.ds(2 * half, 2)}


class Gather:
    COUNTS = (3, 12, 48)

    def __init__(self, place, arrays, send_sem, recv_sem):
        self.place, self.arrays = place, arrays
        self.send_sem, self.recv_sem = send_sem, recv_sem

    def ref(self, name):
        if name == SMALL:
            return self.arrays[name]
        return self.arrays[name].at[self.place.core]

    def send_slot(self, name, phase):
        return self.send_sem.at[4 * name + phase]

    def recv_slot(self, name, phase, kind):
        if name == SMALL:
            return self.recv_sem.at[phase]
        return self.recv_sem.at[8 * name - 5 + (0, 1, 4)[phase] + (min(kind, 2) if phase else 0)]

    def slab(self, name, part, phase, step, half=None):
        order = ORDERS[part]
        where = {axis: self.place.at[axis] for axis in order[phase:]}
        where[order[phase]] = self.place.moved(order[phase], step)
        if half is not None:
            where |= halved(part, order[phase], half, order[: phase + 1])
        return self.ref(name).at[block_index(where, *PARTS[name][part])]

    def copy(self, name, part, phase, kind):
        step, source, half = (
            ((1, 0, None), (3, 0, None), (2, 0, None))
            if phase == 0 or name == SMALL
            else ((1, 0, None), (3, 0, None), (1, 3, 0), (3, 1, 1))
        )[kind]
        view = self.slab(name, part, phase, source, half)
        return push(
            view,
            view,
            self.send_slot(name, phase),
            self.recv_slot(name, phase, kind),
            self.place.peer(ORDERS[part][phase], step),
        )

    def start(self, name, phase, kinds=(0, 1)):
        if phase == 0 or name == SMALL:
            kinds = (0, 1, 2)
        for kind in kinds:
            for part in range(len(PARTS[name])):
                self.copy(name, part, phase, kind).start()

    def arrived(self, name, phase, kind=0):
        count = self.COUNTS[phase]
        if phase and name != SMALL:
            count //= 3
        slot = self.recv_slot(name, phase, kind)
        expect(self.ref(name), count, slot, self.place).wait_recv()

    def hand_on(self, name, phase):
        for kind in (0, 1):
            self.arrived(name, phase, kind)
            self.start(name, phase, (kind + 2,))
            if phase == 2:
                self.pass_on(name, (3, 1)[kind])

    def pass_on(self, name, step):
        for part in range(len(PARTS[name])):
            view = self.slab(name, part, 2, step)
            push(
                view,
                view,
                self.send_slot(name, 3),
                self.recv_sem.at[8 * name + 2],
                self.place.sibling,
            ).start()

    def passed(self, name):
        expect(self.ref(name), 64, self.recv_sem.at[8 * name + 2], self.place).wait_recv()

    def finish(self, name):
        for phase in range(3 if name == SMALL else 4):
            count = (*self.COUNTS, 64)[phase]
            expect(self.ref(name), count, self.send_slot(name, phase), self.place).wait_send()


def each(count, body):
    def step(index, nothing):
        body(index)
        return nothing

    lax.fori_loop(0, count, step, 0)


class Enter:
    def __init__(self, place, gather, pack, got, shards, sems):
        self.place, self.gather = place, gather
        self.pack, self.got, self.shards = pack, got, shards
        self.send_sem, self.recv_sem = sems

    def own(self, name, core):
        at = self.place.at
        return self.gather.arrays[name].at[core, at[Y], at[X], at[Z]]

    def copies(self):
        core = self.place.core
        pairs = [(self.pack, self.got)]
        for name in (OUT, DOWN):
            shard = self.shards[name]
            columns = pl.ds(pl.multiple_of((1 - core) * 512, 512), 512)
            rows = pl.ds(pl.multiple_of(core * 16, 16), 16)
            pairs.append((shard.at[:, columns], self.own(name, 1 - core).at[rows, :]))
        return [
            push(src, dst, self.send_sem.at[i], self.recv_sem.at[i], self.place.sibling)
            for i, (src, dst) in enumerate(pairs)
        ]

    COLUMNS = ((INA, 0, 1024), (INB, 1024, 1024), (GU, 2048, 2048), (SMALL, 4096, 128))

    def run(self, greet):
        core, at = self.place.core, self.place.at
        wide = jnp.float32
        for name, low, size in self.COLUMNS[:3]:
            ref = self.shards[GU] if name == GU else self.shards[INA]
            first = 2048 if name == INB else 0
            both = jnp.concatenate(
                [
                    ref[:, first + size * half : first + size * half + size].astype(wide)
                    for half in range(2)
                ],
                axis=0,
            )
            self.pack[:, low : low + size] = both.astype(jnp.bfloat16)
        small = self.shards[SMALL][...]
        self.pack[:, 4096:4224] = jnp.concatenate([small, small], axis=0).astype(jnp.bfloat16)
        greet()
        copies = self.copies()
        for copy in copies:
            copy.start()
        for name in (OUT, DOWN):
            columns = pl.ds(pl.multiple_of(core * 512, 512), 512)
            rows = pl.ds(pl.multiple_of(core * 16, 16), 16)
            self.own(name, core)[rows, :] = self.shards[name][:, columns]
        copies[0].wait_recv()
        for name, low, size in self.COLUMNS:
            mine = self.pack[:, low : low + size].astype(wide)
            other = self.got[:, low : low + size].astype(wide)
            other = jnp.concatenate([other[8:16], other[0:8]], axis=0)
            upper = lax.broadcasted_iota(jnp.int32, (16, size), 0) < 8
            take = upper == (core == 0)
            block = jnp.where(take, mine, other).astype(jnp.bfloat16)
            if name == SMALL:
                self.gather.arrays[name][at[Y], at[X], at[Z]] = block
            else:
                self.own(name, core)[...] = block
        for copy in copies[1:]:
            copy.wait_recv()

    def finish(self):
        for copy in self.copies():
            copy.wait_send()


class Scatter:
    COUNTS = (48, 12, 3)

    def __init__(self, place, grads, first, second, third, send_sem, recv_sem):
        self.place, self.grads = place, grads
        self.got = (first, second, third)
        self.send_sem, self.recv_sem = send_sem, recv_sem

    def send_slot(self, name, phase):
        return self.send_sem.at[3 * name + phase]

    def recv_slot(self, name, phase, early=False):
        return self.recv_sem.at[4 * name + (3 if early else phase)]

    def slab(self, name, part, phase, step, half=None):
        order = ORDERS[part][::-1]
        where = {axis: self.place.at[axis] for axis in order[:phase]}
        where[order[phase]] = self.place.moved(order[phase], step)
        if half is not None:
            where |= halved(part, order[phase], half, order[phase:])
        return self.grads[name].at[block_index(where, *PARTS[name][part])]

    def landing(self, name, part, phase, slot, half=None):
        low, high = PARTS[name][part]
        lead = [slice(None)] * (2 - phase)
        if half is not None:
            lead[0] = pl.ds(2 * half, 2)
        return (slot, *lead, slice(None), pl.ds(low, high - low))

    def push(self, name, part, phase, to, source, half, slot, early=False):
        dst = self.got[phase][name].at[self.landing(name, part, phase, slot, half)]
        push(
            self.slab(name, part, phase, source, half),
            dst,
            self.send_slot(name, phase),
            self.recv_slot(name, phase, early),
            self.place.peer(ORDERS[part][2 - phase], to),
        ).start()

    def start(self, name, phase, parts=None):
        for part in range(len(PARTS[name])) if parts is None else parts:
            if phase or name == SMALL:
                for slot, step in enumerate(STEPS):
                    self.push(name, part, phase, step, step, None, slot)
            else:
                self.push(name, part, 0, 3, 2, 0, 2, True)
                self.push(name, part, 0, 1, 2, 1, 2, True)
                self.push(name, part, 0, 3, 3, 1, 0)
                self.push(name, part, 0, 1, 1, 0, 1)

    def arrived(self, name, phase, early=False):
        count = self.COUNTS[phase]
        if phase == 0 and name != SMALL:
            count = 16 if early else 32
        slot = self.recv_slot(name, phase, early)
        expect(self.grads[name], count, slot, self.place).wait_recv()

    def hand_on(self, name):
        self.arrived(name, 0, True)
        for part in range(len(PARTS[name])):
            for step, half, slot in ((3, 0, 0), (1, 1, 1)):
                own = self.slab(name, part, 0, step, half)
                came = self.got[0][name].at[self.landing(name, part, 0, 2, half)]

                def body(i):
                    own[i] = (own[i].astype(jnp.float32) + came[i].astype(jnp.float32)).astype(
                        jnp.bfloat16
                    )

                each(2, body)
                self.push(name, part, 0, step, step, half, slot)

    def add(self, name, part, phase, pick=()):
        total = self.slab(name, part, phase, 0)[(*pick, Ellipsis)].astype(jnp.float32)
        for slot in range(3 if phase or name == SMALL else 2):
            piece = self.got[phase][name].at[self.landing(name, part, phase, slot)]
            total = total + piece[(*pick, Ellipsis)].astype(jnp.float32)
        return total

    def relay(self, name, phase):
        self.arrived(name, phase)
        for part in range(len(PARTS[name])):
            own = self.slab(name, part, phase, 0)

            def body(i):
                own[i] = self.add(name, part, phase, (i,)).astype(jnp.bfloat16)

            each(4, body)
            self.start(name, phase + 1, (part,))

    def finish(self):
        for name in WEIGHTS:
            for phase, count in enumerate(self.COUNTS):
                slot = self.send_slot(name, phase)
                expect(self.grads[name], count, slot, self.place).wait_send()


class SumAll:
    def __init__(self, place, got, send_sem, recv_sem):
        self.place, self.got = place, got
        self.send_sem, self.recv_sem = send_sem, recv_sem

    def start(self, stage, value):
        if stage == 0:
            slot, devices = self.place.core, [self.place.sibling]
        else:
            axis = AXES[stage - 1]
            slot, devices = self.place.at[axis], [self.place.peer(axis, s) for s in STEPS]
        self.got[stage, slot] = value
        view = self.got.at[stage, slot]
        for device in devices:
            push(view, view, self.send_sem.at[stage], self.recv_sem.at[stage], device).start()

    def expect(self, stage):
        view = self.got.at[stage, pl.ds(0, 3 if stage else 1)]
        return push(
            view, view, self.send_sem.at[stage], self.recv_sem.at[stage], self.place.sibling
        )

    def total(self, stage):
        self.expect(stage).wait_recv()
        total = self.got[stage, 0]
        for slot in range(1, 4 if stage else 2):
            total = total + self.got[stage, slot]
        return total

    def finish(self):
        for stage in range(4):
            self.expect(stage).wait_send()


class End:
    def __init__(self, place, ends, got, outs, send_sem, recv_sem):
        self.place, self.ends, self.got, self.outs = place, ends, got, outs
        self.send_sem, self.recv_sem = send_sem, recv_sem

    def rows(self, name, core):
        half = ROWS[name] // 2
        return pl.ds(pl.multiple_of(core * half, 8), half)

    def copy(self, name):
        slot = name - 1
        return push(
            self.ends[name].at[self.rows(name, 1 - self.place.core), :],
            self.got[name],
            self.send_sem.at[slot],
            self.recv_sem.at[slot],
            self.place.sibling,
        )

    def columns(self, name, core):
        size = COLS[name]
        first = 2048 if name == INB else 0
        return pl.ds(pl.multiple_of(first + core * size, size), size)

    def start(self, name):
        self.copy(name).start()
        core = self.place.core
        self.outs[name][:, self.columns(name, core)] = self.ends[name][self.rows(name, core), :]

    def take(self, name):
        self.copy(name).wait_recv()
        self.outs[name][:, self.columns(name, 1 - self.place.core)] = self.got[name][...]

    def finish(self):
        for name in WEIGHTS[1:]:
            self.copy(name).wait_send()


LOW, WIDE = jnp.bfloat16, jnp.float32


def dot(left, right):
    return jnp.dot(left, right, preferred_element_type=WIDE)


def dot_back(left, right):
    return lax.dot_general(left, right, (((1,), (1,)), ((), ())), preferred_element_type=WIDE)


def dot_over_rows(left, right):
    return lax.dot_general(left, right, (((0,), (0,)), ((), ())), preferred_element_type=WIDE)


def exact_dot(left, right):
    return jnp.dot(left, right, precision=lax.Precision.HIGHEST, preferred_element_type=WIDE)


def sigmoid(v):
    return 1.0 / (1.0 + jnp.exp(-v))


def tile(index, size):
    return pl.ds(pl.multiple_of(index * size, size), size)


def lanes(shape):
    return lax.broadcasted_iota(jnp.int32, shape, len(shape) - 1)


def rows_of(shape):
    return lax.broadcasted_iota(jnp.int32, shape, 0)


def pair_stack(value):
    first = lanes(value.shape) < HD
    zero = jnp.zeros_like(value)
    return jnp.concatenate([jnp.where(first, value, zero), jnp.where(first, zero, value)], axis=0)


def pair_join(stacked):
    first = lanes((TOK, 128)) < HD
    return jnp.where(first, stacked[:TOK], stacked[TOK:])


def swap_halves(value):
    first = lax.rem(lanes(value.shape), HD) < HD // 2
    return jnp.where(first, pltpu.roll(value, 128 - HD // 2, 1), pltpu.roll(value, HD // 2, 1))


def doubled(value, which):
    first = lanes(value.shape) < HD
    turned = pltpu.roll(value, HD, 1)
    return jnp.where(first, value, turned) if which == 0 else jnp.where(first, turned, value)


class Layer:
    def __init__(self, refs):
        vars(self).update(refs)


    def enter(self):
        self.vectors[...] = jnp.zeros((8, 1792), WIDE)
        self.skip_sum[...] = jnp.zeros((8, 1536), WIDE)
        self.heads[...] = jnp.zeros((8, 128), WIDE)
        self.heads[0:1, 0:24] = self.decay_log[...]
        self.heads[1:2, 0:24] = self.step_bias[...]
        own = self.small_shard
        own[...] = jnp.zeros((8, 128), WIDE)
        own[0:2, 0:8] = self.norm_gains[...].astype(WIDE)
        own[2:7, 0:14] = self.conv_params[...].astype(WIDE)
        own[7:8, 0:12] = self.mixer_scale[...].astype(WIDE)
        moved = pltpu.roll(own[...], 32, 1)
        own[...] = jnp.zeros((8, 128), WIDE)
        own[:, 0:24] = self.in_shard[:, 4096:4120].astype(WIDE)
        own[...] = own[...] + moved

    def tables(self):
        position = rows_of((TOK, 128)).astype(WIDE)
        column = lax.rem(lanes((TOK, 128)), HD // 2).astype(WIDE)
        angle = position * jnp.exp(column * (-2.0 * math.log(rope_base) / HD))
        sine = jnp.sin(angle)
        first = lax.rem(lanes((TOK, 128)), HD) < HD // 2
        self.cosines[...] = jnp.cos(angle)
        self.sines[...] = jnp.where(first, -sine, sine)
        first = lanes((1, 128)) < HD
        for i in range(12):
            self.skip[0:1, 128 * i : 128 * i + 128] = jnp.where(
                first,
                self.mixer_skip[0:1, 2 * i : 2 * i + 1],
                self.mixer_skip[0:1, 2 * i + 1 : 2 * i + 2],
            )

    def spread(self):
        self.small_wide[...] = self.g_small[...].astype(WIDE).reshape(1024, 128)

        def turned(row):
            got = self.small_wide[pl.ds(row, 128, stride=8), :]
            return jnp.transpose(got)[32:48]

        for group, size, first, count, into in (
            (8, 1024, 0, 2, self.gains),
            (14, 1792, 2, 5, self.taps),
            (12, 1536, 7, 1, self.scale),
        ):
            stacked = jnp.concatenate([turned(first + i) for i in range(count)], axis=0)
            stacked = stacked.astype(LOW)
            for low in range(0, size, 256):
                start = rows_of((128, 256)) * group
                column = lanes((128, 256)) + low
                hot = (column >= start) & (column < start + group)
                index = jnp.sum(jnp.where(hot, start, 0).astype(WIDE), axis=0, keepdims=True)
                within = (lanes((1, 256)) + low).astype(WIDE) - index
                found = dot(stacked, jnp.where(hot, 1.0, 0.0).astype(LOW))
                mask = rows_of((16, 256)).astype(WIDE) == within
                for i in range(count):
                    into[i : i + 1, low : low + 256] = jnp.sum(
                        jnp.where(mask, found[16 * i : 16 * i + 16], 0.0), axis=0, keepdims=True
                    )


    def norm_in(self):
        x = self.tokens[...].astype(WIDE)
        self.inverse_in[...] = lax.rsqrt(jnp.mean(x * x, axis=-1, keepdims=True) + norm_eps)
        normed = x * self.inverse_in[...] * self.gains[0:1, :]
        self.normed[...] = normed.astype(LOW)
        self.left_in[:, 0:128] = jnp.transpose(normed).astype(LOW)

    def project(self):
        for weights, first in ((self.g_ina, 0), (self.g_inb, 2048)):

            def body(i):
                weight = weights[lax.div(i, 2), :, :, :, :, tile(lax.rem(i, 2), 512)]
                self.proj[:, pl.ds(pl.multiple_of(first + i * 512, 512), 512)] = dot(
                    self.normed[...], weight.reshape(1024, 512)
                )

            each(4, body)
        raw = dot(self.normed[...], self.g_small[...].reshape(1024, 128))
        self.step_raw[...] = jnp.where(lanes((TOK, 128)) < MIXER_HEADS, raw, 0.0)

    def convolved(self, i):
        low = 128 * i
        own = self.proj[:, 2304 + low : 2432 + low]
        row = rows_of((TOK, 128))
        shifted = [own] + [
            jnp.where(row >= k, pltpu.roll(own, k, 0), 0.0) for k in range(1, CONVK)
        ]
        total = self.taps[4:5, low : low + 128]
        for k in range(CONVK):
            total = total + self.taps[3 - k : 4 - k, low : low + 128] * shifted[k]
        return shifted, total

    def activate(self):
        for i in range(14):
            _, total = self.convolved(i)
            active = total * sigmoid(total)
            self.active[:, 128 * i : 128 * i + 128] = active
            self.active_low[:, 128 * i : 128 * i + 128] = active.astype(LOW)

    def steps(self):
        raw = self.step_raw[...] + self.heads[1:2, :]
        step = jnp.maximum(raw, 0.0) + jnp.log1p(jnp.exp(-jnp.abs(raw)))
        rate = -jnp.exp(self.heads[0:1, :])
        lower = jnp.where(rows_of((TOK, TOK)) >= lanes((TOK, TOK)), 1.0, 0.0)
        total = exact_dot(lower, step * rate)
        self.step[...] = step
        self.cum[...] = total
        self.step_rows[...] = jnp.transpose(step)
        self.cum_rows[...] = jnp.transpose(total)

    def causal(self):
        return rows_of((TOK, TOK)) >= lanes((TOK, TOK))

    def attend(self):
        for i in range(5):
            value = self.proj[:, 128 * i : 128 * i + 128]
            turned = value * self.cosines[...] + swap_halves(value) * self.sines[...]
            self.turned[:, 128 * i : 128 * i + 128] = turned.astype(LOW)
        key = self.turned[:, 512:640].astype(WIDE)
        values = self.proj[:, 640:768]
        for which in range(2):
            self.keys[which] = doubled(key, which).astype(LOW)
            self.values[which] = doubled(values, which).astype(LOW)
        causal = self.causal()
        causal = jnp.concatenate([causal, causal], axis=0)
        for i in range(4):
            queries = pair_stack(self.turned[:, 128 * i : 128 * i + 128])
            scores = dot_back(queries, self.keys[i // 2]) * (1.0 / math.sqrt(HD))
            scores = jnp.where(causal, scores, masked_value)
            power = jnp.exp(scores - jnp.max(scores, axis=-1, keepdims=True))
            probs = power / jnp.sum(power, axis=-1, keepdims=True)
            self.probs[i] = probs
            self.mixed[:, 128 * i : 128 * i + 128] = pair_join(
                dot(probs.astype(LOW), self.values[i // 2])
            ).astype(LOW)

    def decay(self, head):
        gaps = self.cum[:, head : head + 1] - self.cum_rows[head : head + 1, :]
        return jnp.exp(jnp.where(self.causal(), gaps, masked_value))

    def mix(self):
        self.inner[...] = dot_back(self.active_low[:, 1664:1792], self.active_low[:, 1536:1664])
        inner = self.inner[...]
        square = jnp.zeros((TOK, 1), WIDE)
        for i in range(12):
            mixing = jnp.concatenate(
                [
                    inner * self.decay(head) * self.step_rows[head : head + 1, :]
                    for head in (2 * i, 2 * i + 1)
                ],
                axis=0,
            ).astype(LOW)
            self.mixing[i] = mixing
            at = slice(128 * i, 128 * i + 128)
            state = pair_join(dot(mixing, self.active_low[:, at]))
            central = state + self.skip[0:1, at] * self.active[:, at]
            self.central[:, at] = central
            gate = self.proj[:, 768 + 128 * i : 896 + 128 * i]
            gated = central * (gate * sigmoid(gate))
            square = square + jnp.sum(gated * gated, axis=-1, keepdims=True)
        inverse = lax.rsqrt(square * (1.0 / MIXER_FEATURES) + norm_eps)
        self.inverse_state[...] = inverse
        for i in range(12):
            at = slice(128 * i, 128 * i + 128)
            gate = self.proj[:, 768 + 128 * i : 896 + 128 * i]
            gated = self.central[:, at] * (gate * sigmoid(gate))
            self.mixed[:, 512 + 128 * i : 640 + 128 * i] = (
                gated * inverse * self.scale[0:1, at]
            ).astype(LOW)

    def turn_left(self, source, into, count):
        for i in range(count):
            block = source[:, 128 * i : 128 * i + 128].astype(WIDE)
            into[128 * i : 128 * i + 128, 0:128] = jnp.transpose(block).astype(LOW)

    def branch(self):
        for half in range(2):
            at = slice(512 * half, 512 * half + 512)
            self.residual[:, at] = self.tokens[:, at].astype(WIDE) + dot(
                self.mixed[...], self.g_out[half].reshape(2048, 512)
            )
        x = self.residual[...]
        self.inverse_ff[...] = lax.rsqrt(jnp.mean(x * x, axis=-1, keepdims=True) + norm_eps)
        normed = x * self.inverse_ff[...] * self.gains[1:2, :]
        self.normed_ff[...] = normed.astype(LOW)
        self.left_gu[:, 0:128] = jnp.transpose(normed).astype(LOW)

    def feed(self):
        for half in range(2):

            def body(i):
                weight = self.g_gu[half, :, :, :, :, tile(i, 512)].reshape(1024, 512)
                self.gate_up[:, pl.ds(pl.multiple_of(half * 2048 + i * 512, 512), 512)] = dot(
                    self.normed_ff[...], weight
                )

            each(4, body)
        for i in range(16):
            at = slice(128 * i, 128 * i + 128)
            gate = self.gate_up[:, at]
            self.hidden[:, at] = (
                gate * sigmoid(gate) * self.gate_up[:, 2048 + 128 * i : 2176 + 128 * i]
            ).astype(LOW)

    def down(self):
        for half in range(2):
            at = slice(512 * half, 512 * half + 512)
            self.layer_output[:, at] = (
                self.residual[:, at] + dot(self.hidden[...], self.g_down[half].reshape(2048, 512))
            ).astype(LOW)


    def back_down(self):
        def body(y):
            grad = dot_back(
                self.cotangent[:, 0:512], self.g_down[0, y].reshape(512, 512)
            ) + dot_back(self.cotangent[:, 512:1024], self.g_down[1, y].reshape(512, 512))
            at = tile(y, 512)
            gate = self.gate_up[:, at]
            up = self.gate_up[:, pl.ds(pl.multiple_of(2048 + y * 512, 512), 512)]
            share = sigmoid(gate)
            self.d_gate[:, at] = (grad * up * (share * (1.0 + gate * (1.0 - share)))).astype(LOW)
            self.d_gate[:, pl.ds(pl.multiple_of(2048 + y * 512, 512), 512)] = (
                grad * (gate * share)
            ).astype(LOW)

        each(4, body)

    def norm_back(self, grad, x, inverse, gain):
        turned = x * inverse
        d_gain = jnp.sum(grad * turned, axis=0, keepdims=True)
        scaled = grad * gain
        d_x = inverse * (scaled - turned * jnp.mean(scaled * turned, axis=-1, keepdims=True))
        return d_x, d_gain

    def back_feed(self):
        def body(y):
            grad = dot_back(self.d_gate[:, 0:2048], self.g_gu[0, y].reshape(256, 2048)) + dot_back(
                self.d_gate[:, 2048:4096], self.g_gu[1, y].reshape(256, 2048)
            )
            self.d_wide[:, tile(y, 256)] = grad

        each(4, body)
        d_x, d_gain = self.norm_back(
            self.d_wide[:, 0:1024], self.residual[...], self.inverse_ff[...], self.gains[1:2, :]
        )
        self.vectors[1:2, 0:1024] = d_gain
        d_residual = self.cotangent[...].astype(WIDE) + d_x
        self.residual[...] = d_residual
        self.d_branch[...] = d_residual.astype(LOW)

    def back_branch(self):
        def body(y):
            self.d_wide[:, tile(y, 512)] = dot_back(
                self.d_branch[:, 0:512], self.g_out[0, y].reshape(512, 512)
            ) + dot_back(self.d_branch[:, 512:1024], self.g_out[1, y].reshape(512, 512))

        each(4, body)

    def back_gated(self):
        inverse = self.inverse_state[...]
        mean = jnp.zeros((TOK, 1), WIDE)
        for i in range(12):
            at = slice(128 * i, 128 * i + 128)
            gate = self.proj[:, 768 + 128 * i : 896 + 128 * i]
            gated = self.central[:, at] * (gate * sigmoid(gate))
            grad = self.d_wide[:, 512 + 128 * i : 640 + 128 * i]
            turned = gated * inverse
            self.vectors[7:8, at] = jnp.sum(grad * turned, axis=0, keepdims=True)
            mean = mean + jnp.sum(grad * self.scale[0:1, at] * turned, axis=-1, keepdims=True)
        mean = mean * (1.0 / MIXER_FEATURES)
        for i in range(12):
            at = slice(128 * i, 128 * i + 128)
            gate = self.proj[:, 768 + 128 * i : 896 + 128 * i]
            share = sigmoid(gate)
            open_gate = gate * share
            central = self.central[:, at]
            grad = self.d_wide[:, 512 + 128 * i : 640 + 128 * i]
            d_gated = inverse * (
                grad * self.scale[0:1, at] - central * open_gate * inverse * mean
            )
            d_central = d_gated * open_gate
            self.d_proj[:, 768 + 128 * i : 896 + 128 * i] = (
                d_gated * central * (share * (1.0 + gate * (1.0 - share)))
            ).astype(LOW)
            self.d_state[:, at] = d_central.astype(LOW)
            self.d_active[:, at] = d_central * self.skip[0:1, at]
            self.skip_sum[0:1, at] = jnp.sum(
                d_central * self.active[:, at], axis=0, keepdims=True
            )

    def back_mix(self):
        inner = self.inner[...]
        self.d_inner[...] = jnp.zeros((TOK, TOK), WIDE)
        self.d_cum[...] = jnp.zeros((TOK, TOK), WIDE)
        self.flow_rows[...] = jnp.zeros((TOK, TOK), WIDE)
        self.d_step_rows[...] = jnp.zeros((TOK, TOK), WIDE)
        lane = lanes((TOK, TOK))
        for i in range(12):
            at = slice(128 * i, 128 * i + 128)
            stacked = pair_stack(self.d_state[:, at])
            d_mixing = dot_back(stacked, self.active_low[:, at])
            self.d_active[:, at] += dot_over_rows(self.mixing[i], stacked)
            for which, head in enumerate((2 * i, 2 * i + 1)):
                grad = d_mixing[TOK * which : TOK * which + TOK]
                decay = self.decay(head)
                step = self.step_rows[head : head + 1, :]
                faded = grad * decay
                self.d_inner[...] += faded * step
                part = faded * inner
                d_step = jnp.sum(part, axis=0, keepdims=True)
                self.d_step_rows[head : head + 1, :] = d_step
                self.flow_rows[head : head + 1, :] = d_step * step
                over = jnp.sum(part * step, axis=-1, keepdims=True)
                self.d_cum[...] = jnp.where(lane == head, over, self.d_cum[...])
        d_inner = self.d_inner[...].astype(LOW)
        self.d_active[:, 1664:1792] = dot(d_inner, self.active_low[:, 1536:1664])
        self.d_active[:, 1536:1664] = dot_over_rows(d_inner, self.active_low[:, 1664:1792])
        d_cum = self.d_cum[...] - jnp.transpose(self.flow_rows[...])
        upper = jnp.where(rows_of((TOK, TOK)) <= lanes((TOK, TOK)), 1.0, 0.0)
        d_rated = exact_dot(upper, d_cum)
        rate = -jnp.exp(self.heads[0:1, :])
        d_step = jnp.transpose(self.d_step_rows[...]) + d_rated * rate
        self.vectors[7:8, 1536:1664] = (
            jnp.sum(d_rated * self.step[...], axis=0, keepdims=True) * rate
        )
        raw = self.step_raw[...] + self.heads[1:2, :]
        d_raw = jnp.where(lane < MIXER_HEADS, d_step * sigmoid(raw), 0.0)
        self.vectors[7:8, 1664:1792] = jnp.sum(d_raw, axis=0, keepdims=True)
        self.right_dt[0:128, :] = d_raw.astype(LOW)
        hot = jnp.where(
            lax.div(rows_of((1536, 128)), MIXER_HEAD_SIZE) == lanes((1536, 128)), 1.0, 0.0
        )
        self.vectors[0:1, 1024:1152] = exact_dot(self.skip_sum[...], hot)[0:1]

    def back_attend(self):
        d_keys, d_values = [], []
        for i in range(4):
            at = slice(128 * i, 128 * i + 128)
            which = i // 2
            d_out = pair_stack(self.d_wide[:, at].astype(LOW))
            d_probs = dot_back(d_out, self.values[which])
            probs = self.probs[i]
            d_scores = probs * (d_probs - jnp.sum(probs * d_probs, axis=-1, keepdims=True))
            d_raw = (d_scores * (1.0 / math.sqrt(HD))).astype(LOW)
            self.unturn(i, pair_join(dot(d_raw, self.keys[which])))
            d_keys.append(dot_over_rows(d_raw, pair_stack(self.turned[:, at])))
            d_values.append(dot_over_rows(probs.astype(LOW), d_out))
        first = lanes((TOK, 128)) < HD

        def joined(parts):
            one, two = parts[0] + parts[1], parts[2] + parts[3]
            return jnp.where(first, one + pltpu.roll(one, HD, 1), two + pltpu.roll(two, HD, 1))

        self.unturn(4, joined(d_keys))
        self.d_proj[:, 640:768] = joined(d_values).astype(LOW)

    def unturn(self, i, grad):
        self.d_proj[:, 128 * i : 128 * i + 128] = (
            grad * self.cosines[...] - swap_halves(grad) * self.sines[...]
        ).astype(LOW)

    def back_activate(self):
        row = rows_of((TOK, 128))
        for i in range(14):
            at = slice(128 * i, 128 * i + 128)
            shifted, total = self.convolved(i)
            share = sigmoid(total)
            grad = self.d_active[:, at] * (share * (1.0 + total * (1.0 - share)))
            self.vectors[6:7, at] = jnp.sum(grad, axis=0, keepdims=True)
            d_in = self.taps[3:4, at] * grad
            for k in range(CONVK):
                self.vectors[5 - k : 6 - k, at] = jnp.sum(grad * shifted[k], axis=0, keepdims=True)
                if k:
                    later = jnp.where(row < TOK - k, pltpu.roll(grad, TOK - k, 0), 0.0)
                    d_in = d_in + self.taps[3 - k : 4 - k, at] * later
            self.d_proj[:, 2304 + 128 * i : 2432 + 128 * i] = d_in.astype(LOW)

    def back_project(self):
        small = self.g_small[...].reshape(1024, 128)
        self.d_wide[:, 0:1024] = dot_back(self.right_dt[0:128, :], small)

        def body(y):
            total = self.d_wide[:, tile(y, 256)]
            for half in range(2):
                low = 1024 * half
                total = total + dot_back(
                    self.d_proj[:, low : low + 1024], self.g_ina[half, y].reshape(256, 1024)
                )
                total = total + dot_back(
                    self.d_proj[:, 2048 + low : 3072 + low], self.g_inb[half, y].reshape(256, 1024)
                )
            self.d_wide[:, tile(y, 256)] = total

        each(4, body)
        d_x, d_gain = self.norm_back(
            self.d_wide[:, 0:1024],
            self.tokens[...].astype(WIDE),
            self.inverse_in[...],
            self.gains[0:1, :],
        )
        self.vectors[0:1, 0:1024] = d_gain
        self.input_grad[...] = (self.residual[...] + d_x).astype(LOW)


    def grad_wide(self, left, right, into):
        width = right.shape[1]
        size = min(width, 512)

        def body(i):
            y, at = lax.rem(i, 4), tile(lax.div(i, 4), size)
            block = dot(left[tile(y, 256), :], right[:, at])
            into[y, :, :, :, at] = block.astype(LOW).reshape(4, 4, 16, size)

        each(4 * (width // size), body)

    def grad_tall(self, left, right, into):
        def body(y):
            block = dot(left[tile(y, 512), :], right[...])
            into[y] = block.astype(LOW).reshape(4, 4, 32, 512)

        each(4, body)


class Swap:
    def __init__(self, place, layer, send_sem, recv_sem):
        self.place, self.layer = place, layer
        self.send_sem, self.recv_sem = send_sem, recv_sem
        self.lefts = (
            None, layer.left_in, None, layer.left_out, layer.left_gu, layer.left_down,
        )
        self.rights = (
            layer.right_dt, layer.right_ina, layer.right_inb, layer.right_out, layer.right_gu,
            layer.right_down,
        )
        self.sources = (
            None, layer.d_proj, layer.d_proj, layer.d_branch, layer.d_gate, layer.cotangent,
        )

    def half(self, name, core):
        size = COLS[name]
        first = 2048 if name == INB else 0
        return pl.ds(pl.multiple_of(first + core * size, size), size)

    def left_copy(self, name):
        ref = self.lefts[name]
        src, dst = ref.at[:, pl.ds(0, 128)], ref.at[:, pl.ds(128, 128)]
        return push(
            src, dst, self.send_sem.at[name], self.recv_sem.at[name], self.place.sibling
        )

    def right_copy(self, name):
        ref, source = self.rights[name], self.sources[name]
        if source is None:
            src = ref.at[pl.ds(0, 128), :]
        else:
            src = source.at[:, self.half(name, 1 - self.place.core)]
        slot = 6 + name
        return push(
            src,
            ref.at[pl.ds(128, 128), :],
            self.send_sem.at[slot],
            self.recv_sem.at[slot],
            self.place.sibling,
        )

    def start_left(self, name):
        self.left_copy(name).start()

    def start_right(self, name):
        ref, source = self.rights[name], self.sources[name]
        if source is not None:
            ref[0:128, :] = source[:, self.half(name, self.place.core)]
        self.right_copy(name).start()

    def arrived(self, name):
        if self.lefts[name] is not None:
            self.left_copy(name).wait_recv()
        self.right_copy(name).wait_recv()

    def finish(self):
        for name in WEIGHTS:
            if name != GU:
                self.right_copy(name).wait_send()
            if self.lefts[name] is not None:
                self.left_copy(name).wait_send()


INS = dict(
    tokens=0, cotangent=1, in_shard=2, out_shard=3, gu_shard=4, down_shard=5, norm_gains=6,
    conv_params=7, mixer_scale=8, decay_log=9, step_bias=10, mixer_skip=11,
)
OUTS = dict(
    layer_output=((TOK, 1024), LOW),
    input_grad=((TOK, 1024), LOW),
    grad_in=((8, 4120), WIDE),
    grad_out=((16, 1024), WIDE),
    grad_gu=((8, 4096), WIDE),
    grad_down=((16, 1024), WIDE),
    total=((8, 1792), WIDE),
)
SCRATCH = dict(
    g_small=((4, 4, 4, 16, 128), LOW),
    g_ina=((2, 4, 4, 4, 16, 1024), LOW),
    g_inb=((2, 4, 4, 4, 16, 1024), LOW),
    g_out=((2, 4, 4, 4, 32, 512), LOW),
    g_gu=((2, 4, 4, 4, 16, 2048), LOW),
    g_down=((2, 4, 4, 4, 32, 512), LOW),
    grad_small=((4, 4, 4, 16, 128), LOW),
    grad_down_low=((4, 4, 4, 32, 512), LOW),
    small_shard=((8, 128), WIDE),
    heads=((8, 128), WIDE),
    skip=((8, 1536), WIDE),
    cosines=((TOK, 128), WIDE),
    sines=((TOK, 128), WIDE),
    pack=((16, 4224), LOW),
    got=((16, 4224), LOW),
    small_wide=((1024, 128), WIDE),
    gains=((8, 1024), WIDE),
    taps=((8, 1792), WIDE),
    scale=((8, 1536), WIDE),
    normed=((TOK, 1024), LOW),
    inverse_in=((TOK, 1), WIDE),
    proj=((TOK, 4096), WIDE),
    step_raw=((TOK, 128), WIDE),
    active=((TOK, 1792), WIDE),
    active_low=((TOK, 1792), LOW),
    step=((TOK, TOK), WIDE),
    cum=((TOK, TOK), WIDE),
    step_rows=((TOK, TOK), WIDE),
    cum_rows=((TOK, TOK), WIDE),
    turned=((TOK, 640), LOW),
    keys=((2, TOK, 128), LOW),
    values=((2, TOK, 128), LOW),
    probs=((4, 256, TOK), WIDE),
    mixed=((TOK, 2048), LOW),
    inner=((TOK, TOK), WIDE),
    mixing=((12, 256, TOK), LOW),
    central=((TOK, 1536), WIDE),
    inverse_state=((TOK, 1), WIDE),
    residual=((TOK, 1024), WIDE),
    inverse_ff=((TOK, 1), WIDE),
    gate_up=((TOK, 4096), WIDE),
    d_gate=((TOK, 4096), LOW),
    d_branch=((TOK, 1024), LOW),
    d_state=((TOK, 1536), LOW),
    skip_sum=((8, 1536), WIDE),
    d_inner=((TOK, TOK), WIDE),
    d_cum=((TOK, TOK), WIDE),
    flow_rows=((TOK, TOK), WIDE),
    d_step_rows=((TOK, TOK), WIDE),
    vectors=((8, 1792), WIDE),
    left_in=((1024, 256), LOW),
    left_out=((2048, 256), LOW),
    left_gu=((1024, 256), LOW),
    left_down=((2048, 256), LOW),
    right_ina=((256, 1024), LOW),
    right_inb=((256, 1024), LOW),
    right_out=((256, 512), LOW),
    right_gu=((256, 2048), LOW),
    right_down=((256, 512), LOW),
    right_dt=((256, 128), LOW),
    sums=((4, 4, 8, 1792), WIDE),
)
LANDINGS = ((3, 4, 4), (3, 4), (3,))
SEMS = dict(
    enter=3, gather=43, scatter=24, sums=4, end=5, swap=12,
)


class Plan:
    def __init__(self, refs):
        names = [*INS, *OUTS, *SCRATCH]
        layer = Layer(dict(zip(names, refs)))
        rest = list(refs[len(names) :])
        landings = [[rest.pop(0) for _ in WEIGHTS] for _ in LANDINGS]
        ends = [None] + [rest.pop(0) for _ in WEIGHTS[1:]]
        ends_got = [None] + [rest.pop(0) for _ in WEIGHTS[1:]]
        sems = {name: (rest.pop(0), rest.pop(0)) for name in SEMS}
        layer.normed_ff, layer.hidden = layer.normed, layer.mixed
        layer.d_proj = layer.d_gate
        layer.d_wide = layer.gate_up.at[:, pl.ds(0, 2048)]
        layer.d_active = layer.gate_up.at[:, pl.ds(2048, 1792)]
        place = Place()
        arrays = (layer.g_small, layer.g_ina, layer.g_inb, layer.g_out, layer.g_gu, layer.g_down)
        shards = (
            layer.small_shard, layer.in_shard, None, layer.out_shard, layer.gu_shard,
            layer.down_shard,
        )
        grads = (
            layer.grad_small,
            layer.g_gu.at[1, :, :, :, :, pl.ds(0, 1024)],
            layer.g_gu.at[1, :, :, :, :, pl.ds(1024, 1024)],
            layer.g_out.at[0],
            layer.g_gu.at[0],
            layer.grad_down_low,
        )
        outs = (None, layer.grad_in, layer.grad_in, layer.grad_out, layer.grad_gu, layer.grad_down)
        self.place, self.layer, self.grads = place, layer, grads
        self.gather = Gather(place, arrays, *sems["gather"])
        self.enter = Enter(place, self.gather, layer.pack, layer.got, shards, sems["enter"])
        self.scatter = Scatter(place, grads, *landings, *sems["scatter"])
        self.sum_all = SumAll(place, layer.sums, *sems["sums"])
        self.end = End(place, ends, ends_got, outs, *sems["end"])
        self.swap = Swap(place, layer, *sems["swap"])

    def last(self, name):
        self.scatter.arrived(name, 2)
        for part, (low, high) in enumerate(PARTS[name]):
            value = self.scatter.add(name, part, 2)
            if name == SMALL:
                mine = jnp.where(self.place.core == 0, value[0:8], value[8:16])
                self.layer.grad_in[:, 4096:4120] = mine[:, 0:24]
            else:
                self.end.ends[name][:, low:high] = value
        if name != SMALL:
            self.end.start(name)


def layer_kernel(*refs):
    plan = Plan(refs)
    place, layer, grads, gather = plan.place, plan.layer, plan.grads, plan.gather
    enter, scatter, sum_all, end, swap = (
        plan.enter, plan.scatter, plan.sum_all, plan.end, plan.swap,
    )

    def onward(name, phase):
        gather.arrived(name, phase, 2 if phase and name != SMALL else 0)
        gather.start(name, phase + 1)
        if phase == 1 and name != SMALL:
            gather.pass_on(name, 0)

    def landed(name):
        gather.arrived(name, 2, 2)
        gather.pass_on(name, 2)

    arrive(place)
    layer.enter()
    enter.run(lambda: meet(place))
    for name in WEIGHTS:
        gather.start(name, 0)
    swap.start_right(DOWN)
    onward(SMALL, 0)
    onward(INA, 0)
    onward(INB, 0)
    onward(OUT, 0)
    onward(SMALL, 1)
    gather.hand_on(INA, 1)
    gather.hand_on(INB, 1)
    onward(GU, 0)
    gather.hand_on(OUT, 1)
    onward(INA, 1)
    onward(INB, 1)
    onward(DOWN, 0)
    onward(OUT, 1)
    gather.hand_on(GU, 1)
    layer.tables()
    gather.arrived(SMALL, 2)
    layer.spread()
    layer.norm_in()
    swap.start_left(INA)
    gather.hand_on(DOWN, 1)
    gather.hand_on(INA, 2)
    gather.hand_on(INB, 2)
    onward(GU, 1)
    gather.hand_on(OUT, 2)
    landed(INA)
    landed(INB)
    onward(DOWN, 1)
    gather.passed(INA)
    gather.passed(INB)
    layer.project()
    landed(OUT)
    layer.activate()
    layer.steps()
    gather.hand_on(GU, 2)
    layer.attend()
    layer.mix()
    gather.hand_on(DOWN, 2)
    gather.passed(OUT)
    layer.branch()
    swap.start_left(GU)
    layer.turn_left(layer.mixed, layer.left_out, 16)
    swap.start_left(OUT)
    landed(GU)
    gather.passed(GU)
    layer.feed()
    layer.turn_left(layer.hidden, layer.left_down, 16)
    swap.start_left(DOWN)
    landed(DOWN)
    swap.arrived(DOWN)
    layer.grad_tall(layer.left_down, layer.right_down, grads[DOWN])
    scatter.start(DOWN, 0)
    gather.passed(DOWN)
    layer.back_down()
    swap.start_right(GU)
    scatter.hand_on(DOWN)
    layer.down()
    layer.back_feed()
    swap.start_right(OUT)
    gather.finish(GU)
    swap.arrived(GU)
    layer.grad_wide(layer.left_gu, layer.right_gu, grads[GU])
    scatter.start(GU, 0)
    layer.back_branch()
    gather.finish(OUT)
    swap.arrived(OUT)
    layer.grad_tall(layer.left_out, layer.right_out, grads[OUT])
    scatter.start(OUT, 0)
    scatter.relay(DOWN, 0)
    swap.right_copy(GU).wait_send()
    layer.back_gated()
    layer.back_attend()
    swap.start_right(INA)
    scatter.hand_on(GU)
    swap.arrived(INA)
    layer.grad_wide(layer.left_in, layer.right_ina, grads[INA])
    scatter.start(INA, 0)
    layer.back_mix()
    swap.start_right(SMALL)
    scatter.hand_on(OUT)
    layer.back_activate()
    swap.start_right(INB)
    swap.arrived(SMALL)
    layer.grad_wide(layer.left_in, layer.right_dt, grads[SMALL])
    scatter.start(SMALL, 0)
    swap.arrived(INB)
    layer.grad_wide(layer.left_in, layer.right_inb, grads[INB])
    scatter.start(INB, 0)
    scatter.relay(DOWN, 1)
    scatter.relay(GU, 0)
    layer.back_project()
    sum_all.start(0, layer.vectors[...])
    scatter.hand_on(INA)
    scatter.relay(SMALL, 0)
    scatter.relay(OUT, 0)
    sum_all.start(1, sum_all.total(0))
    scatter.hand_on(INB)
    plan.last(DOWN)
    scatter.relay(SMALL, 1)
    scatter.relay(GU, 1)
    scatter.relay(INA, 0)
    scatter.relay(OUT, 1)
    sum_all.start(2, sum_all.total(1))
    scatter.relay(INB, 0)
    plan.last(GU)
    plan.last(SMALL)
    scatter.relay(INA, 1)
    plan.last(OUT)
    sum_all.start(3, sum_all.total(2))
    scatter.relay(INB, 1)
    plan.last(INA)
    plan.last(INB)
    for name in (DOWN, GU, OUT, INA, INB):
        end.take(name)
    layer.total[...] = sum_all.total(3)
    for name in (SMALL, INA, INB, DOWN):
        gather.finish(name)
    scatter.finish()
    sum_all.finish()
    end.finish()
    swap.finish()
    enter.finish()


def finish_kernel(*refs):
    ins, outs = refs[:7], refs[7:]
    for ref, into in zip(ins[:6], outs[:6]):
        into[...] = ref[...]
    me = lax.axis_index("fsdp")
    total = ins[6][...]
    column = lanes((8, 1792))

    def share(size):
        start = me * size
        picked = jnp.where((column >= start) & (column < start + size), total, 0.0)
        folded = picked[:, 0:128]
        for i in range(1, 14):
            folded = folded + picked[:, 128 * i : 128 * i + 128]
        return pltpu.roll(folded, lax.rem(1792 - start, 128), 1)

    outs[6][...] = share(8)[0:2, 0:8]
    outs[7][...] = share(14)[2:7, 0:14]
    outs[8][...] = share(12)[7:8, 0:12]
    outs[9][...] = total[7:8, 1536:1560]
    outs[10][...] = total[7:8, 1664:1688]
    outs[11][...] = total[0:1, 1024:1048]


def local(
    tokens, cotangent, input_weight, output_weight, gate_up_weight, down_weight,
    norm_gains, conv_params, mixer_scale, decay_log, step_bias, mixer_skip_factor,
):
    ins = (
        tokens, cotangent, input_weight, output_weight, gate_up_weight, down_weight, norm_gains,
        conv_params, mixer_scale, decay_log[None], step_bias[None], mixer_skip_factor[None],
    )
    blocks = [(ROWS[name], COLS[name]) for name in WEIGHTS]
    scratch = [pltpu.VMEM(*one) for one in SCRATCH.values()]
    scratch += [pltpu.VMEM(lead + block, LOW) for lead in LANDINGS for block in blocks]
    scratch += [pltpu.VMEM(block, WIDE) for block in blocks[1:]]
    scratch += [pltpu.VMEM((block[0] // 2, block[1]), WIDE) for block in blocks[1:]]
    scratch += [pltpu.SemaphoreType.DMA((count,)) for count in SEMS.values() for _ in range(2)]
    whole = pl.BlockSpec(memory_space=pltpu.VMEM)
    results = pl.pallas_call(
        layer_kernel,
        out_shape=[jax.ShapeDtypeStruct(*one) for one in OUTS.values()],
        in_specs=[whole] * len(INS),
        out_specs=[whole] * len(OUTS),
        scratch_shapes=scratch,
        compiler_params=pltpu.CompilerParams(
            collective_id=0, has_side_effects=True, vmem_limit_bytes=63 * 2**20
        ),
        name="layer",
    )(*ins)
    shares = [(2, 8), (5, 14), (1, 12), (1, 24), (1, 24), (1, 24)]
    final = pl.pallas_call(
        finish_kernel,
        out_shape=[jax.ShapeDtypeStruct(*one) for one in list(OUTS.values())[:6]]
        + [jax.ShapeDtypeStruct(one, WIDE) for one in shares],
        in_specs=[whole] * len(OUTS),
        out_specs=[whole] * 12,
        name="finish",
    )(*results)
    return (*final[:9], *(one[0] for one in final[9:]))


def solution(mesh):
    in_specs = (
        P("fsdp", None),
        P("fsdp", None),
        P("fsdp", None),
        P("fsdp", None),
        P("fsdp", None),
        P("fsdp", None),
        P(None, "fsdp"),
        P(None, "fsdp"),
        P(None, "fsdp"),
        P(),
        P(),
        P(),
    )
    out_specs = (
        P("fsdp", None),
        P("fsdp", None),
        P("fsdp", None),
        P("fsdp", None),
        P("fsdp", None),
        P("fsdp", None),
        P(None, "fsdp"),
        P(None, "fsdp"),
        P(None, "fsdp"),
        P(),
        P(),
        P(),
    )
    return jax.shard_map(local, mesh=mesh, in_specs=in_specs, out_specs=out_specs, check_vma=False)
```

time: 2570 us -> 142 us (0.06)
  waiting for transfers between devices: 2170 us -> 0 us
  blocking collectives: 196 us -> 0 us
  Pallas kernels: 0 us -> 141 us
  matrix products: 96.8 us -> 0 us
  other arithmetic: 39.7 us -> 0 us
  local copies, waits for them, and re-layouts: 37.2 us -> 0 us
    reduce_scatter x3 -> x0, waiting for transfers between devices: 1950 us -> none  [the longest x1 662 us: local(): lax.psum_scatter(grad_rows(normed_ff_low, d_gate_low), 'fsdp', scatter_di...]
    pallas_call x0 -> x2, Pallas kernels: none -> 141 us  [the longest x1 139 us: local(): pl.pallas_call(layer_kernel, out_shape=[jax.ShapeDtypeStruct(*one) for on...]
    unnamed x9 -> x0, waiting for transfers between devices: 115 us -> none
    all_gather x4 -> x0, waiting for transfers between devices: 104 us -> none  [the longest x1 61.5 us: local(): lax.all_gather(down_weight, 'fsdp', axis=0, tiled=True)]
    dot_general x30 -> x0, matrix products: 96.8 us -> none  [the longest x4 26.1 us: grad_rows(): lax.dot_general(left_low, right_low, (((0,), (0,)), ((), ())), preferred_...]
    all_gather x2 -> x0, blocking collectives: 68.1 us -> none  [the longest x1 34.5 us: local(): lax.all_gather(norm_gains, 'fsdp', axis=1, tiled=True)]
    psum x1 -> x0, blocking collectives: 64.2 us -> none  [local(): lax.psum((jnp.stack([d_gain_in, d_gain_ff]), d_conv, d_scale[None, :], d_...]
    unnamed x1 -> x0, blocking collectives: 63.6 us -> none
  transfers between devices with their start and end apart: 8 -> 0, of which waited for: 6 -> 0; matrix products, arithmetic and copies ran while one was open for 3% -> 0% of each run, Pallas kernels for 0% -> 0%
where the time goes in v1:
time: 142 us
  Pallas kernels  141 us (99%)
    pallas_call x1, Pallas kernels, local(): pl.pallas_call(layer_kernel, out_shape=[jax.ShapeDtypeStruct(*one) for on...  139 us

profile of v1, /device:TPU:1, one launch (start us, length us, event | category | flops | bytes accessed | tf_op | source)
XLA Modules:
  0.0 141.8 jit_solution(985896094530366632)
XLA Ops:
  0.6 138.8 %layer.1 = (bf16[128,1024]{1,0:T(8,128)(2,1)}, bf16[128,1024]{1,0:T(8,128)(2,1)}, f32[8,4120]{1,0:T(8,128)}, f32[16,1024]{1,0:T(8,128)}, f32[8,4096]{1,0:T(8,128...) custom-call(bf16[128,1024]{1,0:T(8,128)(2,1)} %refs_0_.1, bf16[128,1024]{1,0:T(8,128)(2,1)} %refs_1_.1, ...), custom_call_target="tpu_custom_call" | custom-call | tf_op jit(solution)/shard_map/layer/pallas_call | solution.py:1303
  139.5 2.2 %finish.1 = (bf16[128,1024]{1,0:T(8,128)(2,1)}, bf16[128,1024]{1,0:T(8,128)(2,1)}, f32[8,4120]{1,0:T(8,128)}, f32[16,1024]{1,0:T(8,128)}, f32[8,4096]{1,0:T(8,12...) custom-call(bf16[128,1024]{1,0:T(8,128)(2,1)} %get-tuple-element.31., ...), custom_call_target="tpu_custom_call" | custom-call | tf_op jit(solution)/shard_map/finish/pallas_call | solution.py:1315

commit v2 on v1

--- a/solution.py
+++ b/solution.py
@@ -22,18 +22,27 @@
 AXES = (Y, X, Z)
 ORDERS = ((X, Y, Z), (Y, Z, X), (Z, X, Y))
 STEPS = (1, 3, 2)
-SMALL, INA, INB, OUT, GU, DOWN = range(6)
-WEIGHTS = (SMALL, INA, INB, OUT, GU, DOWN)
-ROWS = (16, 16, 16, 32, 16, 32)
-COLS = (128, 1024, 1024, 512, 2048, 512)
+SMALL, INA, INB, OUT, GUA, GUB, DOWN = range(7)
+WEIGHTS = (SMALL, INA, INB, OUT, GUA, GUB, DOWN)
+ROWS = (16, 16, 16, 32, 16, 16, 32)
+COLS = (128, 1024, 1024, 512, 1024, 1024, 512)
+FIRST = (0, 0, 2048, 0, 0, 1024, 0)
+STRIDE = (0, 1024, 1024, 512, 2048, 2048, 512)
 PARTS = (
     ((0, 128),),
     ((0, 384), (384, 768), (768, 1024)),
     ((0, 384), (384, 640), (640, 1024)),
     ((0, 128), (128, 384), (384, 512)),
-    ((0, 768), (768, 1408), (1408, 2048)),
+    ((0, 384), (384, 768), (768, 1024)),
+    ((0, 384), (384, 640), (640, 1024)),
     ((0, 128), (128, 256), (256, 512)),
 )
+DIRECT = {SMALL: 3, INA: 2}
+BACK_DIRECT = {SMALL: 0, INB: 1}
+
+
+def half_columns(name, core):
+    return pl.ds(pl.multiple_of(FIRST[name] + core * STRIDE[name], 512), COLS[name])
 
 
 class Place:
@@ -90,7 +99,7 @@
 
 def some_blocks(ref, count):
     lead = {1: (0, 0, 0), 3: (0, 0, pl.ds(0, 3)), 4: (0, 0), 12: (0, pl.ds(0, 3)), 16: (0,)}
-    lead |= {32: (pl.ds(0, 2),), 48: (pl.ds(0, 3),), 64: (slice(None),)}
+    lead |= {2: (0, 0, pl.ds(0, 2)), 8: (0, pl.ds(0, 2)), 32: (pl.ds(0, 2),), 48: (pl.ds(0, 3),), 64: (slice(None),)}
     return ref.at[lead[count]]
 
 
@@ -122,7 +131,11 @@
     def recv_slot(self, name, phase, kind):
         if name == SMALL:
             return self.recv_sem.at[phase]
-        return self.recv_sem.at[8 * name - 5 + (0, 1, 4)[phase] + (min(kind, 2) if phase else 0)]
+        if phase < DIRECT.get(name, 1):
+            kind = 0
+        elif kind > 1:
+            kind = 2
+        return self.recv_sem.at[10 * name - 7 + (0, 1, 4)[phase] + kind]
 
     def slab(self, name, part, phase, step, half=None):
         order = ORDERS[part]
@@ -132,41 +145,61 @@
             where |= halved(part, order[phase], half, order[: phase + 1])
         return self.ref(name).at[block_index(where, *PARTS[name][part])]
 
-    def copy(self, name, part, phase, kind):
-        step, source, half = (
+    def copy(self, name, part, phase, kind, half=None, slot=None):
+        step, source, handed = (
             ((1, 0, None), (3, 0, None), (2, 0, None))
-            if phase == 0 or name == SMALL
+            if phase < DIRECT.get(name, 1)
             else ((1, 0, None), (3, 0, None), (1, 3, 0), (3, 1, 1))
         )[kind]
-        view = self.slab(name, part, phase, source, half)
+        view = self.slab(name, part, phase, source, handed if half is None else half)
         return push(
             view,
             view,
             self.send_slot(name, phase),
-            self.recv_slot(name, phase, kind),
+            self.recv_slot(name, phase, kind) if slot is None else slot,
             self.place.peer(ORDERS[part][phase], step),
         )
 
     def start(self, name, phase, kinds=(0, 1)):
-        if phase == 0 or name == SMALL:
+        if phase < DIRECT.get(name, 1):
             kinds = (0, 1, 2)
         for kind in kinds:
             for part in range(len(PARTS[name])):
                 self.copy(name, part, phase, kind).start()
 
+    def late_slot(self, name, kind):
+        return self.recv_sem.at[10 * name + kind]
+
+    def start_early(self, name):
+        for kind in (0, 1):
+            for part in range(len(PARTS[name])):
+                self.copy(name, part, 2, kind, kind).start()
+
+    def start_late(self, name):
+        for kind in (0, 1):
+            slot = self.late_slot(name, kind)
+            for part in range(len(PARTS[name])):
+                self.copy(name, part, 2, kind, 1 - kind, slot).start()
+
     def arrived(self, name, phase, kind=0):
         count = self.COUNTS[phase]
-        if phase and name != SMALL:
+        if phase >= DIRECT.get(name, 1):
             count //= 3
+            if phase == 2 and kind < 2:
+                count //= 2
         slot = self.recv_slot(name, phase, kind)
         expect(self.ref(name), count, slot, self.place).wait_recv()
 
-    def hand_on(self, name, phase):
-        for kind in (0, 1):
+    def hand_on(self, name, phase, kinds=(0, 1)):
+        for kind in kinds:
             self.arrived(name, phase, kind)
             self.start(name, phase, (kind + 2,))
-            if phase == 2:
-                self.pass_on(name, (3, 1)[kind])
+
+    def arrived_late(self, name, kinds=(0, 1)):
+        for kind in kinds:
+            slot = self.late_slot(name, kind)
+            expect(self.ref(name), 8, slot, self.place).wait_recv()
+            self.pass_on(name, (3, 1)[kind])
 
     def pass_on(self, name, step):
         for part in range(len(PARTS[name])):
@@ -175,12 +208,12 @@
                 view,
                 view,
                 self.send_slot(name, 3),
-                self.recv_sem.at[8 * name + 2],
+                self.recv_sem.at[10 * name + 2],
                 self.place.sibling,
             ).start()
 
     def passed(self, name):
-        expect(self.ref(name), 64, self.recv_sem.at[8 * name + 2], self.place).wait_recv()
+        expect(self.ref(name), 64, self.recv_sem.at[10 * name + 2], self.place).wait_recv()
 
     def finish(self, name):
         for phase in range(3 if name == SMALL else 4):
@@ -189,11 +222,8 @@
 
 
 def each(count, body):
-    def step(index, nothing):
+    for index in range(count):
         body(index)
-        return nothing
-
-    lax.fori_loop(0, count, step, 0)
 
 
 class Enter:
@@ -211,7 +241,7 @@
         pairs = [(self.pack, self.got)]
         for name in (OUT, DOWN):
             shard = self.shards[name]
-            columns = pl.ds(pl.multiple_of((1 - core) * 512, 512), 512)
+            columns = half_columns(name, 1 - core)
             rows = pl.ds(pl.multiple_of(core * 16, 16), 16)
             pairs.append((shard.at[:, columns], self.own(name, 1 - core).at[rows, :]))
         return [
@@ -219,22 +249,18 @@
             for i, (src, dst) in enumerate(pairs)
         ]
 
-    COLUMNS = ((INA, 0, 1024), (INB, 1024, 1024), (GU, 2048, 2048), (SMALL, 4096, 128))
+    COLUMNS = (
+        (INA, 0, 1024), (INB, 1024, 1024), (GUA, 2048, 1024), (GUB, 3072, 1024), (SMALL, 4096, 128),
+    )
 
     def run(self, greet):
         core, at = self.place.core, self.place.at
         wide = jnp.float32
-        for name, low, size in self.COLUMNS[:3]:
-            ref = self.shards[GU] if name == GU else self.shards[INA]
-            first = 2048 if name == INB else 0
-            both = jnp.concatenate(
-                [
-                    ref[:, first + size * half : first + size * half + size].astype(wide)
-                    for half in range(2)
-                ],
-                axis=0,
-            )
-            self.pack[:, low : low + size] = both.astype(jnp.bfloat16)
+        for name, low, size in self.COLUMNS[:4]:
+            both = [
+                self.shards[name][:, half_columns(name, half)].astype(wide) for half in range(2)
+            ]
+            self.pack[:, low : low + size] = jnp.concatenate(both, axis=0).astype(jnp.bfloat16)
         small = self.shards[SMALL][...]
         self.pack[:, 4096:4224] = jnp.concatenate([small, small], axis=0).astype(jnp.bfloat16)
         greet()
@@ -242,7 +268,7 @@
         for copy in copies:
             copy.start()
         for name in (OUT, DOWN):
-            columns = pl.ds(pl.multiple_of(core * 512, 512), 512)
+            columns = half_columns(name, core)
             rows = pl.ds(pl.multiple_of(core * 16, 16), 16)
             self.own(name, core)[rows, :] = self.shards[name][:, columns]
         copies[0].wait_recv()
@@ -277,7 +303,10 @@
         return self.send_sem.at[3 * name + phase]
 
     def recv_slot(self, name, phase, early=False):
-        return self.recv_sem.at[4 * name + (3 if early else phase)]
+        return self.recv_sem.at[5 * name + phase + (3 if early else 0)]
+
+    def direct(self, name, phase):
+        return phase >= BACK_DIRECT.get(name, 2)
 
     def slab(self, name, part, phase, step, half=None):
         order = ORDERS[part][::-1]
@@ -306,28 +335,28 @@
 
     def start(self, name, phase, parts=None):
         for part in range(len(PARTS[name])) if parts is None else parts:
-            if phase or name == SMALL:
+            if self.direct(name, phase):
                 for slot, step in enumerate(STEPS):
                     self.push(name, part, phase, step, step, None, slot)
             else:
-                self.push(name, part, 0, 3, 2, 0, 2, True)
-                self.push(name, part, 0, 1, 2, 1, 2, True)
-                self.push(name, part, 0, 3, 3, 1, 0)
-                self.push(name, part, 0, 1, 1, 0, 1)
+                self.push(name, part, phase, 3, 2, 0, 2, True)
+                self.push(name, part, phase, 1, 2, 1, 2, True)
+                self.push(name, part, phase, 3, 3, 1, 0)
+                self.push(name, part, phase, 1, 1, 0, 1)
 
     def arrived(self, name, phase, early=False):
         count = self.COUNTS[phase]
-        if phase == 0 and name != SMALL:
-            count = 16 if early else 32
+        if not self.direct(name, phase):
+            count = count // 3 * (1 if early else 2)
         slot = self.recv_slot(name, phase, early)
         expect(self.grads[name], count, slot, self.place).wait_recv()
 
-    def hand_on(self, name):
-        self.arrived(name, 0, True)
+    def hand_on(self, name, phase):
+        self.arrived(name, phase, True)
         for part in range(len(PARTS[name])):
             for step, half, slot in ((3, 0, 0), (1, 1, 1)):
-                own = self.slab(name, part, 0, step, half)
-                came = self.got[0][name].at[self.landing(name, part, 0, 2, half)]
+                own = self.slab(name, part, phase, step, half)
+                came = self.got[phase][name].at[self.landing(name, part, phase, 2, half)]
 
                 def body(i):
                     own[i] = (own[i].astype(jnp.float32) + came[i].astype(jnp.float32)).astype(
@@ -335,11 +364,11 @@
                     )
 
                 each(2, body)
-                self.push(name, part, 0, step, step, half, slot)
+                self.push(name, part, phase, step, step, half, slot)
 
     def add(self, name, part, phase, pick=()):
         total = self.slab(name, part, phase, 0)[(*pick, Ellipsis)].astype(jnp.float32)
-        for slot in range(3 if phase or name == SMALL else 2):
+        for slot in range(3 if self.direct(name, phase) else 2):
             piece = self.got[phase][name].at[self.landing(name, part, phase, slot)]
             total = total + piece[(*pick, Ellipsis)].astype(jnp.float32)
         return total
@@ -415,19 +444,14 @@
             self.place.sibling,
         )
 
-    def columns(self, name, core):
-        size = COLS[name]
-        first = 2048 if name == INB else 0
-        return pl.ds(pl.multiple_of(first + core * size, size), size)
-
     def start(self, name):
         self.copy(name).start()
         core = self.place.core
-        self.outs[name][:, self.columns(name, core)] = self.ends[name][self.rows(name, core), :]
+        self.outs[name][:, half_columns(name, core)] = self.ends[name][self.rows(name, core), :]
 
     def take(self, name):
         self.copy(name).wait_recv()
-        self.outs[name][:, self.columns(name, 1 - self.place.core)] = self.got[name][...]
+        self.outs[name][:, half_columns(name, 1 - self.place.core)] = self.got[name][...]
 
     def finish(self):
         for name in WEIGHTS[1:]:
@@ -458,7 +482,7 @@
 
 
 def tile(index, size):
-    return pl.ds(pl.multiple_of(index * size, size), size)
+    return pl.ds(index * size, size)
 
 
 def lanes(shape):
@@ -563,16 +587,15 @@
         self.normed[...] = normed.astype(LOW)
         self.left_in[:, 0:128] = jnp.transpose(normed).astype(LOW)
 
-    def project(self):
-        for weights, first in ((self.g_ina, 0), (self.g_inb, 2048)):
-
-            def body(i):
-                weight = weights[lax.div(i, 2), :, :, :, :, tile(lax.rem(i, 2), 512)]
-                self.proj[:, pl.ds(pl.multiple_of(first + i * 512, 512), 512)] = dot(
-                    self.normed[...], weight.reshape(1024, 512)
-                )
-
-            each(4, body)
+    def project_first(self):
+        for i in range(4):
+            weight = self.g_ina[i // 2, :, :, :, :, tile(i % 2, 512)]
+            self.proj[:, tile(i, 512)] = dot(self.normed[...], weight.reshape(1024, 512))
+
+    def project_last(self):
+        for i in range(4):
+            weight = self.g_inb[i // 2, :, :, :, :, tile(i % 2, 512)]
+            self.proj[:, tile(4 + i, 512)] = dot(self.normed[...], weight.reshape(1024, 512))
         raw = dot(self.normed[...], self.g_small[...].reshape(1024, 128))
         self.step_raw[...] = jnp.where(lanes((TOK, 128)) < MIXER_HEADS, raw, 0.0)
 
@@ -593,7 +616,6 @@
             _, total = self.convolved(i)
             active = total * sigmoid(total)
             self.active[:, 128 * i : 128 * i + 128] = active
-            self.active_low[:, 128 * i : 128 * i + 128] = active.astype(LOW)
 
     def steps(self):
         raw = self.step_raw[...] + self.heads[1:2, :]
@@ -627,7 +649,7 @@
             scores = jnp.where(causal, scores, masked_value)
             power = jnp.exp(scores - jnp.max(scores, axis=-1, keepdims=True))
             probs = power / jnp.sum(power, axis=-1, keepdims=True)
-            self.probs[i] = probs
+            self.small_wide[tile(i, 256), :] = probs
             self.mixed[:, 128 * i : 128 * i + 128] = pair_join(
                 dot(probs.astype(LOW), self.values[i // 2])
             ).astype(LOW)
@@ -637,7 +659,7 @@
         return jnp.exp(jnp.where(self.causal(), gaps, masked_value))
 
     def mix(self):
-        self.inner[...] = dot_back(self.active_low[:, 1664:1792], self.active_low[:, 1536:1664])
+        self.inner[...] = dot_back(self.active[:, 1664:1792].astype(LOW), self.active[:, 1536:1664].astype(LOW))
         inner = self.inner[...]
         square = jnp.zeros((TOK, 1), WIDE)
         for i in range(12):
@@ -650,7 +672,7 @@
             ).astype(LOW)
             self.mixing[i] = mixing
             at = slice(128 * i, 128 * i + 128)
-            state = pair_join(dot(mixing, self.active_low[:, at]))
+            state = pair_join(dot(mixing, self.active[:, at].astype(LOW)))
             central = state + self.skip[0:1, at] * self.active[:, at]
             self.central[:, at] = central
             gate = self.proj[:, 768 + 128 * i : 896 + 128 * i]
@@ -683,22 +705,18 @@
         self.normed_ff[...] = normed.astype(LOW)
         self.left_gu[:, 0:128] = jnp.transpose(normed).astype(LOW)
 
-    def feed(self):
-        for half in range(2):
-
-            def body(i):
-                weight = self.g_gu[half, :, :, :, :, tile(i, 512)].reshape(1024, 512)
-                self.gate_up[:, pl.ds(pl.multiple_of(half * 2048 + i * 512, 512), 512)] = dot(
-                    self.normed_ff[...], weight
-                )
-
-            each(4, body)
-        for i in range(16):
+    def feed(self, weights, first):
+        for i in range(2):
+            for half in range(2):
+                weight = weights[half, :, :, :, :, tile(i, 512)].reshape(1024, 512)
+                low = 2048 * half + first + 512 * i
+                self.gate_up[:, low : low + 512] = dot(self.normed_ff[...], weight)
+        for i in range(first // 128, first // 128 + 8):
             at = slice(128 * i, 128 * i + 128)
             gate = self.gate_up[:, at]
-            self.hidden[:, at] = (
-                gate * sigmoid(gate) * self.gate_up[:, 2048 + 128 * i : 2176 + 128 * i]
-            ).astype(LOW)
+            hidden = gate * sigmoid(gate) * self.gate_up[:, 2048 + 128 * i : 2176 + 128 * i]
+            self.hidden[:, at] = hidden.astype(LOW)
+            self.left_down[at, 0:128] = jnp.transpose(hidden).astype(LOW)
 
     def down(self):
         for half in range(2):
@@ -708,21 +726,21 @@
             ).astype(LOW)
 
 
-    def back_down(self):
-        def body(y):
+    def back_down(self, first):
+        for y in (first, first + 1):
             grad = dot_back(
                 self.cotangent[:, 0:512], self.g_down[0, y].reshape(512, 512)
             ) + dot_back(self.cotangent[:, 512:1024], self.g_down[1, y].reshape(512, 512))
-            at = tile(y, 512)
-            gate = self.gate_up[:, at]
-            up = self.gate_up[:, pl.ds(pl.multiple_of(2048 + y * 512, 512), 512)]
-            share = sigmoid(gate)
-            self.d_gate[:, at] = (grad * up * (share * (1.0 + gate * (1.0 - share)))).astype(LOW)
-            self.d_gate[:, pl.ds(pl.multiple_of(2048 + y * 512, 512), 512)] = (
-                grad * (gate * share)
-            ).astype(LOW)
-
-        each(4, body)
+            for i in range(4):
+                low = 512 * y + 128 * i
+                part = grad[:, 128 * i : 128 * i + 128]
+                gate = self.gate_up[:, low : low + 128]
+                up = self.gate_up[:, 2048 + low : 2176 + low]
+                share = sigmoid(gate)
+                self.d_gate[:, low : low + 128] = (
+                    part * up * (share * (1.0 + gate * (1.0 - share)))
+                ).astype(LOW)
+                self.d_gate[:, 2048 + low : 2176 + low] = (part * (gate * share)).astype(LOW)
 
     def norm_back(self, grad, x, inverse, gain):
         turned = x * inverse
@@ -731,20 +749,25 @@
         d_x = inverse * (scaled - turned * jnp.mean(scaled * turned, axis=-1, keepdims=True))
         return d_x, d_gain
 
-    def back_feed(self):
-        def body(y):
-            grad = dot_back(self.d_gate[:, 0:2048], self.g_gu[0, y].reshape(256, 2048)) + dot_back(
-                self.d_gate[:, 2048:4096], self.g_gu[1, y].reshape(256, 2048)
-            )
-            self.d_wide[:, tile(y, 256)] = grad
-
-        each(4, body)
+    def back_feed(self, weights, first):
+        for y in range(4):
+            total = None if first == 0 else self.d_wide[:, tile(y, 256)]
+            for half in range(2):
+                low = 2048 * half + first
+                part = dot_back(
+                    self.d_gate[:, low : low + 1024], weights[half, y].reshape(256, 1024)
+                )
+                total = part if total is None else total + part
+            self.d_wide[:, tile(y, 256)] = total
+
+    def back_residual(self):
         d_x, d_gain = self.norm_back(
             self.d_wide[:, 0:1024], self.residual[...], self.inverse_ff[...], self.gains[1:2, :]
         )
         self.vectors[1:2, 0:1024] = d_gain
         d_residual = self.cotangent[...].astype(WIDE) + d_x
-        self.residual[...] = d_residual
+        self.proj[:, 0:768] = d_residual[:, 0:768]
+        self.gate_up[:, 3840:4096] = d_residual[:, 768:1024]
         self.d_branch[...] = d_residual.astype(LOW)
 
     def back_branch(self):
@@ -797,7 +820,7 @@
         for i in range(12):
             at = slice(128 * i, 128 * i + 128)
             stacked = pair_stack(self.d_state[:, at])
-            d_mixing = dot_back(stacked, self.active_low[:, at])
+            d_mixing = dot_back(stacked, self.active[:, at].astype(LOW))
             self.d_active[:, at] += dot_over_rows(self.mixing[i], stacked)
             for which, head in enumerate((2 * i, 2 * i + 1)):
                 grad = d_mixing[TOK * which : TOK * which + TOK]
@@ -812,8 +835,8 @@
                 over = jnp.sum(part * step, axis=-1, keepdims=True)
                 self.d_cum[...] = jnp.where(lane == head, over, self.d_cum[...])
         d_inner = self.d_inner[...].astype(LOW)
-        self.d_active[:, 1664:1792] = dot(d_inner, self.active_low[:, 1536:1664])
-        self.d_active[:, 1536:1664] = dot_over_rows(d_inner, self.active_low[:, 1664:1792])
+        self.d_active[:, 1664:1792] = dot(d_inner, self.active[:, 1536:1664].astype(LOW))
+        self.d_active[:, 1536:1664] = dot_over_rows(d_inner, self.active[:, 1664:1792].astype(LOW))
         d_cum = self.d_cum[...] - jnp.transpose(self.flow_rows[...])
         upper = jnp.where(rows_of((TOK, TOK)) <= lanes((TOK, TOK)), 1.0, 0.0)
         d_rated = exact_dot(upper, d_cum)
@@ -838,7 +861,7 @@
             which = i // 2
             d_out = pair_stack(self.d_wide[:, at].astype(LOW))
             d_probs = dot_back(d_out, self.values[which])
-            probs = self.probs[i]
+            probs = self.small_wide[tile(i, 256), :]
             d_scores = probs * (d_probs - jnp.sum(probs * d_probs, axis=-1, keepdims=True))
             d_raw = (d_scores * (1.0 / math.sqrt(HD))).astype(LOW)
             self.unturn(i, pair_join(dot(d_raw, self.keys[which])))
@@ -898,26 +921,22 @@
             self.gains[0:1, :],
         )
         self.vectors[0:1, 0:1024] = d_gain
-        self.input_grad[...] = (self.residual[...] + d_x).astype(LOW)
+        d_residual = jnp.concatenate([self.proj[:, 0:768], self.gate_up[:, 3840:4096]], axis=1)
+        self.input_grad[...] = (d_residual + d_x).astype(LOW)
 
 
     def grad_wide(self, left, right, into):
         width = right.shape[1]
         size = min(width, 512)
-
-        def body(i):
-            y, at = lax.rem(i, 4), tile(lax.div(i, 4), size)
-            block = dot(left[tile(y, 256), :], right[:, at])
-            into[y, :, :, :, at] = block.astype(LOW).reshape(4, 4, 16, size)
-
-        each(4 * (width // size), body)
+        for n in range(width // size):
+            for y in range(4):
+                block = dot(left[tile(y, 256), :], right[:, tile(n, size)])
+                into[y, :, :, :, tile(n, size)] = block.astype(LOW).reshape(4, 4, 16, size)
 
     def grad_tall(self, left, right, into):
-        def body(y):
+        for y in range(4):
             block = dot(left[tile(y, 512), :], right[...])
             into[y] = block.astype(LOW).reshape(4, 4, 32, 512)
-
-        each(4, body)
 
 
 class Swap:
@@ -925,20 +944,16 @@
         self.place, self.layer = place, layer
         self.send_sem, self.recv_sem = send_sem, recv_sem
         self.lefts = (
-            None, layer.left_in, None, layer.left_out, layer.left_gu, layer.left_down,
+            None, layer.left_in, None, layer.left_out, layer.left_gu, None, layer.left_down,
         )
         self.rights = (
-            layer.right_dt, layer.right_ina, layer.right_inb, layer.right_out, layer.right_gu,
-            layer.right_down,
+            layer.right_dt, layer.right_ina, layer.right_inb, layer.right_out, layer.right_gua,
+            layer.right_gub, layer.right_down,
         )
         self.sources = (
-            None, layer.d_proj, layer.d_proj, layer.d_branch, layer.d_gate, layer.cotangent,
-        )
-
-    def half(self, name, core):
-        size = COLS[name]
-        first = 2048 if name == INB else 0
-        return pl.ds(pl.multiple_of(first + core * size, size), size)
+            None, layer.d_proj, layer.d_proj, layer.d_branch, layer.d_gate, layer.d_gate,
+            layer.cotangent,
+        )
 
     def left_copy(self, name):
         ref = self.lefts[name]
@@ -952,8 +967,8 @@
         if source is None:
             src = ref.at[pl.ds(0, 128), :]
         else:
-            src = source.at[:, self.half(name, 1 - self.place.core)]
-        slot = 6 + name
+            src = source.at[:, half_columns(name, 1 - self.place.core)]
+        slot = 7 + name
         return push(
             src,
             ref.at[pl.ds(128, 128), :],
@@ -968,7 +983,7 @@
     def start_right(self, name):
         ref, source = self.rights[name], self.sources[name]
         if source is not None:
-            ref[0:128, :] = source[:, self.half(name, self.place.core)]
+            ref[0:128, :] = source[:, half_columns(name, self.place.core)]
         self.right_copy(name).start()
 
     def arrived(self, name):
@@ -978,7 +993,7 @@
 
     def finish(self):
         for name in WEIGHTS:
-            if name != GU:
+            if name not in (GUA, GUB):
                 self.right_copy(name).wait_send()
             if self.lefts[name] is not None:
                 self.left_copy(name).wait_send()
@@ -1002,7 +1017,8 @@
     g_ina=((2, 4, 4, 4, 16, 1024), LOW),
     g_inb=((2, 4, 4, 4, 16, 1024), LOW),
     g_out=((2, 4, 4, 4, 32, 512), LOW),
-    g_gu=((2, 4, 4, 4, 16, 2048), LOW),
+    g_gua=((2, 4, 4, 4, 16, 1024), LOW),
+    g_gub=((2, 4, 4, 4, 16, 1024), LOW),
     g_down=((2, 4, 4, 4, 32, 512), LOW),
     grad_small=((4, 4, 4, 16, 128), LOW),
     grad_down_low=((4, 4, 4, 32, 512), LOW),
@@ -1022,7 +1038,6 @@
     proj=((TOK, 4096), WIDE),
     step_raw=((TOK, 128), WIDE),
     active=((TOK, 1792), WIDE),
-    active_low=((TOK, 1792), LOW),
     step=((TOK, TOK), WIDE),
     cum=((TOK, TOK), WIDE),
     step_rows=((TOK, TOK), WIDE),
@@ -1030,7 +1045,6 @@
     turned=((TOK, 640), LOW),
     keys=((2, TOK, 128), LOW),
     values=((2, TOK, 128), LOW),
-    probs=((4, 256, TOK), WIDE),
     mixed=((TOK, 2048), LOW),
     inner=((TOK, TOK), WIDE),
     mixing=((12, 256, TOK), LOW),
@@ -1055,14 +1069,15 @@
     right_ina=((256, 1024), LOW),
     right_inb=((256, 1024), LOW),
     right_out=((256, 512), LOW),
-    right_gu=((256, 2048), LOW),
+    right_gua=((256, 1024), LOW),
+    right_gub=((256, 1024), LOW),
     right_down=((256, 512), LOW),
     right_dt=((256, 128), LOW),
     sums=((4, 4, 8, 1792), WIDE),
 )
 LANDINGS = ((3, 4, 4), (3, 4), (3,))
 SEMS = dict(
-    enter=3, gather=43, scatter=24, sums=4, end=5, swap=12,
+    enter=3, gather=63, scatter=35, sums=4, end=6, swap=14,
 )
 
 
@@ -1080,20 +1095,27 @@
         layer.d_wide = layer.gate_up.at[:, pl.ds(0, 2048)]
         layer.d_active = layer.gate_up.at[:, pl.ds(2048, 1792)]
         place = Place()
-        arrays = (layer.g_small, layer.g_ina, layer.g_inb, layer.g_out, layer.g_gu, layer.g_down)
+        arrays = (
+            layer.g_small, layer.g_ina, layer.g_inb, layer.g_out, layer.g_gua, layer.g_gub,
+            layer.g_down,
+        )
         shards = (
-            layer.small_shard, layer.in_shard, None, layer.out_shard, layer.gu_shard,
-            layer.down_shard,
+            layer.small_shard, layer.in_shard, layer.in_shard, layer.out_shard, layer.gu_shard,
+            layer.gu_shard, layer.down_shard,
         )
         grads = (
             layer.grad_small,
-            layer.g_gu.at[1, :, :, :, :, pl.ds(0, 1024)],
-            layer.g_gu.at[1, :, :, :, :, pl.ds(1024, 1024)],
+            layer.g_gua.at[1],
+            layer.g_gub.at[1],
             layer.g_out.at[0],
-            layer.g_gu.at[0],
+            layer.g_gua.at[0],
+            layer.g_gub.at[0],
             layer.grad_down_low,
         )
-        outs = (None, layer.grad_in, layer.grad_in, layer.grad_out, layer.grad_gu, layer.grad_down)
+        outs = (
+            None, layer.grad_in, layer.grad_in, layer.grad_out, layer.grad_gu, layer.grad_gu,
+            layer.grad_down,
+        )
         self.place, self.layer, self.grads = place, layer, grads
         self.gather = Gather(place, arrays, *sems["gather"])
         self.enter = Enter(place, self.gather, layer.pack, layer.got, shards, sems["enter"])
@@ -1123,10 +1145,15 @@
     )
 
     def onward(name, phase):
-        gather.arrived(name, phase, 2 if phase and name != SMALL else 0)
-        gather.start(name, phase + 1)
-        if phase == 1 and name != SMALL:
-            gather.pass_on(name, 0)
+        gather.arrived(name, phase, 0 if phase < DIRECT.get(name, 1) else 2)
+        if phase == 0 or name == SMALL:
+            gather.start(name, phase + 1)
+        else:
+            gather.start_early(name)
+
+    def onward_late(name):
+        gather.start_late(name)
+        gather.pass_on(name, 0)
 
     def landed(name):
         gather.arrived(name, 2, 2)
@@ -1135,123 +1162,185 @@
     arrive(place)
     layer.enter()
     enter.run(lambda: meet(place))
-    for name in WEIGHTS:
-        gather.start(name, 0)
+    gather.start(SMALL, 0)
+    gather.start(INA, 0)
+    gather.start(INB, 0)
+    gather.start(OUT, 0)
+    gather.start(GUA, 0)
+    gather.start(DOWN, 0)
+    gather.start(GUB, 0)
     swap.start_right(DOWN)
+    layer.tables()
     onward(SMALL, 0)
     onward(INA, 0)
     onward(INB, 0)
     onward(OUT, 0)
+    onward(GUA, 0)
+    onward(DOWN, 0)
+    onward(GUB, 0)
     onward(SMALL, 1)
-    gather.hand_on(INA, 1)
-    gather.hand_on(INB, 1)
-    onward(GU, 0)
-    gather.hand_on(OUT, 1)
+    gather.hand_on(INB, 1, (0,))
+    gather.hand_on(INB, 1, (1,))
     onward(INA, 1)
+    onward_late(INA)
+    gather.hand_on(OUT, 1, (0,))
+    gather.hand_on(OUT, 1, (1,))
+    gather.hand_on(GUA, 1, (0,))
+    gather.hand_on(GUA, 1, (1,))
+    gather.hand_on(DOWN, 1, (0,))
+    gather.hand_on(DOWN, 1, (1,))
+    gather.hand_on(GUB, 1, (0,))
+    gather.hand_on(GUB, 1, (1,))
     onward(INB, 1)
-    onward(DOWN, 0)
-    onward(OUT, 1)
-    gather.hand_on(GU, 1)
-    layer.tables()
     gather.arrived(SMALL, 2)
     layer.spread()
     layer.norm_in()
     swap.start_left(INA)
-    gather.hand_on(DOWN, 1)
-    gather.hand_on(INA, 2)
-    gather.hand_on(INB, 2)
-    onward(GU, 1)
-    gather.hand_on(OUT, 2)
+    gather.hand_on(INA, 2, (0,))
+    gather.hand_on(INA, 2, (1,))
+    onward_late(INB)
+    gather.arrived_late(INA, (0,))
+    gather.arrived_late(INA, (1,))
+    onward(OUT, 1)
+    onward(GUA, 1)
+    gather.hand_on(INB, 2, (0,))
+    gather.hand_on(INB, 2, (1,))
+    onward_late(OUT)
     landed(INA)
+    gather.passed(INA)
+    layer.project_first()
+    gather.arrived_late(INB, (0,))
+    gather.arrived_late(INB, (1,))
+    onward(DOWN, 1)
+    layer.attend()
+    gather.hand_on(OUT, 2, (0,))
+    gather.hand_on(OUT, 2, (1,))
+    onward_late(GUA)
+    gather.hand_on(GUA, 2, (0,))
+    gather.hand_on(GUA, 2, (1,))
+    onward_late(DOWN)
     landed(INB)
-    onward(DOWN, 1)
-    gather.passed(INA)
+    gather.arrived_late(OUT, (0,))
+    gather.arrived_late(OUT, (1,))
     gather.passed(INB)
-    layer.project()
-    landed(OUT)
+    layer.project_last()
     layer.activate()
     layer.steps()
-    gather.hand_on(GU, 2)
-    layer.attend()
+    gather.hand_on(DOWN, 2, (0,))
+    gather.hand_on(DOWN, 2, (1,))
     layer.mix()
-    gather.hand_on(DOWN, 2)
+    landed(OUT)
+    onward(GUB, 1)
+    onward_late(GUB)
+    gather.arrived_late(GUA, (0,))
+    gather.arrived_late(GUA, (1,))
     gather.passed(OUT)
     layer.branch()
-    swap.start_left(GU)
+    swap.start_left(GUA)
     layer.turn_left(layer.mixed, layer.left_out, 16)
     swap.start_left(OUT)
-    landed(GU)
-    gather.passed(GU)
-    layer.feed()
-    layer.turn_left(layer.hidden, layer.left_down, 16)
+    landed(GUA)
+    gather.arrived_late(DOWN, (0,))
+    gather.arrived_late(DOWN, (1,))
+    landed(DOWN)
+    gather.passed(GUA)
+    layer.feed(layer.g_gua, 0)
+    gather.hand_on(GUB, 2, (0,))
+    gather.hand_on(GUB, 2, (1,))
+    gather.passed(DOWN)
+    layer.back_down(0)
+    swap.start_right(GUA)
+    gather.arrived_late(GUB, (0,))
+    gather.arrived_late(GUB, (1,))
+    layer.back_feed(layer.g_gua, 0)
+    gather.finish(GUA)
+    swap.arrived(GUA)
+    layer.grad_wide(layer.left_gu, layer.right_gua, grads[GUA])
+    scatter.start(GUA, 0)
+    landed(GUB)
+    gather.passed(GUB)
+    layer.feed(layer.g_gub, 1024)
     swap.start_left(DOWN)
-    landed(DOWN)
+    layer.back_down(2)
+    swap.start_right(GUB)
+    layer.back_feed(layer.g_gub, 1024)
+    layer.back_residual()
+    swap.start_right(OUT)
+    scatter.hand_on(GUA, 0)
     swap.arrived(DOWN)
     layer.grad_tall(layer.left_down, layer.right_down, grads[DOWN])
     scatter.start(DOWN, 0)
-    gather.passed(DOWN)
-    layer.back_down()
-    swap.start_right(GU)
-    scatter.hand_on(DOWN)
-    layer.down()
-    layer.back_feed()
-    swap.start_right(OUT)
-    gather.finish(GU)
-    swap.arrived(GU)
-    layer.grad_wide(layer.left_gu, layer.right_gu, grads[GU])
-    scatter.start(GU, 0)
+    gather.finish(GUB)
+    swap.arrived(GUB)
+    layer.grad_wide(layer.left_gu, layer.right_gub, grads[GUB])
+    scatter.start(GUB, 0)
     layer.back_branch()
+    swap.right_copy(GUA).wait_send()
+    swap.right_copy(GUB).wait_send()
+    layer.back_gated()
+    layer.back_attend()
+    swap.start_right(INA)
+    scatter.relay(GUA, 0)
+    scatter.hand_on(DOWN, 0)
+    layer.back_mix()
+    swap.start_right(SMALL)
     gather.finish(OUT)
     swap.arrived(OUT)
     layer.grad_tall(layer.left_out, layer.right_out, grads[OUT])
     scatter.start(OUT, 0)
-    scatter.relay(DOWN, 0)
-    swap.right_copy(GU).wait_send()
-    layer.back_gated()
-    layer.back_attend()
-    swap.start_right(INA)
-    scatter.hand_on(GU)
+    scatter.hand_on(GUB, 0)
     swap.arrived(INA)
     layer.grad_wide(layer.left_in, layer.right_ina, grads[INA])
     scatter.start(INA, 0)
-    layer.back_mix()
-    swap.start_right(SMALL)
-    scatter.hand_on(OUT)
     layer.back_activate()
     swap.start_right(INB)
+    scatter.hand_on(GUA, 1)
     swap.arrived(SMALL)
     layer.grad_wide(layer.left_in, layer.right_dt, grads[SMALL])
     scatter.start(SMALL, 0)
+    layer.down()
     swap.arrived(INB)
     layer.grad_wide(layer.left_in, layer.right_inb, grads[INB])
     scatter.start(INB, 0)
-    scatter.relay(DOWN, 1)
-    scatter.relay(GU, 0)
     layer.back_project()
     sum_all.start(0, layer.vectors[...])
-    scatter.hand_on(INA)
+    scatter.relay(DOWN, 0)
+    scatter.hand_on(OUT, 0)
+    sum_all.start(1, sum_all.total(0))
+    scatter.relay(GUB, 0)
+    scatter.hand_on(INA, 0)
+    scatter.relay(GUA, 1)
     scatter.relay(SMALL, 0)
+    scatter.hand_on(INB, 0)
+    scatter.hand_on(DOWN, 1)
     scatter.relay(OUT, 0)
-    sum_all.start(1, sum_all.total(0))
-    scatter.hand_on(INB)
+    scatter.hand_on(GUB, 1)
+    sum_all.start(2, sum_all.total(1))
+    scatter.relay(INA, 0)
+    plan.last(GUA)
+    scatter.relay(SMALL, 1)
+    end.take(GUA)
+    scatter.relay(INB, 0)
+    scatter.relay(DOWN, 1)
+    scatter.hand_on(OUT, 1)
+    scatter.relay(GUB, 1)
+    scatter.hand_on(INA, 1)
+    sum_all.start(3, sum_all.total(2))
+    plan.last(SMALL)
+    scatter.relay(OUT, 1)
+    scatter.relay(INB, 1)
+    scatter.relay(INA, 1)
     plan.last(DOWN)
-    scatter.relay(SMALL, 1)
-    scatter.relay(GU, 1)
-    scatter.relay(INA, 0)
-    scatter.relay(OUT, 1)
-    sum_all.start(2, sum_all.total(1))
-    scatter.relay(INB, 0)
-    plan.last(GU)
-    plan.last(SMALL)
-    scatter.relay(INA, 1)
+    plan.last(GUB)
+    end.take(DOWN)
+    end.take(GUB)
+    layer.total[...] = sum_all.total(3)
     plan.last(OUT)
-    sum_all.start(3, sum_all.total(2))
-    scatter.relay(INB, 1)
+    plan.last(INB)
     plan.last(INA)
-    plan.last(INB)
-    for name in (DOWN, GU, OUT, INA, INB):
-        end.take(name)
-    layer.total[...] = sum_all.total(3)
+    end.take(OUT)
+    end.take(INB)
+    end.take(INA)
     for name in (SMALL, INA, INB, DOWN):
         gather.finish(name)
     scatter.finish()
@@ -1307,7 +1396,7 @@
         out_specs=[whole] * len(OUTS),
         scratch_shapes=scratch,
         compiler_params=pltpu.CompilerParams(
-            collective_id=0, has_side_effects=True, vmem_limit_bytes=63 * 2**20
+            collective_id=0, has_side_effects=True, vmem_limit_bytes=127 * 2**19
         ),
         name="layer",
     )(*ins)

time: 142 us -> 127 us (0.89)
  Pallas kernels: 141 us -> 126 us
    pallas_call x1, Pallas kernels: 139 us -> 123 us  [local(): pl.pallas_call(layer_kernel, out_shape=[jax.ShapeDtypeStruct(*one) for on...]
where the time goes in v2:
time: 127 us; the launch traced here: 126 us
  Pallas kernels  126 us (99%)
    pallas_call x1, Pallas kernels, local(): pl.pallas_call(layer_kernel, out_shape=[jax.ShapeDtypeStruct(*one) for on...  123 us

profile of v2, /device:TPU:1, one launch (start us, length us, event | category | flops | bytes accessed | tf_op | source)
XLA Modules:
  0.0 126.5 jit_solution(6645091353529956071)
XLA Ops:
  0.6 123.4 %layer.1 = (bf16[128,1024]{1,0:T(8,128)(2,1)}, bf16[128,1024]{1,0:T(8,128)(2,1)}, f32[8,4120]{1,0:T(8,128)}, f32[16,1024]{1,0:T(8,128)}, f32[8,4096]{1,0:T(8,128...) custom-call(bf16[128,1024]{1,0:T(8,128)(2,1)} %refs_0_.1, bf16[128,1024]{1,0:T(8,128)(2,1)} %refs_1_.1, ...), custom_call_target="tpu_custom_call" | custom-call | tf_op jit(solution)/shard_map/layer/pallas_call | solution.py:1392
  124.1 2.2 %finish.1 = (bf16[128,1024]{1,0:T(8,128)(2,1)}, bf16[128,1024]{1,0:T(8,128)(2,1)}, f32[8,4120]{1,0:T(8,128)}, f32[16,1024]{1,0:T(8,128)}, f32[8,4096]{1,0:T(8,12...) custom-call(bf16[128,1024]{1,0:T(8,128)(2,1)} %get-tuple-element.31., ...), custom_call_target="tpu_custom_call" | custom-call | tf_op jit(solution)/shard_map/finish/pallas_call | solution.py:1404

commit v3 on v2

--- a/solution.py
+++ b/solution.py
@@ -20,29 +20,42 @@
 
 Y, X, Z = range(3)
 AXES = (Y, X, Z)
+STEPS = (1, 3, 2)
+SMALL, INA, INB, OUT, GU, DOWN = range(6)
+WEIGHTS = (SMALL, INA, INB, OUT, GU, DOWN)
+PAIRED = (GU, DOWN)
+ROWS = (16, 16, 16, 32, 16, 32)
+COLS = (128, 1024, 1024, 512, 1024, 512)
+FIRST = (0, 0, 2048, 0, 0, 0)
+DEPTH = (4, 4, 4, 4, 4, 2)
 ORDERS = ((X, Y, Z), (Y, Z, X), (Z, X, Y))
-STEPS = (1, 3, 2)
-SMALL, INA, INB, OUT, GUA, GUB, DOWN = range(7)
-WEIGHTS = (SMALL, INA, INB, OUT, GUA, GUB, DOWN)
-ROWS = (16, 16, 16, 32, 16, 16, 32)
-COLS = (128, 1024, 1024, 512, 1024, 1024, 512)
-FIRST = (0, 0, 2048, 0, 0, 1024, 0)
-STRIDE = (0, 1024, 1024, 512, 2048, 2048, 512)
+PAIR_ORDERS = ((Y, X, Z), (Y, Z, X))
 PARTS = (
     ((0, 128),),
+    ((0, 256), (256, 512), (512, 1024)),
     ((0, 384), (384, 768), (768, 1024)),
-    ((0, 384), (384, 640), (640, 1024)),
-    ((0, 128), (128, 384), (384, 512)),
-    ((0, 384), (384, 768), (768, 1024)),
-    ((0, 384), (384, 640), (640, 1024)),
     ((0, 128), (128, 256), (256, 512)),
+    ((0, 512), (512, 1024)),
+    ((0, 256), (256, 512)),
 )
-DIRECT = {SMALL: 3, INA: 2}
-BACK_DIRECT = {SMALL: 0, INB: 1}
+DIRECT = {SMALL: 3, INA: 2, INB: 2, OUT: 2}
+BACK_DIRECT = {SMALL: 0, INB: 1, OUT: 1}
+
+
+def order_of(name, part):
+    return (PAIR_ORDERS if name in PAIRED else ORDERS)[part]
+
+
+def extent(name, axis):
+    return DEPTH[name] if axis == Y else 4
+
+
+def steps_of(name, axis):
+    return (2,) if name in PAIRED and axis == Y else STEPS
 
 
 def half_columns(name, core):
-    return pl.ds(pl.multiple_of(FIRST[name] + core * STRIDE[name], 512), COLS[name])
+    return pl.ds(pl.multiple_of(FIRST[name] + core * COLS[name], 512), COLS[name])
 
 
 class Place:
@@ -52,9 +65,18 @@
         self.core = lax.rem(me, 2)
         self.at = [lax.div(me, 32), lax.rem(lax.div(me, 8), 4), lax.rem(lax.div(me, 2), 4)]
         self.sibling = me + 1 - 2 * self.core
+        self.parity = lax.rem(self.at[Y], 2)
+        self.pair = lax.div(self.at[Y], 2)
+        self.mate = me + 32 - 64 * self.parity
 
     def moved(self, axis, step):
         return lax.rem(self.at[axis] + step, 4)
+
+    def spot(self, name, axis, step):
+        if name in PAIRED and axis == Y:
+            pair = lax.rem(self.pair + step // 2, 2)
+            return pl.ds(2 * pair, 2) if name == GU else pair
+        return self.moved(axis, step)
 
     def peer(self, axis, step):
         at = list(self.at)
@@ -97,25 +119,32 @@
     )
 
 
-def some_blocks(ref, count):
-    lead = {1: (0, 0, 0), 3: (0, 0, pl.ds(0, 3)), 4: (0, 0), 12: (0, pl.ds(0, 3)), 16: (0,)}
-    lead |= {2: (0, 0, pl.ds(0, 2)), 8: (0, pl.ds(0, 2)), 32: (pl.ds(0, 2),), 48: (pl.ds(0, 3),), 64: (slice(None),)}
-    return ref.at[lead[count]]
-
-
 def expect(ref, count, sem, place):
-    view = some_blocks(ref, count)
+    sizes = [
+        (i, j, k)
+        for i in range(1, ref.shape[0] + 1)
+        for j in range(1, 5)
+        for k in range(1, 5)
+        if i * j * k == count
+    ][0]
+    view = ref.at[tuple(pl.ds(0, size) for size in sizes)]
     return push(view, view, sem, sem, place.sibling)
 
 
-def halved(part, phase_axis, half, order):
-    axis = min(one for one in order if one != phase_axis)
-    return {axis: pl.ds(2 * half, 2)}
+def halved(name, axes, half):
+    axis = min(axes)
+    size = extent(name, axis) // 2
+    return {axis: pl.ds(size * half, size)}
+
+
+def slab_blocks(name, axes, axis):
+    count = 2 if name == GU and axis == Y else 1
+    for one in axes:
+        count *= extent(name, one)
+    return count
 
 
 class Gather:
-    COUNTS = (3, 12, 48)
-
     def __init__(self, place, arrays, send_sem, recv_sem):
         self.place, self.arrays = place, arrays
         self.send_sem, self.recv_sem = send_sem, recv_sem
@@ -125,30 +154,38 @@
             return self.arrays[name]
         return self.arrays[name].at[self.place.core]
 
+    def direct(self, name, phase):
+        return phase < DIRECT.get(name, 1)
+
+    def blocks(self, name, phase):
+        order = order_of(name, 0)
+        return slab_blocks(name, order[:phase], order[phase])
+
     def send_slot(self, name, phase):
         return self.send_sem.at[4 * name + phase]
 
     def recv_slot(self, name, phase, kind):
-        if name == SMALL:
-            return self.recv_sem.at[phase]
-        if phase < DIRECT.get(name, 1):
+        if self.direct(name, phase):
             kind = 0
         elif kind > 1:
             kind = 2
+        if name == SMALL:
+            return self.recv_sem.at[phase]
         return self.recv_sem.at[10 * name - 7 + (0, 1, 4)[phase] + kind]
 
     def slab(self, name, part, phase, step, half=None):
-        order = ORDERS[part]
-        where = {axis: self.place.at[axis] for axis in order[phase:]}
-        where[order[phase]] = self.place.moved(order[phase], step)
+        order = order_of(name, part)
+        where = {axis: self.place.spot(name, axis, 0) for axis in order[phase:]}
+        where[order[phase]] = self.place.spot(name, order[phase], step)
         if half is not None:
-            where |= halved(part, order[phase], half, order[: phase + 1])
+            where |= halved(name, order[:phase], half)
         return self.ref(name).at[block_index(where, *PARTS[name][part])]
 
     def copy(self, name, part, phase, kind, half=None, slot=None):
+        axis = order_of(name, part)[phase]
         step, source, handed = (
-            ((1, 0, None), (3, 0, None), (2, 0, None))
-            if phase < DIRECT.get(name, 1)
+            [(one, 0, None) for one in steps_of(name, axis)]
+            if self.direct(name, phase)
             else ((1, 0, None), (3, 0, None), (1, 3, 0), (3, 1, 1))
         )[kind]
         view = self.slab(name, part, phase, source, handed if half is None else half)
@@ -157,12 +194,12 @@
             view,
             self.send_slot(name, phase),
             self.recv_slot(name, phase, kind) if slot is None else slot,
-            self.place.peer(ORDERS[part][phase], step),
+            self.place.peer(axis, step),
         )
 
     def start(self, name, phase, kinds=(0, 1)):
-        if phase < DIRECT.get(name, 1):
-            kinds = (0, 1, 2)
+        if self.direct(name, phase):
+            kinds = range(len(steps_of(name, order_of(name, 0)[phase])))
         for kind in kinds:
             for part in range(len(PARTS[name])):
                 self.copy(name, part, phase, kind).start()
@@ -182,11 +219,11 @@
                 self.copy(name, part, 2, kind, 1 - kind, slot).start()
 
     def arrived(self, name, phase, kind=0):
-        count = self.COUNTS[phase]
-        if phase >= DIRECT.get(name, 1):
-            count //= 3
-            if phase == 2 and kind < 2:
-                count //= 2
+        count = self.blocks(name, phase)
+        if self.direct(name, phase):
+            count *= len(steps_of(name, order_of(name, 0)[phase]))
+        elif phase == 2 and kind < 2:
+            count //= 2
         slot = self.recv_slot(name, phase, kind)
         expect(self.ref(name), count, slot, self.place).wait_recv()
 
@@ -198,7 +235,7 @@
     def arrived_late(self, name, kinds=(0, 1)):
         for kind in kinds:
             slot = self.late_slot(name, kind)
-            expect(self.ref(name), 8, slot, self.place).wait_recv()
+            expect(self.ref(name), self.blocks(name, 2) // 2, slot, self.place).wait_recv()
             self.pass_on(name, (3, 1)[kind])
 
     def pass_on(self, name, step):
@@ -213,12 +250,20 @@
             ).start()
 
     def passed(self, name):
-        expect(self.ref(name), 64, self.recv_sem.at[10 * name + 2], self.place).wait_recv()
+        count = 16 * DEPTH[name]
+        expect(self.ref(name), count, self.recv_sem.at[10 * name + 2], self.place).wait_recv()
 
     def finish(self, name):
-        for phase in range(3 if name == SMALL else 4):
-            count = (*self.COUNTS, 64)[phase]
+        for phase in range(3):
+            count = self.blocks(name, phase)
+            if self.direct(name, phase):
+                count *= len(steps_of(name, order_of(name, 0)[phase]))
+            else:
+                count *= 3
             expect(self.ref(name), count, self.send_slot(name, phase), self.place).wait_send()
+        if name != SMALL:
+            slot = self.send_slot(name, 3)
+            expect(self.ref(name), 16 * DEPTH[name], slot, self.place).wait_send()
 
 
 def each(count, body):
@@ -227,39 +272,49 @@
 
 
 class Enter:
-    def __init__(self, place, gather, pack, got, shards, sems):
+    COLUMNS = ((INA, 0, 1024), (INB, 1024, 1024), (GU, 2048, 2048), (SMALL, 4096, 128))
+
+    def __init__(self, place, gather, pack, got, stage, shards, sems):
         self.place, self.gather = place, gather
-        self.pack, self.got, self.shards = pack, got, shards
+        self.pack, self.got, self.stage, self.shards = pack, got, stage, shards
         self.send_sem, self.recv_sem = sems
 
     def own(self, name, core):
         at = self.place.at
-        return self.gather.arrays[name].at[core, at[Y], at[X], at[Z]]
+        first = self.place.pair if name == DOWN else at[Y]
+        return self.gather.arrays[name].at[core, first, at[X], at[Z]]
 
     def copies(self):
         core = self.place.core
         pairs = [(self.pack, self.got)]
         for name in (OUT, DOWN):
-            shard = self.shards[name]
-            columns = half_columns(name, 1 - core)
             rows = pl.ds(pl.multiple_of(core * 16, 16), 16)
-            pairs.append((shard.at[:, columns], self.own(name, 1 - core).at[rows, :]))
+            src = self.shards[name].at[:, half_columns(name, 1 - core)]
+            pairs.append((src, self.own(name, 1 - core).at[rows, :]))
         return [
             push(src, dst, self.send_sem.at[i], self.recv_sem.at[i], self.place.sibling)
             for i, (src, dst) in enumerate(pairs)
         ]
 
-    COLUMNS = (
-        (INA, 0, 1024), (INB, 1024, 1024), (GUA, 2048, 1024), (GUB, 3072, 1024), (SMALL, 4096, 128),
-    )
+    def mate_copy(self):
+        return push(
+            self.stage,
+            self.own(GU, self.place.core),
+            self.send_sem.at[3],
+            self.recv_sem.at[3],
+            self.place.mate,
+        )
 
     def run(self, greet):
         core, at = self.place.core, self.place.at
         wide = jnp.float32
-        for name, low, size in self.COLUMNS[:4]:
+        for name, low, size in self.COLUMNS[:3]:
+            first = FIRST[name]
             both = [
-                self.shards[name][:, half_columns(name, half)].astype(wide) for half in range(2)
+                self.shards[name][:, first + size * half : first + size * half + size]
+                for half in range(2)
             ]
+            both = [one.astype(wide) for one in both]
             self.pack[:, low : low + size] = jnp.concatenate(both, axis=0).astype(jnp.bfloat16)
         small = self.shards[SMALL][...]
         self.pack[:, 4096:4224] = jnp.concatenate([small, small], axis=0).astype(jnp.bfloat16)
@@ -268,9 +323,8 @@
         for copy in copies:
             copy.start()
         for name in (OUT, DOWN):
-            columns = half_columns(name, core)
             rows = pl.ds(pl.multiple_of(core * 16, 16), 16)
-            self.own(name, core)[rows, :] = self.shards[name][:, columns]
+            self.own(name, core)[rows, :] = self.shards[name][:, half_columns(name, core)]
         copies[0].wait_recv()
         for name, low, size in self.COLUMNS:
             mine = self.pack[:, low : low + size].astype(wide)
@@ -278,22 +332,29 @@
             other = jnp.concatenate([other[8:16], other[0:8]], axis=0)
             upper = lax.broadcasted_iota(jnp.int32, (16, size), 0) < 8
             take = upper == (core == 0)
-            block = jnp.where(take, mine, other).astype(jnp.bfloat16)
+            block = jnp.where(take, mine, other)
             if name == SMALL:
-                self.gather.arrays[name][at[Y], at[X], at[Z]] = block
+                self.gather.arrays[name][at[Y], at[X], at[Z]] = block.astype(jnp.bfloat16)
+            elif name == GU:
+                even = jnp.concatenate([block[:, 0:512], block[:, 1024:1536]], axis=1)
+                odd = jnp.concatenate([block[:, 512:1024], block[:, 1536:2048]], axis=1)
+                first = self.place.parity == 0
+                own = jnp.where(first, even, odd).astype(jnp.bfloat16)
+                self.own(GU, core)[...] = own
+                self.stage[...] = jnp.where(first, odd, even).astype(jnp.bfloat16)
+                self.mate_copy().start()
             else:
-                self.own(name, core)[...] = block
+                self.own(name, core)[...] = block.astype(jnp.bfloat16)
         for copy in copies[1:]:
             copy.wait_recv()
 
     def finish(self):
         for copy in self.copies():
             copy.wait_send()
+        self.mate_copy().wait_send()
 
 
 class Scatter:
-    COUNTS = (48, 12, 3)
-
     def __init__(self, place, grads, first, second, third, send_sem, recv_sem):
         self.place, self.grads = place, grads
         self.got = (first, second, third)
@@ -308,19 +369,32 @@
     def direct(self, name, phase):
         return phase >= BACK_DIRECT.get(name, 2)
 
+    def order(self, name, part):
+        return order_of(name, part)[::-1]
+
+    def blocks(self, name, phase):
+        order = self.order(name, 0)
+        return slab_blocks(name, order[phase + 1 :], order[phase])
+
+    def steps(self, name, phase):
+        return steps_of(name, self.order(name, 0)[phase])
+
     def slab(self, name, part, phase, step, half=None):
-        order = ORDERS[part][::-1]
-        where = {axis: self.place.at[axis] for axis in order[:phase]}
-        where[order[phase]] = self.place.moved(order[phase], step)
+        order = self.order(name, part)
+        where = {axis: self.place.spot(name, axis, 0) for axis in order[:phase]}
+        where[order[phase]] = self.place.spot(name, order[phase], step)
         if half is not None:
-            where |= halved(part, order[phase], half, order[phase:])
+            where |= halved(name, order[phase + 1 :], half)
         return self.grads[name].at[block_index(where, *PARTS[name][part])]
 
     def landing(self, name, part, phase, slot, half=None):
         low, high = PARTS[name][part]
-        lead = [slice(None)] * (2 - phase)
+        left = self.order(name, part)[phase + 1 :]
+        lead = [slice(None)] * len(left)
         if half is not None:
-            lead[0] = pl.ds(2 * half, 2)
+            lead[0] = halved(name, left, half)[min(left)]
+        if name == GU and phase == 2:
+            lead = [slice(None)]
         return (slot, *lead, slice(None), pl.ds(low, high - low))
 
     def push(self, name, part, phase, to, source, half, slot, early=False):
@@ -330,13 +404,13 @@
             dst,
             self.send_slot(name, phase),
             self.recv_slot(name, phase, early),
-            self.place.peer(ORDERS[part][2 - phase], to),
+            self.place.peer(self.order(name, part)[phase], to),
         ).start()
 
     def start(self, name, phase, parts=None):
         for part in range(len(PARTS[name])) if parts is None else parts:
             if self.direct(name, phase):
-                for slot, step in enumerate(STEPS):
+                for slot, step in enumerate(self.steps(name, phase)):
                     self.push(name, part, phase, step, step, None, slot)
             else:
                 self.push(name, part, phase, 3, 2, 0, 2, True)
@@ -345,9 +419,11 @@
                 self.push(name, part, phase, 1, 1, 0, 1)
 
     def arrived(self, name, phase, early=False):
-        count = self.COUNTS[phase]
-        if not self.direct(name, phase):
-            count = count // 3 * (1 if early else 2)
+        count = self.blocks(name, phase)
+        if self.direct(name, phase):
+            count *= len(self.steps(name, phase))
+        elif not early:
+            count *= 2
         slot = self.recv_slot(name, phase, early)
         expect(self.grads[name], count, slot, self.place).wait_recv()
 
@@ -363,12 +439,12 @@
                         jnp.bfloat16
                     )
 
-                each(2, body)
+                each(own.shape[0], body)
                 self.push(name, part, phase, step, step, half, slot)
 
     def add(self, name, part, phase, pick=()):
         total = self.slab(name, part, phase, 0)[(*pick, Ellipsis)].astype(jnp.float32)
-        for slot in range(3 if self.direct(name, phase) else 2):
+        for slot in range(len(self.steps(name, phase)) if self.direct(name, phase) else 2):
             piece = self.got[phase][name].at[self.landing(name, part, phase, slot)]
             total = total + piece[(*pick, Ellipsis)].astype(jnp.float32)
         return total
@@ -381,12 +457,14 @@
             def body(i):
                 own[i] = self.add(name, part, phase, (i,)).astype(jnp.bfloat16)
 
-            each(4, body)
+            each(own.shape[0], body)
             self.start(name, phase + 1, (part,))
 
     def finish(self):
         for name in WEIGHTS:
-            for phase, count in enumerate(self.COUNTS):
+            for phase in range(3):
+                times = len(self.steps(name, phase)) if self.direct(name, phase) else 3
+                count = self.blocks(name, phase) * times
                 slot = self.send_slot(name, phase)
                 expect(self.grads[name], count, slot, self.place).wait_send()
 
@@ -425,6 +503,47 @@
             self.expect(stage).wait_send()
 
 
+class Mate:
+    COTANGENT, NORMED, DOWN_PART, BACK_PART, GRAD = range(5)
+
+    def __init__(self, place, layer, send_sem, recv_sem):
+        self.place, self.layer = place, layer
+        self.send_sem, self.recv_sem = send_sem, recv_sem
+
+    def copy(self, which):
+        layer = self.layer
+        src, dst = (
+            (layer.both_cotangent.at[pl.ds(0, 128)], layer.both_cotangent.at[pl.ds(128, 128)]),
+            (layer.both_normed.at[pl.ds(0, 128)], layer.both_normed.at[pl.ds(128, 128)]),
+            (layer.down_part, layer.down_got),
+            (layer.back_part, layer.back_got),
+            (layer.gu_sum.at[1 - self.place.parity], layer.gu_got),
+        )[which]
+        return push(
+            src, dst, self.send_sem.at[which], self.recv_sem.at[which], self.place.mate
+        )
+
+    def start(self, which):
+        self.copy(which).start()
+
+    def start_columns(self, y):
+        at = pl.ds(256 * y, 256)
+        push(
+            self.layer.back_part.at[:, at],
+            self.layer.back_got.at[:, at],
+            self.send_sem.at[self.BACK_PART],
+            self.recv_sem.at[self.BACK_PART],
+            self.place.mate,
+        ).start()
+
+    def arrived(self, which):
+        self.copy(which).wait_recv()
+
+    def finish(self):
+        for which in range(5):
+            self.copy(which).wait_send()
+
+
 class End:
     def __init__(self, place, ends, got, outs, send_sem, recv_sem):
         self.place, self.ends, self.got, self.outs = place, ends, got, outs
@@ -433,6 +552,11 @@
     def rows(self, name, core):
         half = ROWS[name] // 2
         return pl.ds(pl.multiple_of(core * half, 8), half)
+
+    def columns(self, name, core):
+        if name == GU:
+            return pl.ds(pl.multiple_of(core * 2048, 512), 2048)
+        return half_columns(name, core)
 
     def copy(self, name):
         slot = name - 1
@@ -447,11 +571,11 @@
     def start(self, name):
         self.copy(name).start()
         core = self.place.core
-        self.outs[name][:, half_columns(name, core)] = self.ends[name][self.rows(name, core), :]
+        self.outs[name][:, self.columns(name, core)] = self.ends[name][self.rows(name, core), :]
 
     def take(self, name):
         self.copy(name).wait_recv()
-        self.outs[name][:, half_columns(name, 1 - self.place.core)] = self.got[name][...]
+        self.outs[name][:, self.columns(name, 1 - self.place.core)] = self.got[name][...]
 
     def finish(self):
         for name in WEIGHTS[1:]:
@@ -658,11 +782,14 @@
         gaps = self.cum[:, head : head + 1] - self.cum_rows[head : head + 1, :]
         return jnp.exp(jnp.where(self.causal(), gaps, masked_value))
 
-    def mix(self):
-        self.inner[...] = dot_back(self.active[:, 1664:1792].astype(LOW), self.active[:, 1536:1664].astype(LOW))
+    def mix(self, low, high):
+        if low == 0:
+            self.inner[...] = dot_back(
+                self.active[:, 1664:1792].astype(LOW), self.active[:, 1536:1664].astype(LOW)
+            )
         inner = self.inner[...]
-        square = jnp.zeros((TOK, 1), WIDE)
-        for i in range(12):
+        square = jnp.zeros((TOK, 1), WIDE) if low == 0 else self.inverse_state[...]
+        for i in range(low, high):
             mixing = jnp.concatenate(
                 [
                     inner * self.decay(head) * self.step_rows[head : head + 1, :]
@@ -678,7 +805,10 @@
             gate = self.proj[:, 768 + 128 * i : 896 + 128 * i]
             gated = central * (gate * sigmoid(gate))
             square = square + jnp.sum(gated * gated, axis=-1, keepdims=True)
-        inverse = lax.rsqrt(square * (1.0 / MIXER_FEATURES) + norm_eps)
+        self.inverse_state[...] = square
+
+    def mix_norm(self):
+        inverse = lax.rsqrt(self.inverse_state[...] * (1.0 / MIXER_FEATURES) + norm_eps)
         self.inverse_state[...] = inverse
         for i in range(12):
             at = slice(128 * i, 128 * i + 128)
@@ -702,45 +832,50 @@
         x = self.residual[...]
         self.inverse_ff[...] = lax.rsqrt(jnp.mean(x * x, axis=-1, keepdims=True) + norm_eps)
         normed = x * self.inverse_ff[...] * self.gains[1:2, :]
-        self.normed_ff[...] = normed.astype(LOW)
+        self.both_normed[0:128, :] = normed.astype(LOW)
         self.left_gu[:, 0:128] = jnp.transpose(normed).astype(LOW)
 
-    def feed(self, weights, first):
+    def turn_other(self):
+        other = self.both_normed[128:256, :].astype(WIDE)
+        self.left_gu[:, 128:256] = jnp.transpose(other).astype(LOW)
+
+    def feed(self):
         for i in range(2):
             for half in range(2):
-                weight = weights[half, :, :, :, :, tile(i, 512)].reshape(1024, 512)
-                low = 2048 * half + first + 512 * i
-                self.gate_up[:, low : low + 512] = dot(self.normed_ff[...], weight)
-        for i in range(first // 128, first // 128 + 8):
-            at = slice(128 * i, 128 * i + 128)
+                weight = self.g_gu[half, :, :, :, :, tile(i, 512)].reshape(1024, 512)
+                self.gate_up[:, tile(2 * half + i, 512)] = dot(self.both_normed[...], weight)
+        for i in range(8):
+            at = tile(i, 128)
             gate = self.gate_up[:, at]
-            hidden = gate * sigmoid(gate) * self.gate_up[:, 2048 + 128 * i : 2176 + 128 * i]
+            hidden = gate * sigmoid(gate) * self.gate_up[:, tile(8 + i, 128)]
             self.hidden[:, at] = hidden.astype(LOW)
-            self.left_down[at, 0:128] = jnp.transpose(hidden).astype(LOW)
+            self.left_down[at, 0:256] = jnp.transpose(hidden).astype(LOW)
 
     def down(self):
         for half in range(2):
-            at = slice(512 * half, 512 * half + 512)
-            self.layer_output[:, at] = (
-                self.residual[:, at] + dot(self.hidden[...], self.g_down[half].reshape(2048, 512))
-            ).astype(LOW)
-
-
-    def back_down(self, first):
-        for y in (first, first + 1):
+            at = tile(half, 512)
+            part = dot(self.hidden[...], self.g_down[half].reshape(1024, 512))
+            self.down_own[:, at] = self.residual[:, at] + part[0:128]
+            self.down_part[:, at] = part[128:256].astype(LOW)
+
+    def down_sum(self):
+        self.layer_output[...] = (self.down_own[...] + self.down_got[...].astype(WIDE)).astype(LOW)
+
+
+    def back_down(self):
+        for q in range(2):
             grad = dot_back(
-                self.cotangent[:, 0:512], self.g_down[0, y].reshape(512, 512)
-            ) + dot_back(self.cotangent[:, 512:1024], self.g_down[1, y].reshape(512, 512))
+                self.both_cotangent[:, 0:512], self.g_down[0, q].reshape(512, 512)
+            ) + dot_back(self.both_cotangent[:, 512:1024], self.g_down[1, q].reshape(512, 512))
             for i in range(4):
-                low = 512 * y + 128 * i
                 part = grad[:, 128 * i : 128 * i + 128]
-                gate = self.gate_up[:, low : low + 128]
-                up = self.gate_up[:, 2048 + low : 2176 + low]
+                at, up_at = tile(4 * q + i, 128), tile(8 + 4 * q + i, 128)
+                gate = self.gate_up[:, at]
                 share = sigmoid(gate)
-                self.d_gate[:, low : low + 128] = (
-                    part * up * (share * (1.0 + gate * (1.0 - share)))
+                self.d_gate[:, at] = (
+                    part * self.gate_up[:, up_at] * (share * (1.0 + gate * (1.0 - share)))
                 ).astype(LOW)
-                self.d_gate[:, 2048 + low : 2176 + low] = (part * (gate * share)).astype(LOW)
+                self.d_gate[:, up_at] = (part * (gate * share)).astype(LOW)
 
     def norm_back(self, grad, x, inverse, gain):
         turned = x * inverse
@@ -749,25 +884,21 @@
         d_x = inverse * (scaled - turned * jnp.mean(scaled * turned, axis=-1, keepdims=True))
         return d_x, d_gain
 
-    def back_feed(self, weights, first):
-        for y in range(4):
-            total = None if first == 0 else self.d_wide[:, tile(y, 256)]
-            for half in range(2):
-                low = 2048 * half + first
-                part = dot_back(
-                    self.d_gate[:, low : low + 1024], weights[half, y].reshape(256, 1024)
-                )
-                total = part if total is None else total + part
-            self.d_wide[:, tile(y, 256)] = total
+    def back_feed(self, y):
+        total = dot_back(self.d_gate[:, 0:1024], self.g_gu[0, y].reshape(256, 1024)) + dot_back(
+            self.d_gate[:, 1024:2048], self.g_gu[1, y].reshape(256, 1024)
+        )
+        self.d_wide[:, tile(y, 256)] = total[0:128]
+        self.back_part[:, tile(y, 256)] = total[128:256].astype(LOW)
 
     def back_residual(self):
+        grad = self.d_wide[:, 0:1024] + self.back_got[...].astype(WIDE)
         d_x, d_gain = self.norm_back(
-            self.d_wide[:, 0:1024], self.residual[...], self.inverse_ff[...], self.gains[1:2, :]
+            grad, self.residual[...], self.inverse_ff[...], self.gains[1:2, :]
         )
         self.vectors[1:2, 0:1024] = d_gain
         d_residual = self.cotangent[...].astype(WIDE) + d_x
-        self.proj[:, 0:768] = d_residual[:, 0:768]
-        self.gate_up[:, 3840:4096] = d_residual[:, 768:1024]
+        self.d_residual[...] = d_residual
         self.d_branch[...] = d_residual.astype(LOW)
 
     def back_branch(self):
@@ -810,14 +941,15 @@
                 d_central * self.active[:, at], axis=0, keepdims=True
             )
 
-    def back_mix(self):
+    def back_mix(self, low, high):
         inner = self.inner[...]
-        self.d_inner[...] = jnp.zeros((TOK, TOK), WIDE)
-        self.d_cum[...] = jnp.zeros((TOK, TOK), WIDE)
-        self.flow_rows[...] = jnp.zeros((TOK, TOK), WIDE)
-        self.d_step_rows[...] = jnp.zeros((TOK, TOK), WIDE)
         lane = lanes((TOK, TOK))
-        for i in range(12):
+        zero = jnp.zeros((TOK, TOK), WIDE)
+        d_inner, d_cum = (zero, zero) if low == 0 else (self.d_inner[...], self.d_cum[...])
+        if low == 0:
+            self.flow_rows[...] = zero
+            self.d_step_rows[...] = zero
+        for i in range(low, high):
             at = slice(128 * i, 128 * i + 128)
             stacked = pair_stack(self.d_state[:, at])
             d_mixing = dot_back(stacked, self.active[:, at].astype(LOW))
@@ -827,13 +959,18 @@
                 decay = self.decay(head)
                 step = self.step_rows[head : head + 1, :]
                 faded = grad * decay
-                self.d_inner[...] += faded * step
+                d_inner = d_inner + faded * step
                 part = faded * inner
                 d_step = jnp.sum(part, axis=0, keepdims=True)
                 self.d_step_rows[head : head + 1, :] = d_step
                 self.flow_rows[head : head + 1, :] = d_step * step
                 over = jnp.sum(part * step, axis=-1, keepdims=True)
-                self.d_cum[...] = jnp.where(lane == head, over, self.d_cum[...])
+                d_cum = jnp.where(lane == head, over, d_cum)
+        self.d_inner[...] = d_inner
+        self.d_cum[...] = d_cum
+
+    def back_steps(self):
+        lane = lanes((TOK, TOK))
         d_inner = self.d_inner[...].astype(LOW)
         self.d_active[:, 1664:1792] = dot(d_inner, self.active[:, 1536:1664].astype(LOW))
         self.d_active[:, 1536:1664] = dot_over_rows(d_inner, self.active[:, 1664:1792].astype(LOW))
@@ -897,23 +1034,18 @@
                     d_in = d_in + self.taps[3 - k : 4 - k, at] * later
             self.d_proj[:, 2304 + 128 * i : 2432 + 128 * i] = d_in.astype(LOW)
 
-    def back_project(self):
+    def back_project(self, low, high):
         small = self.g_small[...].reshape(1024, 128)
-        self.d_wide[:, 0:1024] = dot_back(self.right_dt[0:128, :], small)
-
-        def body(y):
-            total = self.d_wide[:, tile(y, 256)]
+        for y in range(low, high):
+            total = dot_back(self.right_dt[0:128, :], small[256 * y : 256 * y + 256])
             for half in range(2):
-                low = 1024 * half
-                total = total + dot_back(
-                    self.d_proj[:, low : low + 1024], self.g_ina[half, y].reshape(256, 1024)
-                )
-                total = total + dot_back(
-                    self.d_proj[:, 2048 + low : 3072 + low], self.g_inb[half, y].reshape(256, 1024)
-                )
+                at = tile(half, 1024)
+                total = total + dot_back(self.d_proj[:, at], self.g_ina[half, y].reshape(256, 1024))
+                at = tile(2 + half, 1024)
+                total = total + dot_back(self.d_proj[:, at], self.g_inb[half, y].reshape(256, 1024))
             self.d_wide[:, tile(y, 256)] = total
 
-        each(4, body)
+    def back_input(self):
         d_x, d_gain = self.norm_back(
             self.d_wide[:, 0:1024],
             self.tokens[...].astype(WIDE),
@@ -921,8 +1053,7 @@
             self.gains[0:1, :],
         )
         self.vectors[0:1, 0:1024] = d_gain
-        d_residual = jnp.concatenate([self.proj[:, 0:768], self.gate_up[:, 3840:4096]], axis=1)
-        self.input_grad[...] = (d_residual + d_x).astype(LOW)
+        self.input_grad[...] = (self.d_residual[...] + d_x).astype(LOW)
 
 
     def grad_wide(self, left, right, into):
@@ -934,7 +1065,7 @@
                 into[y, :, :, :, tile(n, size)] = block.astype(LOW).reshape(4, 4, 16, size)
 
     def grad_tall(self, left, right, into):
-        for y in range(4):
+        for y in range(into.shape[0]):
             block = dot(left[tile(y, 512), :], right[...])
             into[y] = block.astype(LOW).reshape(4, 4, 32, 512)
 
@@ -944,34 +1075,35 @@
         self.place, self.layer = place, layer
         self.send_sem, self.recv_sem = send_sem, recv_sem
         self.lefts = (
-            None, layer.left_in, None, layer.left_out, layer.left_gu, None, layer.left_down,
+            None, layer.left_in, None, layer.left_out, layer.left_gu, layer.left_down,
         )
         self.rights = (
-            layer.right_dt, layer.right_ina, layer.right_inb, layer.right_out, layer.right_gua,
-            layer.right_gub, layer.right_down,
+            layer.right_dt, layer.right_ina, layer.right_inb, layer.right_out, layer.right_gu,
+            layer.right_down,
         )
         self.sources = (
-            None, layer.d_proj, layer.d_proj, layer.d_branch, layer.d_gate, layer.d_gate,
-            layer.cotangent,
+            None, layer.d_proj, layer.d_proj, layer.d_branch, layer.d_gate, layer.both_cotangent,
         )
 
     def left_copy(self, name):
         ref = self.lefts[name]
-        src, dst = ref.at[:, pl.ds(0, 128)], ref.at[:, pl.ds(128, 128)]
+        size = ref.shape[1] // 2
+        src, dst = ref.at[:, pl.ds(0, size)], ref.at[:, pl.ds(size, size)]
         return push(
             src, dst, self.send_sem.at[name], self.recv_sem.at[name], self.place.sibling
         )
 
     def right_copy(self, name):
         ref, source = self.rights[name], self.sources[name]
+        size = ref.shape[0] // 2
         if source is None:
-            src = ref.at[pl.ds(0, 128), :]
+            src = ref.at[pl.ds(0, size), :]
         else:
             src = source.at[:, half_columns(name, 1 - self.place.core)]
-        slot = 7 + name
+        slot = 6 + name
         return push(
             src,
-            ref.at[pl.ds(128, 128), :],
+            ref.at[pl.ds(size, size), :],
             self.send_sem.at[slot],
             self.recv_sem.at[slot],
             self.place.sibling,
@@ -983,7 +1115,8 @@
     def start_right(self, name):
         ref, source = self.rights[name], self.sources[name]
         if source is not None:
-            ref[0:128, :] = source[:, half_columns(name, self.place.core)]
+            size = ref.shape[0] // 2
+            ref[0:size, :] = source[:, half_columns(name, self.place.core)]
         self.right_copy(name).start()
 
     def arrived(self, name):
@@ -993,8 +1126,7 @@
 
     def finish(self):
         for name in WEIGHTS:
-            if name not in (GUA, GUB):
-                self.right_copy(name).wait_send()
+            self.right_copy(name).wait_send()
             if self.lefts[name] is not None:
                 self.left_copy(name).wait_send()
 
@@ -1017,11 +1149,11 @@
     g_ina=((2, 4, 4, 4, 16, 1024), LOW),
     g_inb=((2, 4, 4, 4, 16, 1024), LOW),
     g_out=((2, 4, 4, 4, 32, 512), LOW),
-    g_gua=((2, 4, 4, 4, 16, 1024), LOW),
-    g_gub=((2, 4, 4, 4, 16, 1024), LOW),
-    g_down=((2, 4, 4, 4, 32, 512), LOW),
-    grad_small=((4, 4, 4, 16, 128), LOW),
-    grad_down_low=((4, 4, 4, 32, 512), LOW),
+    g_gu=((2, 4, 4, 4, 16, 1024), LOW),
+    g_down=((2, 2, 4, 4, 32, 512), LOW),
+    low_small=((4, 4, 4, 16, 128), LOW),
+    low_gu=((4, 4, 4, 16, 1024), LOW),
+    low_down=((2, 4, 4, 32, 512), LOW),
     small_shard=((8, 128), WIDE),
     heads=((8, 128), WIDE),
     skip=((8, 1536), WIDE),
@@ -1029,6 +1161,7 @@
     sines=((TOK, 128), WIDE),
     pack=((16, 4224), LOW),
     got=((16, 4224), LOW),
+    stage=((16, 1024), LOW),
     small_wide=((1024, 128), WIDE),
     gains=((8, 1024), WIDE),
     taps=((8, 1792), WIDE),
@@ -1051,11 +1184,23 @@
     central=((TOK, 1536), WIDE),
     inverse_state=((TOK, 1), WIDE),
     residual=((TOK, 1024), WIDE),
+    d_residual=((TOK, 1024), WIDE),
     inverse_ff=((TOK, 1), WIDE),
-    gate_up=((TOK, 4096), WIDE),
-    d_gate=((TOK, 4096), LOW),
+    both_normed=((256, 1024), LOW),
+    both_cotangent=((256, 1024), LOW),
+    gate_up=((256, 2048), WIDE),
+    hidden=((256, 1024), LOW),
+    down_own=((TOK, 1024), WIDE),
+    down_part=((TOK, 1024), LOW),
+    down_got=((TOK, 1024), LOW),
+    back_part=((TOK, 1024), LOW),
+    back_got=((TOK, 1024), LOW),
+    gu_sum=((2, 16, 1024), WIDE),
+    gu_got=((16, 1024), WIDE),
+    d_gate=((256, 2048), LOW),
     d_branch=((TOK, 1024), LOW),
     d_state=((TOK, 1536), LOW),
+    d_proj=((TOK, 4096), LOW),
     skip_sum=((8, 1536), WIDE),
     d_inner=((TOK, TOK), WIDE),
     d_cum=((TOK, TOK), WIDE),
@@ -1064,20 +1209,23 @@
     vectors=((8, 1792), WIDE),
     left_in=((1024, 256), LOW),
     left_out=((2048, 256), LOW),
-    left_gu=((1024, 256), LOW),
-    left_down=((2048, 256), LOW),
+    left_gu=((1024, 512), LOW),
+    left_down=((1024, 512), LOW),
     right_ina=((256, 1024), LOW),
     right_inb=((256, 1024), LOW),
     right_out=((256, 512), LOW),
-    right_gua=((256, 1024), LOW),
-    right_gub=((256, 1024), LOW),
-    right_down=((256, 512), LOW),
+    right_gu=((512, 1024), LOW),
+    right_down=((512, 512), LOW),
     right_dt=((256, 128), LOW),
     sums=((4, 4, 8, 1792), WIDE),
 )
-LANDINGS = ((3, 4, 4), (3, 4), (3,))
+BLOCKS = tuple((ROWS[name], COLS[name]) for name in WEIGHTS)
+LANDINGS = tuple((3, DEPTH[name], 4) for name in WEIGHTS)
+LANDINGS += tuple((3, DEPTH[name]) for name in WEIGHTS)
+LANDINGS += tuple({GU: (1, 2), DOWN: (1,)}.get(name, (3,)) for name in WEIGHTS)
+ENDS = tuple((ROWS[name], 2048 if name == GU else COLS[name]) for name in WEIGHTS[1:])
 SEMS = dict(
-    enter=3, gather=63, scatter=35, sums=4, end=6, swap=14,
+    enter=4, gather=53, scatter=30, sums=4, end=5, swap=12, mate=5,
 )
 
 
@@ -1086,43 +1234,35 @@
         names = [*INS, *OUTS, *SCRATCH]
         layer = Layer(dict(zip(names, refs)))
         rest = list(refs[len(names) :])
-        landings = [[rest.pop(0) for _ in WEIGHTS] for _ in LANDINGS]
+        landings = [[rest.pop(0) for _ in WEIGHTS] for _ in range(3)]
         ends = [None] + [rest.pop(0) for _ in WEIGHTS[1:]]
         ends_got = [None] + [rest.pop(0) for _ in WEIGHTS[1:]]
         sems = {name: (rest.pop(0), rest.pop(0)) for name in SEMS}
-        layer.normed_ff, layer.hidden = layer.normed, layer.mixed
-        layer.d_proj = layer.d_gate
-        layer.d_wide = layer.gate_up.at[:, pl.ds(0, 2048)]
-        layer.d_active = layer.gate_up.at[:, pl.ds(2048, 1792)]
+        layer.d_wide = layer.gate_up.at[pl.ds(0, 128), :]
+        layer.d_active = layer.gate_up.at[pl.ds(128, 128), pl.ds(0, 1792)]
         place = Place()
-        arrays = (
-            layer.g_small, layer.g_ina, layer.g_inb, layer.g_out, layer.g_gua, layer.g_gub,
-            layer.g_down,
-        )
+        arrays = (layer.g_small, layer.g_ina, layer.g_inb, layer.g_out, layer.g_gu, layer.g_down)
         shards = (
             layer.small_shard, layer.in_shard, layer.in_shard, layer.out_shard, layer.gu_shard,
-            layer.gu_shard, layer.down_shard,
+            layer.down_shard,
         )
         grads = (
-            layer.grad_small,
-            layer.g_gua.at[1],
-            layer.g_gub.at[1],
-            layer.g_out.at[0],
-            layer.g_gua.at[0],
-            layer.g_gub.at[0],
-            layer.grad_down_low,
+            layer.low_small, layer.g_gu.at[0], layer.g_gu.at[1], layer.g_out.at[0], layer.low_gu,
+            layer.low_down,
         )
         outs = (
-            None, layer.grad_in, layer.grad_in, layer.grad_out, layer.grad_gu, layer.grad_gu,
-            layer.grad_down,
+            None, layer.grad_in, layer.grad_in, layer.grad_out, layer.grad_gu, layer.grad_down,
         )
         self.place, self.layer, self.grads = place, layer, grads
         self.gather = Gather(place, arrays, *sems["gather"])
-        self.enter = Enter(place, self.gather, layer.pack, layer.got, shards, sems["enter"])
+        self.enter = Enter(
+            place, self.gather, layer.pack, layer.got, layer.stage, shards, sems["enter"]
+        )
         self.scatter = Scatter(place, grads, *landings, *sems["scatter"])
         self.sum_all = SumAll(place, layer.sums, *sems["sums"])
         self.end = End(place, ends, ends_got, outs, *sems["end"])
         self.swap = Swap(place, layer, *sems["swap"])
+        self.mate = Mate(place, layer, *sems["mate"])
 
     def last(self, name):
         self.scatter.arrived(name, 2)
@@ -1131,10 +1271,23 @@
             if name == SMALL:
                 mine = jnp.where(self.place.core == 0, value[0:8], value[8:16])
                 self.layer.grad_in[:, 4096:4120] = mine[:, 0:24]
+            elif name == GU:
+                self.layer.gu_sum[:, :, low:high] = value
             else:
                 self.end.ends[name][:, low:high] = value
-        if name != SMALL:
+        if name == GU:
+            self.mate.start(Mate.GRAD)
+        elif name != SMALL:
             self.end.start(name)
+
+    def last_gu(self):
+        self.mate.arrived(Mate.GRAD)
+        layer, parity, into = self.layer, self.place.parity, self.end.ends[GU]
+        for which, value in ((parity, layer.gu_sum[parity]), (1 - parity, layer.gu_got[...])):
+            for q in range(2):
+                at = pl.ds(pl.multiple_of(1024 * q + 512 * which, 512), 512)
+                into[:, at] = value[:, 512 * q : 512 * q + 512]
+        self.end.start(GU)
 
 
 def layer_kernel(*refs):
@@ -1143,9 +1296,10 @@
     enter, scatter, sum_all, end, swap = (
         plan.enter, plan.scatter, plan.sum_all, plan.end, plan.swap,
     )
+    mate = plan.mate
 
     def onward(name, phase):
-        gather.arrived(name, phase, 0 if phase < DIRECT.get(name, 1) else 2)
+        gather.arrived(name, phase, 0 if gather.direct(name, phase) else 2)
         if phase == 0 or name == SMALL:
             gather.start(name, phase + 1)
         else:
@@ -1162,63 +1316,56 @@
     arrive(place)
     layer.enter()
     enter.run(lambda: meet(place))
-    gather.start(SMALL, 0)
     gather.start(INA, 0)
     gather.start(INB, 0)
+    gather.start(DOWN, 0)
     gather.start(OUT, 0)
-    gather.start(GUA, 0)
-    gather.start(DOWN, 0)
-    gather.start(GUB, 0)
-    swap.start_right(DOWN)
+    gather.start(SMALL, 0)
     layer.tables()
-    onward(SMALL, 0)
+    enter.mate_copy().wait_recv()
+    gather.start(GU, 0)
     onward(INA, 0)
     onward(INB, 0)
+    onward(SMALL, 0)
+    onward(DOWN, 0)
     onward(OUT, 0)
-    onward(GUA, 0)
-    onward(DOWN, 0)
-    onward(GUB, 0)
-    onward(SMALL, 1)
-    gather.hand_on(INB, 1, (0,))
-    gather.hand_on(INB, 1, (1,))
+    onward(GU, 0)
     onward(INA, 1)
     onward_late(INA)
-    gather.hand_on(OUT, 1, (0,))
-    gather.hand_on(OUT, 1, (1,))
-    gather.hand_on(GUA, 1, (0,))
-    gather.hand_on(GUA, 1, (1,))
     gather.hand_on(DOWN, 1, (0,))
+    onward(SMALL, 1)
     gather.hand_on(DOWN, 1, (1,))
-    gather.hand_on(GUB, 1, (0,))
-    gather.hand_on(GUB, 1, (1,))
     onward(INB, 1)
+    onward_late(INB)
+    onward(OUT, 1)
+    gather.hand_on(GU, 1, (0,))
+    gather.hand_on(GU, 1, (1,))
+    gather.hand_on(INA, 2, (0,))
+    gather.hand_on(INA, 2, (1,))
+    gather.arrived_late(INA, (0,))
+    gather.arrived_late(INA, (1,))
+    onward(DOWN, 1)
     gather.arrived(SMALL, 2)
     layer.spread()
     layer.norm_in()
     swap.start_left(INA)
-    gather.hand_on(INA, 2, (0,))
-    gather.hand_on(INA, 2, (1,))
-    onward_late(INB)
-    gather.arrived_late(INA, (0,))
-    gather.arrived_late(INA, (1,))
-    onward(OUT, 1)
-    onward(GUA, 1)
     gather.hand_on(INB, 2, (0,))
     gather.hand_on(INB, 2, (1,))
     onward_late(OUT)
+    gather.arrived_late(INB, (0,))
+    gather.arrived_late(INB, (1,))
+    gather.hand_on(OUT, 2, (0,))
+    gather.hand_on(OUT, 2, (1,))
+    layer.both_cotangent[0:128, :] = layer.cotangent[...]
+    mate.start(Mate.COTANGENT)
+    onward(GU, 1)
+    onward_late(GU)
     landed(INA)
+    gather.hand_on(DOWN, 2, (0,))
+    gather.hand_on(DOWN, 2, (1,))
     gather.passed(INA)
     layer.project_first()
-    gather.arrived_late(INB, (0,))
-    gather.arrived_late(INB, (1,))
-    onward(DOWN, 1)
     layer.attend()
-    gather.hand_on(OUT, 2, (0,))
-    gather.hand_on(OUT, 2, (1,))
-    onward_late(GUA)
-    gather.hand_on(GUA, 2, (0,))
-    gather.hand_on(GUA, 2, (1,))
-    onward_late(DOWN)
     landed(INB)
     gather.arrived_late(OUT, (0,))
     gather.arrived_late(OUT, (1,))
@@ -1226,127 +1373,122 @@
     layer.project_last()
     layer.activate()
     layer.steps()
-    gather.hand_on(DOWN, 2, (0,))
-    gather.hand_on(DOWN, 2, (1,))
-    layer.mix()
     landed(OUT)
-    onward(GUB, 1)
-    onward_late(GUB)
-    gather.arrived_late(GUA, (0,))
-    gather.arrived_late(GUA, (1,))
+    layer.mix(0, 6)
+    layer.mix(6, 12)
+    layer.mix_norm()
     gather.passed(OUT)
     layer.branch()
-    swap.start_left(GUA)
+    mate.start(Mate.NORMED)
     layer.turn_left(layer.mixed, layer.left_out, 16)
     swap.start_left(OUT)
-    landed(GUA)
+    gather.hand_on(GU, 2, (1,))
+    gather.hand_on(GU, 2, (0,))
+    onward_late(DOWN)
+    gather.arrived_late(GU, (0,))
+    gather.arrived_late(GU, (1,))
+    mate.arrived(Mate.COTANGENT)
+    swap.start_right(DOWN)
+    landed(GU)
     gather.arrived_late(DOWN, (0,))
     gather.arrived_late(DOWN, (1,))
     landed(DOWN)
-    gather.passed(GUA)
-    layer.feed(layer.g_gua, 0)
-    gather.hand_on(GUB, 2, (0,))
-    gather.hand_on(GUB, 2, (1,))
+    mate.arrived(Mate.NORMED)
+    layer.turn_other()
+    swap.start_left(GU)
+    gather.passed(GU)
+    layer.feed()
+    swap.start_left(DOWN)
     gather.passed(DOWN)
-    layer.back_down(0)
-    swap.start_right(GUA)
-    gather.arrived_late(GUB, (0,))
-    gather.arrived_late(GUB, (1,))
-    layer.back_feed(layer.g_gua, 0)
-    gather.finish(GUA)
-    swap.arrived(GUA)
-    layer.grad_wide(layer.left_gu, layer.right_gua, grads[GUA])
-    scatter.start(GUA, 0)
-    landed(GUB)
-    gather.passed(GUB)
-    layer.feed(layer.g_gub, 1024)
-    swap.start_left(DOWN)
-    layer.back_down(2)
-    swap.start_right(GUB)
-    layer.back_feed(layer.g_gub, 1024)
-    layer.back_residual()
-    swap.start_right(OUT)
-    scatter.hand_on(GUA, 0)
+    layer.back_down()
+    swap.start_right(GU)
+    for y in range(4):
+        layer.back_feed(y)
+        mate.start_columns(y)
     swap.arrived(DOWN)
     layer.grad_tall(layer.left_down, layer.right_down, grads[DOWN])
     scatter.start(DOWN, 0)
-    gather.finish(GUB)
-    swap.arrived(GUB)
-    layer.grad_wide(layer.left_gu, layer.right_gub, grads[GUB])
-    scatter.start(GUB, 0)
+    swap.arrived(GU)
+    layer.grad_wide(layer.left_gu, layer.right_gu, grads[GU])
+    scatter.start(GU, 0)
+    layer.down()
+    mate.start(Mate.DOWN_PART)
+    scatter.hand_on(DOWN, 0)
+    mate.arrived(Mate.BACK_PART)
+    layer.back_residual()
+    swap.start_right(OUT)
     layer.back_branch()
-    swap.right_copy(GUA).wait_send()
-    swap.right_copy(GUB).wait_send()
-    layer.back_gated()
-    layer.back_attend()
-    swap.start_right(INA)
-    scatter.relay(GUA, 0)
-    scatter.hand_on(DOWN, 0)
-    layer.back_mix()
-    swap.start_right(SMALL)
     gather.finish(OUT)
     swap.arrived(OUT)
     layer.grad_tall(layer.left_out, layer.right_out, grads[OUT])
     scatter.start(OUT, 0)
-    scatter.hand_on(GUB, 0)
+    scatter.hand_on(GU, 0)
+    layer.back_gated()
+    layer.back_attend()
+    swap.start_right(INA)
+    layer.back_mix(0, 6)
+    layer.back_mix(6, 12)
+    gather.finish(GU)
     swap.arrived(INA)
     layer.grad_wide(layer.left_in, layer.right_ina, grads[INA])
     scatter.start(INA, 0)
+    scatter.relay(DOWN, 0)
+    layer.back_steps()
+    swap.start_right(SMALL)
+    scatter.hand_on(OUT, 0)
     layer.back_activate()
     swap.start_right(INB)
-    scatter.hand_on(GUA, 1)
     swap.arrived(SMALL)
     layer.grad_wide(layer.left_in, layer.right_dt, grads[SMALL])
     scatter.start(SMALL, 0)
-    layer.down()
+    mate.arrived(Mate.DOWN_PART)
+    layer.down_sum()
+    scatter.relay(GU, 0)
     swap.arrived(INB)
     layer.grad_wide(layer.left_in, layer.right_inb, grads[INB])
     scatter.start(INB, 0)
-    layer.back_project()
+    scatter.hand_on(INA, 0)
+    layer.back_project(0, 2)
+    scatter.hand_on(DOWN, 1)
+    layer.back_project(2, 4)
+    layer.back_input()
     sum_all.start(0, layer.vectors[...])
-    scatter.relay(DOWN, 0)
-    scatter.hand_on(OUT, 0)
     sum_all.start(1, sum_all.total(0))
-    scatter.relay(GUB, 0)
-    scatter.hand_on(INA, 0)
-    scatter.relay(GUA, 1)
+    scatter.relay(OUT, 0)
+    scatter.hand_on(GU, 1)
     scatter.relay(SMALL, 0)
     scatter.hand_on(INB, 0)
-    scatter.hand_on(DOWN, 1)
-    scatter.relay(OUT, 0)
-    scatter.hand_on(GUB, 1)
+    scatter.relay(INA, 0)
+    scatter.relay(DOWN, 1)
     sum_all.start(2, sum_all.total(1))
-    scatter.relay(INA, 0)
-    plan.last(GUA)
+    scatter.relay(GU, 1)
+    scatter.relay(OUT, 1)
     scatter.relay(SMALL, 1)
-    end.take(GUA)
     scatter.relay(INB, 0)
-    scatter.relay(DOWN, 1)
-    scatter.hand_on(OUT, 1)
-    scatter.relay(GUB, 1)
     scatter.hand_on(INA, 1)
+    plan.last(DOWN)
+    end.take(DOWN)
     sum_all.start(3, sum_all.total(2))
+    plan.last(GU)
+    plan.last(OUT)
     plan.last(SMALL)
-    scatter.relay(OUT, 1)
+    end.take(OUT)
+    scatter.relay(INA, 1)
     scatter.relay(INB, 1)
-    scatter.relay(INA, 1)
-    plan.last(DOWN)
-    plan.last(GUB)
-    end.take(DOWN)
-    end.take(GUB)
+    plan.last_gu()
+    end.take(GU)
     layer.total[...] = sum_all.total(3)
-    plan.last(OUT)
+    plan.last(INA)
     plan.last(INB)
-    plan.last(INA)
-    end.take(OUT)
+    end.take(INA)
     end.take(INB)
-    end.take(INA)
     for name in (SMALL, INA, INB, DOWN):
         gather.finish(name)
     scatter.finish()
     sum_all.finish()
     end.finish()
     swap.finish()
+    mate.finish()
     enter.finish()
 
 
@@ -1382,11 +1524,10 @@
         tokens, cotangent, input_weight, output_weight, gate_up_weight, down_weight, norm_gains,
         conv_params, mixer_scale, decay_log[None], step_bias[None], mixer_skip_factor[None],
     )
-    blocks = [(ROWS[name], COLS[name]) for name in WEIGHTS]
     scratch = [pltpu.VMEM(*one) for one in SCRATCH.values()]
-    scratch += [pltpu.VMEM(lead + block, LOW) for lead in LANDINGS for block in blocks]
-    scratch += [pltpu.VMEM(block, WIDE) for block in blocks[1:]]
-    scratch += [pltpu.VMEM((block[0] // 2, block[1]), WIDE) for block in blocks[1:]]
+    scratch += [pltpu.VMEM(lead + block, LOW) for lead, block in zip(LANDINGS, BLOCKS * 3)]
+    scratch += [pltpu.VMEM(block, WIDE) for block in ENDS]
+    scratch += [pltpu.VMEM((block[0] // 2, block[1]), WIDE) for block in ENDS]
     scratch += [pltpu.SemaphoreType.DMA((count,)) for count in SEMS.values() for _ in range(2)]
     whole = pl.BlockSpec(memory_space=pltpu.VMEM)
     results = pl.pallas_call(

time: 127 us -> 116 us (0.913)
  Pallas kernels: 126 us -> 115 us
    pallas_call x1, Pallas kernels: 123 us -> 113 us  [local(): pl.pallas_call(layer_kernel, out_shape=[jax.ShapeDtypeStruct(*one) for on...]
where the time goes in v3:
time: 116 us
  Pallas kernels  115 us (99%)
    pallas_call x1, Pallas kernels, local(): pl.pallas_call(layer_kernel, out_shape=[jax.ShapeDtypeStruct(*one) for on...  113 us

profile of v3, /device:TPU:1, one launch (start us, length us, event | category | flops | bytes accessed | tf_op | source)
XLA Modules:
  0.0 115.8 jit_solution(2111675581523898974)
XLA Ops:
  0.6 112.8 %layer.1 = (bf16[128,1024]{1,0:T(8,128)(2,1)}, bf16[128,1024]{1,0:T(8,128)(2,1)}, f32[8,4120]{1,0:T(8,128)}, f32[16,1024]{1,0:T(8,128)}, f32[8,4096]{1,0:T(8,128...) custom-call(bf16[128,1024]{1,0:T(8,128)(2,1)} %refs_0_.1, bf16[128,1024]{1,0:T(8,128)(2,1)} %refs_1_.1, ...), custom_call_target="tpu_custom_call" | custom-call | tf_op jit(solution)/shard_map/layer/pallas_call | solution.py:1533
  113.4 2.2 %finish.1 = (bf16[128,1024]{1,0:T(8,128)(2,1)}, bf16[128,1024]{1,0:T(8,128)(2,1)}, f32[8,4120]{1,0:T(8,128)}, f32[16,1024]{1,0:T(8,128)}, f32[8,4096]{1,0:T(8,12...) custom-call(bf16[128,1024]{1,0:T(8,128)(2,1)} %get-tuple-element.31., ...), custom_call_target="tpu_custom_call" | custom-call | tf_op jit(solution)/shard_map/finish/pallas_call | solution.py:1545

commit v4 on v3

--- a/solution.py
+++ b/solution.py
@@ -32,14 +32,14 @@
 PAIR_ORDERS = ((Y, X, Z), (Y, Z, X))
 PARTS = (
     ((0, 128),),
-    ((0, 256), (256, 512), (512, 1024)),
+    ((0, 256), (256, 640), (640, 1024)),
     ((0, 384), (384, 768), (768, 1024)),
     ((0, 128), (128, 256), (256, 512)),
     ((0, 512), (512, 1024)),
     ((0, 256), (256, 512)),
 )
-DIRECT = {SMALL: 3, INA: 2, INB: 2, OUT: 2}
-BACK_DIRECT = {SMALL: 0, INB: 1, OUT: 1}
+DIRECT = {SMALL: 3, INA: 2}
+BACK_DIRECT = {SMALL: 0, INB: 1}
 
 
 def order_of(name, part):
@@ -305,7 +305,7 @@
             self.place.mate,
         )
 
-    def run(self, greet):
+    def run(self, greet, begin):
         core, at = self.place.core, self.place.at
         wide = jnp.float32
         for name, low, size in self.COLUMNS[:3]:
@@ -322,9 +322,6 @@
         copies = self.copies()
         for copy in copies:
             copy.start()
-        for name in (OUT, DOWN):
-            rows = pl.ds(pl.multiple_of(core * 16, 16), 16)
-            self.own(name, core)[rows, :] = self.shards[name][:, half_columns(name, core)]
         copies[0].wait_recv()
         for name, low, size in self.COLUMNS:
             mine = self.pack[:, low : low + size].astype(wide)
@@ -345,6 +342,10 @@
                 self.mate_copy().start()
             else:
                 self.own(name, core)[...] = block.astype(jnp.bfloat16)
+                begin(name)
+        for name in (OUT, DOWN):
+            rows = pl.ds(pl.multiple_of(core * 16, 16), 16)
+            self.own(name, core)[rows, :] = self.shards[name][:, half_columns(name, core)]
         for copy in copies[1:]:
             copy.wait_recv()
 
@@ -711,15 +712,13 @@
         self.normed[...] = normed.astype(LOW)
         self.left_in[:, 0:128] = jnp.transpose(normed).astype(LOW)
 
-    def project_first(self):
-        for i in range(4):
-            weight = self.g_ina[i // 2, :, :, :, :, tile(i % 2, 512)]
-            self.proj[:, tile(i, 512)] = dot(self.normed[...], weight.reshape(1024, 512))
-
-    def project_last(self):
-        for i in range(4):
-            weight = self.g_inb[i // 2, :, :, :, :, tile(i % 2, 512)]
-            self.proj[:, tile(4 + i, 512)] = dot(self.normed[...], weight.reshape(1024, 512))
+    def project(self, weights, first, half):
+        for i in range(2):
+            weight = weights[half, :, :, :, :, tile(i, 512)].reshape(1024, 512)
+            at = pl.ds(pl.multiple_of(first + half * 1024 + 512 * i, 512), 512)
+            self.proj[:, at] = dot(self.normed[...], weight)
+
+    def project_steps(self):
         raw = dot(self.normed[...], self.g_small[...].reshape(1024, 128))
         self.step_raw[...] = jnp.where(lanes((TOK, 128)) < MIXER_HEADS, raw, 0.0)
 
@@ -823,12 +822,13 @@
             block = source[:, 128 * i : 128 * i + 128].astype(WIDE)
             into[128 * i : 128 * i + 128, 0:128] = jnp.transpose(block).astype(LOW)
 
+    def branch_half(self, half):
+        at = pl.ds(pl.multiple_of(512 * half, 512), 512)
+        self.residual[:, at] = self.tokens[:, at].astype(WIDE) + dot(
+            self.mixed[...], self.g_out[half].reshape(2048, 512)
+        )
+
     def branch(self):
-        for half in range(2):
-            at = slice(512 * half, 512 * half + 512)
-            self.residual[:, at] = self.tokens[:, at].astype(WIDE) + dot(
-                self.mixed[...], self.g_out[half].reshape(2048, 512)
-            )
         x = self.residual[...]
         self.inverse_ff[...] = lax.rsqrt(jnp.mean(x * x, axis=-1, keepdims=True) + norm_eps)
         normed = x * self.inverse_ff[...] * self.gains[1:2, :]
@@ -839,17 +839,21 @@
         other = self.both_normed[128:256, :].astype(WIDE)
         self.left_gu[:, 128:256] = jnp.transpose(other).astype(LOW)
 
-    def feed(self):
+    def feed_half(self, half):
         for i in range(2):
-            for half in range(2):
-                weight = self.g_gu[half, :, :, :, :, tile(i, 512)].reshape(1024, 512)
-                self.gate_up[:, tile(2 * half + i, 512)] = dot(self.both_normed[...], weight)
+            weight = self.g_gu[half, :, :, :, :, tile(i, 512)].reshape(1024, 512)
+            at = pl.ds(pl.multiple_of(half * 1024 + 512 * i, 512), 512)
+            self.gate_up[:, at] = dot(self.both_normed[...], weight)
+
+    def feed(self, send):
         for i in range(8):
             at = tile(i, 128)
             gate = self.gate_up[:, at]
             hidden = gate * sigmoid(gate) * self.gate_up[:, tile(8 + i, 128)]
             self.hidden[:, at] = hidden.astype(LOW)
             self.left_down[at, 0:256] = jnp.transpose(hidden).astype(LOW)
+            if i % 4 == 3:
+                send(i // 4)
 
     def down(self):
         for half in range(2):
@@ -1111,6 +1115,16 @@
 
     def start_left(self, name):
         self.left_copy(name).start()
+
+    def start_left_rows(self, q):
+        ref, rows = self.lefts[DOWN], tile(q, 512)
+        push(
+            ref.at[rows, pl.ds(0, 256)],
+            ref.at[rows, pl.ds(256, 256)],
+            self.send_sem.at[DOWN],
+            self.recv_sem.at[DOWN],
+            self.place.sibling,
+        ).start()
 
     def start_right(self, name):
         ref, source = self.rights[name], self.sources[name]
@@ -1225,7 +1239,7 @@
 LANDINGS += tuple({GU: (1, 2), DOWN: (1,)}.get(name, (3,)) for name in WEIGHTS)
 ENDS = tuple((ROWS[name], 2048 if name == GU else COLS[name]) for name in WEIGHTS[1:])
 SEMS = dict(
-    enter=4, gather=53, scatter=30, sums=4, end=5, swap=12, mate=5,
+    enter=(4, 4), gather=(24, 53), scatter=(18, 30), sums=(4, 4), end=(5, 5), swap=(12, 12), mate=(5, 5),
 )
 
 
@@ -1296,7 +1310,7 @@
     enter, scatter, sum_all, end, swap = (
         plan.enter, plan.scatter, plan.sum_all, plan.end, plan.swap,
     )
-    mate = plan.mate
+    mate, core = plan.mate, place.core
 
     def onward(name, phase):
         gather.arrived(name, phase, 0 if gather.direct(name, phase) else 2)
@@ -1315,80 +1329,87 @@
 
     arrive(place)
     layer.enter()
-    enter.run(lambda: meet(place))
-    gather.start(INA, 0)
-    gather.start(INB, 0)
+    enter.run(lambda: meet(place), lambda name: gather.start(name, 0))
+    gather.start(SMALL, 0)
+    gather.start(OUT, 0)
     gather.start(DOWN, 0)
-    gather.start(OUT, 0)
-    gather.start(SMALL, 0)
     layer.tables()
     enter.mate_copy().wait_recv()
     gather.start(GU, 0)
+    onward(SMALL, 0)
+    onward(INB, 0)
+    onward(OUT, 0)
     onward(INA, 0)
-    onward(INB, 0)
-    onward(SMALL, 0)
     onward(DOWN, 0)
-    onward(OUT, 0)
     onward(GU, 0)
+    onward(SMALL, 1)
+    gather.hand_on(INB, 1, (0,))
+    gather.hand_on(INB, 1, (1,))
+    gather.hand_on(OUT, 1, (0,))
+    gather.hand_on(OUT, 1, (1,))
+    gather.hand_on(DOWN, 1, (0,))
+    gather.hand_on(DOWN, 1, (1,))
     onward(INA, 1)
     onward_late(INA)
-    gather.hand_on(DOWN, 1, (0,))
-    onward(SMALL, 1)
-    gather.hand_on(DOWN, 1, (1,))
+    gather.hand_on(GU, 1, (0,))
+    gather.hand_on(GU, 1, (1,))
     onward(INB, 1)
     onward_late(INB)
-    onward(OUT, 1)
-    gather.hand_on(GU, 1, (0,))
-    gather.hand_on(GU, 1, (1,))
-    gather.hand_on(INA, 2, (0,))
-    gather.hand_on(INA, 2, (1,))
-    gather.arrived_late(INA, (0,))
-    gather.arrived_late(INA, (1,))
-    onward(DOWN, 1)
     gather.arrived(SMALL, 2)
     layer.spread()
     layer.norm_in()
     swap.start_left(INA)
+    layer.project_steps()
+    gather.hand_on(INA, 2, (0,))
+    gather.hand_on(INA, 2, (1,))
+    gather.arrived_late(INA, (0,))
+    onward(OUT, 1)
+    onward_late(OUT)
+    gather.arrived_late(INA, (1,))
     gather.hand_on(INB, 2, (0,))
     gather.hand_on(INB, 2, (1,))
-    onward_late(OUT)
     gather.arrived_late(INB, (0,))
     gather.arrived_late(INB, (1,))
+    onward(DOWN, 1)
+    landed(INA)
+    layer.project(layer.g_ina, 0, core)
     gather.hand_on(OUT, 2, (0,))
     gather.hand_on(OUT, 2, (1,))
+    onward(GU, 1)
+    onward_late(GU)
+    gather.passed(INA)
+    layer.project(layer.g_ina, 0, 1 - core)
+    layer.attend()
+    gather.arrived_late(OUT, (0,))
+    gather.arrived_late(OUT, (1,))
     layer.both_cotangent[0:128, :] = layer.cotangent[...]
     mate.start(Mate.COTANGENT)
-    onward(GU, 1)
-    onward_late(GU)
-    landed(INA)
+    landed(INB)
+    layer.project(layer.g_inb, 2048, core)
     gather.hand_on(DOWN, 2, (0,))
     gather.hand_on(DOWN, 2, (1,))
-    gather.passed(INA)
-    layer.project_first()
-    layer.attend()
-    landed(INB)
-    gather.arrived_late(OUT, (0,))
-    gather.arrived_late(OUT, (1,))
     gather.passed(INB)
-    layer.project_last()
+    layer.project(layer.g_inb, 2048, 1 - core)
     layer.activate()
     layer.steps()
     landed(OUT)
     layer.mix(0, 6)
     layer.mix(6, 12)
     layer.mix_norm()
+    layer.branch_half(core)
+    gather.hand_on(GU, 2, (1,))
     gather.passed(OUT)
+    layer.branch_half(1 - core)
     layer.branch()
     mate.start(Mate.NORMED)
     layer.turn_left(layer.mixed, layer.left_out, 16)
     swap.start_left(OUT)
-    gather.hand_on(GU, 2, (1,))
     gather.hand_on(GU, 2, (0,))
     onward_late(DOWN)
-    gather.arrived_late(GU, (0,))
-    gather.arrived_late(GU, (1,))
     mate.arrived(Mate.COTANGENT)
     swap.start_right(DOWN)
+    gather.arrived_late(GU, (1,))
+    gather.arrived_late(GU, (0,))
     landed(GU)
     gather.arrived_late(DOWN, (0,))
     gather.arrived_late(DOWN, (1,))
@@ -1396,18 +1417,24 @@
     mate.arrived(Mate.NORMED)
     layer.turn_other()
     swap.start_left(GU)
+    layer.feed_half(core)
     gather.passed(GU)
-    layer.feed()
-    swap.start_left(DOWN)
+    layer.feed_half(1 - core)
+    layer.feed(swap.start_left_rows)
     gather.passed(DOWN)
     layer.back_down()
     swap.start_right(GU)
-    for y in range(4):
-        layer.back_feed(y)
-        mate.start_columns(y)
+    layer.back_feed(0)
+    mate.start_columns(0)
+    layer.back_feed(1)
+    mate.start_columns(1)
     swap.arrived(DOWN)
     layer.grad_tall(layer.left_down, layer.right_down, grads[DOWN])
     scatter.start(DOWN, 0)
+    layer.back_feed(2)
+    mate.start_columns(2)
+    layer.back_feed(3)
+    mate.start_columns(3)
     swap.arrived(GU)
     layer.grad_wide(layer.left_gu, layer.right_gu, grads[GU])
     scatter.start(GU, 0)
@@ -1418,65 +1445,66 @@
     layer.back_residual()
     swap.start_right(OUT)
     layer.back_branch()
+    scatter.hand_on(GU, 0)
     gather.finish(OUT)
     swap.arrived(OUT)
     layer.grad_tall(layer.left_out, layer.right_out, grads[OUT])
     scatter.start(OUT, 0)
-    scatter.hand_on(GU, 0)
     layer.back_gated()
     layer.back_attend()
     swap.start_right(INA)
     layer.back_mix(0, 6)
+    scatter.relay(DOWN, 0)
     layer.back_mix(6, 12)
     gather.finish(GU)
     swap.arrived(INA)
     layer.grad_wide(layer.left_in, layer.right_ina, grads[INA])
     scatter.start(INA, 0)
-    scatter.relay(DOWN, 0)
+    scatter.relay(GU, 0)
+    scatter.hand_on(OUT, 0)
     layer.back_steps()
     swap.start_right(SMALL)
-    scatter.hand_on(OUT, 0)
+    scatter.hand_on(DOWN, 1)
     layer.back_activate()
     swap.start_right(INB)
+    mate.arrived(Mate.DOWN_PART)
+    layer.down_sum()
     swap.arrived(SMALL)
     layer.grad_wide(layer.left_in, layer.right_dt, grads[SMALL])
     scatter.start(SMALL, 0)
-    mate.arrived(Mate.DOWN_PART)
-    layer.down_sum()
-    scatter.relay(GU, 0)
     swap.arrived(INB)
     layer.grad_wide(layer.left_in, layer.right_inb, grads[INB])
     scatter.start(INB, 0)
-    scatter.hand_on(INA, 0)
     layer.back_project(0, 2)
-    scatter.hand_on(DOWN, 1)
     layer.back_project(2, 4)
     layer.back_input()
     sum_all.start(0, layer.vectors[...])
+    scatter.hand_on(GU, 1)
+    scatter.hand_on(INA, 0)
+    scatter.relay(OUT, 0)
     sum_all.start(1, sum_all.total(0))
-    scatter.relay(OUT, 0)
-    scatter.hand_on(GU, 1)
+    scatter.relay(DOWN, 1)
     scatter.relay(SMALL, 0)
     scatter.hand_on(INB, 0)
+    scatter.relay(GU, 1)
     scatter.relay(INA, 0)
-    scatter.relay(DOWN, 1)
+    scatter.hand_on(OUT, 1)
     sum_all.start(2, sum_all.total(1))
-    scatter.relay(GU, 1)
-    scatter.relay(OUT, 1)
+    plan.last(DOWN)
     scatter.relay(SMALL, 1)
+    end.take(DOWN)
     scatter.relay(INB, 0)
     scatter.hand_on(INA, 1)
-    plan.last(DOWN)
-    end.take(DOWN)
+    plan.last(GU)
+    scatter.relay(OUT, 1)
     sum_all.start(3, sum_all.total(2))
-    plan.last(GU)
+    plan.last(SMALL)
+    scatter.relay(INA, 1)
+    plan.last_gu()
+    scatter.relay(INB, 1)
     plan.last(OUT)
-    plan.last(SMALL)
+    end.take(GU)
     end.take(OUT)
-    scatter.relay(INA, 1)
-    scatter.relay(INB, 1)
-    plan.last_gu()
-    end.take(GU)
     layer.total[...] = sum_all.total(3)
     plan.last(INA)
     plan.last(INB)
@@ -1528,7 +1556,7 @@
     scratch += [pltpu.VMEM(lead + block, LOW) for lead, block in zip(LANDINGS, BLOCKS * 3)]
     scratch += [pltpu.VMEM(block, WIDE) for block in ENDS]
     scratch += [pltpu.VMEM((block[0] // 2, block[1]), WIDE) for block in ENDS]
-    scratch += [pltpu.SemaphoreType.DMA((count,)) for count in SEMS.values() for _ in range(2)]
+    scratch += [pltpu.SemaphoreType.DMA((n,)) for counts in SEMS.values() for n in counts]
     whole = pl.BlockSpec(memory_space=pltpu.VMEM)
     results = pl.pallas_call(
         layer_kernel,

time: 116 us -> 115 us (level)
  no operation moved by 1% of the time
where the time goes in v4:
time: 115 us
  Pallas kernels  114 us (99%)
    pallas_call x1, Pallas kernels, local(): pl.pallas_call(layer_kernel, out_shape=[jax.ShapeDtypeStruct(*one) for on...  112 us

profile of v4, /device:TPU:1, one launch (start us, length us, event | category | flops | bytes accessed | tf_op | source)
XLA Modules:
  0.0 114.8 jit_solution(542936570127018653)
XLA Ops:
  0.6 111.7 %layer.1 = (bf16[128,1024]{1,0:T(8,128)(2,1)}, bf16[128,1024]{1,0:T(8,128)(2,1)}, f32[8,4120]{1,0:T(8,128)}, f32[16,1024]{1,0:T(8,128)}, f32[8,4096]{1,0:T(8,128...) custom-call(bf16[128,1024]{1,0:T(8,128)(2,1)} %refs_0_.1, bf16[128,1024]{1,0:T(8,128)(2,1)} %refs_1_.1, ...), custom_call_target="tpu_custom_call" | custom-call | tf_op jit(solution)/shard_map/layer/pallas_call | solution.py:1561
  112.4 2.2 %finish.1 = (bf16[128,1024]{1,0:T(8,128)(2,1)}, bf16[128,1024]{1,0:T(8,128)(2,1)}, f32[8,4120]{1,0:T(8,128)}, f32[16,1024]{1,0:T(8,128)}, f32[8,4096]{1,0:T(8,12...) custom-call(bf16[128,1024]{1,0:T(8,128)(2,1)} %get-tuple-element.31., ...), custom_call_target="tpu_custom_call" | custom-call | tf_op jit(solution)/shard_map/finish/pallas_call | solution.py:1573

commit v5 on v4

--- a/solution.py
+++ b/solution.py
@@ -159,6 +159,8 @@
 
     def blocks(self, name, phase):
         order = order_of(name, 0)
+        if name == SMALL and phase == 2:
+            return 8
         return slab_blocks(name, order[:phase], order[phase])
 
     def send_slot(self, name, phase):
@@ -179,6 +181,8 @@
         where[order[phase]] = self.place.spot(name, order[phase], step)
         if half is not None:
             where |= halved(name, order[:phase], half)
+        if name == SMALL and phase == 2:
+            where[X] = pl.ds(2 * self.place.core, 2)
         return self.ref(name).at[block_index(where, *PARTS[name][part])]
 
     def copy(self, name, part, phase, kind, half=None, slot=None):
@@ -249,6 +253,17 @@
                 self.place.sibling,
             ).start()
 
+    def share_small(self):
+        self.arrived(SMALL, 2)
+        for step in STEPS:
+            view = self.slab(SMALL, 0, 2, step)
+            push(
+                view, view, self.send_slot(SMALL, 3), self.recv_sem.at[53], self.place.sibling
+            ).start()
+
+    def shared_small(self):
+        expect(self.ref(SMALL), 24, self.recv_sem.at[53], self.place).wait_recv()
+
     def passed(self, name):
         count = 16 * DEPTH[name]
         expect(self.ref(name), count, self.recv_sem.at[10 * name + 2], self.place).wait_recv()
@@ -261,9 +276,9 @@
             else:
                 count *= 3
             expect(self.ref(name), count, self.send_slot(name, phase), self.place).wait_send()
-        if name != SMALL:
-            slot = self.send_slot(name, 3)
-            expect(self.ref(name), 16 * DEPTH[name], slot, self.place).wait_send()
+        slot = self.send_slot(name, 3)
+        count = 24 if name == SMALL else 16 * DEPTH[name]
+        expect(self.ref(name), count, slot, self.place).wait_send()
 
 
 def each(count, body):
@@ -475,19 +490,29 @@
         self.place, self.got = place, got
         self.send_sem, self.recv_sem = send_sem, recv_sem
 
+    def push(self, src, stage, slot, device):
+        dst = self.got.at[stage, slot]
+        push(src, dst, self.send_sem.at[stage], self.recv_sem.at[stage], device).start()
+
+    def begin(self, values):
+        core, size = self.place.core, self.got.shape[3]
+        own = pl.ds(pl.multiple_of(core * size, size), size)
+        other = pl.ds(pl.multiple_of((1 - core) * size, size), size)
+        self.push(values.at[:, other], 0, core, self.place.sibling)
+        self.got[0, core] = values[:, own]
+
     def start(self, stage, value):
-        if stage == 0:
+        if stage == 4:
             slot, devices = self.place.core, [self.place.sibling]
         else:
             axis = AXES[stage - 1]
             slot, devices = self.place.at[axis], [self.place.peer(axis, s) for s in STEPS]
         self.got[stage, slot] = value
-        view = self.got.at[stage, slot]
         for device in devices:
-            push(view, view, self.send_sem.at[stage], self.recv_sem.at[stage], device).start()
+            self.push(self.got.at[stage, slot], stage, slot, device)
 
     def expect(self, stage):
-        view = self.got.at[stage, pl.ds(0, 3 if stage else 1)]
+        view = self.got.at[stage, pl.ds(0, 3 if 0 < stage < 4 else 1)]
         return push(
             view, view, self.send_sem.at[stage], self.recv_sem.at[stage], self.place.sibling
         )
@@ -499,8 +524,14 @@
             total = total + self.got[stage, slot]
         return total
 
+    def into(self, ref):
+        self.expect(4).wait_recv()
+        size = self.got.shape[3]
+        for half in range(2):
+            ref[:, size * half : size * half + size] = self.got[4, half]
+
     def finish(self):
-        for stage in range(4):
+        for stage in range(5):
             self.expect(stage).wait_send()
 
 
@@ -1231,7 +1262,7 @@
     right_gu=((512, 1024), LOW),
     right_down=((512, 512), LOW),
     right_dt=((256, 128), LOW),
-    sums=((4, 4, 8, 1792), WIDE),
+    sums=((5, 4, 8, 896), WIDE),
 )
 BLOCKS = tuple((ROWS[name], COLS[name]) for name in WEIGHTS)
 LANDINGS = tuple((3, DEPTH[name], 4) for name in WEIGHTS)
@@ -1239,7 +1270,7 @@
 LANDINGS += tuple({GU: (1, 2), DOWN: (1,)}.get(name, (3,)) for name in WEIGHTS)
 ENDS = tuple((ROWS[name], 2048 if name == GU else COLS[name]) for name in WEIGHTS[1:])
 SEMS = dict(
-    enter=(4, 4), gather=(24, 53), scatter=(18, 30), sums=(4, 4), end=(5, 5), swap=(12, 12), mate=(5, 5),
+    enter=(4, 4), gather=(24, 54), scatter=(18, 30), sums=(5, 5), end=(5, 5), swap=(12, 12), mate=(5, 5),
 )
 
 
@@ -1355,14 +1386,15 @@
     gather.hand_on(GU, 1, (1,))
     onward(INB, 1)
     onward_late(INB)
-    gather.arrived(SMALL, 2)
+    gather.share_small()
+    gather.hand_on(INA, 2, (0,))
+    gather.hand_on(INA, 2, (1,))
+    gather.arrived_late(INA, (0,))
+    gather.shared_small()
     layer.spread()
     layer.norm_in()
     swap.start_left(INA)
     layer.project_steps()
-    gather.hand_on(INA, 2, (0,))
-    gather.hand_on(INA, 2, (1,))
-    gather.arrived_late(INA, (0,))
     onward(OUT, 1)
     onward_late(OUT)
     gather.arrived_late(INA, (1,))
@@ -1478,7 +1510,7 @@
     layer.back_project(0, 2)
     layer.back_project(2, 4)
     layer.back_input()
-    sum_all.start(0, layer.vectors[...])
+    sum_all.begin(layer.vectors)
     scatter.hand_on(GU, 1)
     scatter.hand_on(INA, 0)
     scatter.relay(OUT, 0)
@@ -1505,11 +1537,12 @@
     plan.last(OUT)
     end.take(GU)
     end.take(OUT)
-    layer.total[...] = sum_all.total(3)
+    sum_all.start(4, sum_all.total(3))
     plan.last(INA)
     plan.last(INB)
     end.take(INA)
     end.take(INB)
+    sum_all.into(layer.total)
     for name in (SMALL, INA, INB, DOWN):
         gather.finish(name)
     scatter.finish()

time: 115 us -> 114 us (level)
  no operation moved by 1% of the time
where the time goes in v5:
time: 114 us
  Pallas kernels  113 us (99%)
    pallas_call x1, Pallas kernels, local(): pl.pallas_call(layer_kernel, out_shape=[jax.ShapeDtypeStruct(*one) for on...  111 us

profile of v5, /device:TPU:1, one launch (start us, length us, event | category | flops | bytes accessed | tf_op | source)
XLA Modules:
  0.0 114.2 jit_solution(10266185525292307336)
XLA Ops:
  0.6 111.2 %layer.1 = (bf16[128,1024]{1,0:T(8,128)(2,1)}, bf16[128,1024]{1,0:T(8,128)(2,1)}, f32[8,4120]{1,0:T(8,128)}, f32[16,1024]{1,0:T(8,128)}, f32[8,4096]{1,0:T(8,128...) custom-call(bf16[128,1024]{1,0:T(8,128)(2,1)} %refs_0_.1, bf16[128,1024]{1,0:T(8,128)(2,1)} %refs_1_.1, ...), custom_call_target="tpu_custom_call" | custom-call | tf_op jit(solution)/shard_map/layer/pallas_call | solution.py:1594
  111.9 2.2 %finish.1 = (bf16[128,1024]{1,0:T(8,128)(2,1)}, bf16[128,1024]{1,0:T(8,128)(2,1)}, f32[8,4120]{1,0:T(8,128)}, f32[16,1024]{1,0:T(8,128)}, f32[8,4096]{1,0:T(8,12...) custom-call(bf16[128,1024]{1,0:T(8,128)(2,1)} %get-tuple-element.31., ...), custom_call_target="tpu_custom_call" | custom-call | tf_op jit(solution)/shard_map/finish/pallas_call | solution.py:1606

commit v6 on v5

--- a/solution.py
+++ b/solution.py
@@ -476,9 +476,9 @@
             each(own.shape[0], body)
             self.start(name, phase + 1, (part,))
 
-    def finish(self):
-        for name in WEIGHTS:
-            for phase in range(3):
+    def finish(self, names, phases):
+        for name in names:
+            for phase in phases:
                 times = len(self.steps(name, phase)) if self.direct(name, phase) else 3
                 count = self.blocks(name, phase) * times
                 slot = self.send_slot(name, phase)
@@ -530,8 +530,8 @@
         for half in range(2):
             ref[:, size * half : size * half + size] = self.got[4, half]
 
-    def finish(self):
-        for stage in range(5):
+    def finish(self, stages):
+        for stage in stages:
             self.expect(stage).wait_send()
 
 
@@ -1538,19 +1538,22 @@
     end.take(GU)
     end.take(OUT)
     sum_all.start(4, sum_all.total(3))
+    for name in (SMALL, INA, INB, DOWN):
+        gather.finish(name)
+    enter.finish()
+    swap.finish()
+    mate.finish()
+    sum_all.finish((0, 1, 2))
+    scatter.finish((SMALL, OUT, GU, DOWN), (0, 1, 2))
+    scatter.finish((INA, INB), (0, 1))
     plan.last(INA)
     plan.last(INB)
     end.take(INA)
     end.take(INB)
     sum_all.into(layer.total)
-    for name in (SMALL, INA, INB, DOWN):
-        gather.finish(name)
-    scatter.finish()
-    sum_all.finish()
+    scatter.finish((INA, INB), (2,))
+    sum_all.finish((3, 4))
     end.finish()
-    swap.finish()
-    mate.finish()
-    enter.finish()
 
 
 def finish_kernel(*refs):

time: 114 us -> 114 us (level)
  no operation moved by 1% of the time
where the time goes in v6:
time: 114 us
  Pallas kernels  113 us (99%)
    pallas_call x1, Pallas kernels, local(): pl.pallas_call(layer_kernel, out_shape=[jax.ShapeDtypeStruct(*one) for on...  111 us

profile of v6, /device:TPU:1, one launch (start us, length us, event | category | flops | bytes accessed | tf_op | source)
XLA Modules:
  0.0 114.1 jit_solution(4551590087755007983)
XLA Ops:
  0.6 111.1 %layer.1 = (bf16[128,1024]{1,0:T(8,128)(2,1)}, bf16[128,1024]{1,0:T(8,128)(2,1)}, f32[8,4120]{1,0:T(8,128)}, f32[16,1024]{1,0:T(8,128)}, f32[8,4096]{1,0:T(8,128...) custom-call(bf16[128,1024]{1,0:T(8,128)(2,1)} %refs_0_.1, bf16[128,1024]{1,0:T(8,128)(2,1)} %refs_1_.1, ...), custom_call_target="tpu_custom_call" | custom-call | tf_op jit(solution)/shard_map/layer/pallas_call | solution.py:1597
  111.8 2.2 %finish.1 = (bf16[128,1024]{1,0:T(8,128)(2,1)}, bf16[128,1024]{1,0:T(8,128)(2,1)}, f32[8,4120]{1,0:T(8,128)}, f32[16,1024]{1,0:T(8,128)}, f32[8,4096]{1,0:T(8,12...) custom-call(bf16[128,1024]{1,0:T(8,128)(2,1)} %get-tuple-element.31., ...), custom_call_target="tpu_custom_call" | custom-call | tf_op jit(solution)/shard_map/finish/pallas_call | solution.py:1609
